TPU v7x, 256 devices: a whole 4x4x8 slice. The times are simulated.
256 devices in a mesh: lat: 32 (over x, z), lev: 8 (over y, core).
Axes of the slice: x: 4, y: 4, z: 8, core: 2. Of those that a mesh axis runs over, the one named last changes fastest.
Arguments:
- fourier: bfloat16 [1280, 3, 128, 128], P('lat', None, 'lev'), may hold values from -6 to 6
- gauss: float32 [1280], P('lat'), may hold values from 0.2 to 2
- legendre: bfloat16 [32, 4, 1280, 640], P('lat'), may hold values from -0.15625 to 0.15625
- owner: int32 [64, 1], replicated, may hold values from 0 to 31; in each aligned block of 64 rows (0 to 63, 64 to 127, ...) at most 4 rows name the same one
- send_list: int32 [32, 32, 2], P('lat'), may hold values from 0 to 799, as said below
- stencil: int32 [8192, 4], P('lat'), may hold values from 0 to 63, as said below
- hweight: float32 [8192, 4, 128], P('lat'), may hold values from -3 to 3
- vweight: float32 [8192, 128], P('lat', 'lev'), may hold values from 0 to 1
Outputs:
- spectral: bfloat16 [32, 4, 3, 128, 2, 640], P('lat', None, None, 'lev')
- arrival: bfloat16 [8192, 3, 128, 128], P('lat', None, 'lev')
Inputs may be any that keep to these rules, and one draw needn't show every extreme that they name: Every owner holds one to 4 wavenumbers, some owner exactly 4. send_list[d, r, :] names blocks of band d; stencil reads only devices d with |d - r| <= 16, and of these only the first one to 2 entries; entries for d = r always all 2; the others repeat the first entry. `stencil`: row a reads slots d * 2 + k of band a // 256 for live entries of send_list[d, a // 256, k], |d - a // 256| <= 16.
All inputs are finite; a program needn't handle non-finite values.
Results may differ from a plain program's by a relative error of at most 0.0072.
Values may be sent and summed in bfloat16 or wider, within the bound.
No kernel may reach another device: no remote copies, remote signals or barrier semaphores. Data moves between devices by JAX's collectives and lax.ppermute only.
A program may use at most 128 MiB of HBM per device.

v0:
```python
import math

import jax
import jax.numpy as jnp
from jax import lax
from jax.sharding import PartitionSpec as P

NLON = 2560
BLK = 128


diffusion = 3.0


def passed_along(shard, axis, by):
    size = lax.axis_size(axis)
    pairs = [(i, i + by) for i in range(size) if 0 <= i + by < size]
    return lax.ppermute(shard, axis, pairs)


def damping_curve(degrees):
    order_n = jnp.arange(degrees, dtype=jnp.float32)
    ratio = order_n * (order_n + 1.0) / float(degrees * (degrees - 1))
    return 1.0 / (1.0 + diffusion * ratio * ratio)


def zonal_rows(wave_number, present, longitudes, wave_total):
    points = jnp.arange(longitudes, dtype=jnp.int32)
    phases = wave_number[:, None] * points[None, :] % longitudes
    angles = phases.astype(jnp.float32) * (2.0 * math.pi / longitudes)
    norm_factor = present[:, None] / math.sqrt(wave_total)
    cosine = jnp.cos(angles) * norm_factor
    sine = -jnp.sin(angles) * norm_factor
    return jnp.stack([cosine, sine], axis=1).reshape(-1, longitudes).astype(jnp.bfloat16)


def per_device(fourier, gauss, legendre, owner, send_list, stencil, hweight, vweight):
    lat_count = lax.axis_size("lat")
    device_row = lax.axis_index("lat")
    lat_dev, fields, levels, columns = fourier.shape
    wave_total = columns // 2
    slot_most = legendre.shape[1]
    degrees = legendre.shape[3]
    slot_count = lat_count * slot_most
    owners = owner[:, 0]
    wave_index = jnp.arange(wave_total, dtype=jnp.int32)
    earlier = (owners[:, None] == owners[None, :]) & (wave_index[:, None] < wave_index[None, :])
    slot_rank = jnp.sum(earlier.astype(jnp.int32), axis=0)
    slot_of = owners * slot_most + slot_rank
    wave_number = wave_index * (degrees // wave_total)
    placed = (slot_of[:, None] == jnp.arange(slot_count, dtype=jnp.int32)[None, :]).astype(
        jnp.int32
    )
    weighted = (fourier.astype(jnp.float32) * gauss[:, None, None, None]).astype(jnp.bfloat16)
    weighted = weighted.reshape(lat_dev, fields, levels, wave_total, 2)
    packed = jnp.einsum(
        "tfvjr,js->sfvrt", weighted, placed.astype(jnp.bfloat16), preferred_element_type=jnp.float32
    ).astype(jnp.bfloat16)
    owned = lax.dynamic_slice_in_dim(placed, device_row * slot_most, slot_most, 1)
    filled = jnp.sum(owned, axis=0) > 0
    slot_wave = jnp.sum(owned * wave_number[:, None], axis=0)
    degree_index = jnp.arange(degrees, dtype=jnp.int32)
    keep_mask = (filled[:, None] & (degree_index[None, :] >= slot_wave[:, None])).astype(
        jnp.float32
    )
    damping = keep_mask * damping_curve(degrees)[None, :]
    tables = legendre[0]
    arrived = lax.all_to_all(packed, "lat", split_axis=0, concat_axis=4, tiled=True)
    spectra = jnp.einsum("sfvrl,sln->sfvrn", arrived, tables, preferred_element_type=jnp.float32)
    spectral = (spectra * damping[:, None, None, None, :]).astype(jnp.bfloat16)
    back_rows = jnp.einsum("sln,sfvrn->sfvrl", tables, spectral, preferred_element_type=jnp.float32)
    returned = lax.all_to_all(
        back_rows.astype(jnp.bfloat16), "lat", split_axis=4, concat_axis=0, tiled=True
    )
    blocks_x = NLON // BLK
    slot_waves = jnp.sum(placed * wave_number[:, None], axis=0)
    present = (jnp.sum(placed, axis=0) > 0).astype(jnp.float32)
    zonal_table = zonal_rows(slot_waves, present, NLON, wave_total).reshape(
        slot_count, 2, blocks_x, BLK
    )
    grid_field = jnp.einsum(
        "sfvrt,srbp->tbfvp", returned, zonal_table, preferred_element_type=jnp.float32
    )
    grid_field = grid_field.astype(jnp.bfloat16)
    at_top = lax.axis_index("lev") == lax.axis_size("lev") - 1
    block_ids = send_list[0].reshape(-1)
    outgoing = grid_field[block_ids // blocks_x, block_ids % blocks_x]
    received = lax.all_to_all(outgoing, "lat", split_axis=0, concat_axis=0, tiled=True)
    picked = received[stencil]
    horizontal = hweight[:, 0][:, None, None, :] * picked[:, 0].astype(jnp.float32)
    for corner in range(1, 4):
        horizontal = horizontal + hweight[:, corner][:, None, None, :] * picked[:, corner].astype(
            jnp.float32
        )
    upper_row = passed_along(horizontal[:, :, 0, :], "lev", -1)
    upper_row = jnp.where(at_top, horizontal[:, :, -1, :], upper_row)
    above_level = jnp.concatenate([horizontal[:, :, 1:], upper_row[:, :, None, :]], axis=2)
    vertical_w = vweight[:, None, :, None]
    arrival = ((1.0 - vertical_w) * horizontal + vertical_w * above_level).astype(jnp.bfloat16)
    return (spectral[None], arrival)


def solution(mesh):
    return jax.shard_map(
        per_device,
        mesh=mesh,
        in_specs=(
            P("lat", None, "lev", None),
            P("lat"),
            P("lat", None, None, None),
            P(),
            P("lat", None, None),
            P("lat", None),
            P("lat", None, None),
            P("lat", "lev"),
        ),
        out_specs=(P("lat", None, None, "lev", None, None), P("lat", None, "lev", None)),
        check_vma=False,
    )
```

profile of v0, /device:TPU:1, one launch (start us, length us, event | category | flops | bytes accessed | tf_op | source)
XLA Modules:
  0.0 258.2 jit_solution(640470551339515965)
XLA Ops:
  0.6 0.8 convert_reduce_fusion
  1.5 0.7 fusion.51
  2.1 1.2 multiply_convert_fusion.2
  3.3 1.2 copy.62
  4.5 1.9 fusion.18
  6.4 6.9 %copy.64 = bf16[128,3,16,2,40]{4,3,2,1,0:T(2,128)(2,1)S(1)} copy(bf16[128,3,16,2,40]{0,4,3,2,1:T(8,128)(2,1)} %fusion.18) | data formatting | bytes 1966080 | tf_op jit(solution)/shard_map/convert_element_type | solution.py:58
  13.3 5.8 %reshape.297 = bf16[32,2,7680]{2,1,0:T(2,128)(2,1)} reshape(bf16[128,3,16,2,40]{4,3,2,1,0:T(2,128)(2,1)S(1)} %copy.64) | data formatting | bytes 1966080
  19.1 12.2 %all-to-all-start = ((bf16[32,2,7680]{2,1,0:T(2,128)(2,1)}), bf16[32,2,7680]{2,1,0:T(2,128)(2,1)}, u32[]{:S(2)}, u32[]{:S(2)}) async-start(bf16[32,2,7680]{2,1,0:T(2,128)(2,1)} %reshape.297), calls=%async_computation | async-start | bytes 1966080 | tf_op jit(solution)/shard_map/all_to_all | solution.py:68
  31.4 0.1 dynamic-slice_reduce_fusion
  31.6 23.0 %all-to-all-done = bf16[32,2,7680]{2,1,0:T(2,128)(2,1)} async-done(((bf16[32,2,7680]{2,1,0:T(2,128)(2,1)}), bf16[32,2,7680]{2,1,0:T(2,128)(2,1)}, u32[]{:S(2)}, u32[]{:S(2)}) %all-to-all-start) | async-done | bytes 983072 | tf_op jit(solution)/shard_map/all_to_all | solution.py:68
  54.7 12.2 %reshape.298 = bf16[128,3,16,2,40]{4,3,2,1,0:T(2,128)(2,1)S(1)} reshape(bf16[32,2,7680]{2,1,0:T(2,128)(2,1)} %all-to-all-done) | data formatting | bytes 1966080
  66.9 0.4 copy.65
  67.3 2.0 copy.66
  69.3 6.4 %all_to_all.32 = bf16[4,3,16,2,1280]{4,2,3,1,0:T(8,128)(2,1)} reshape(bf16[4,3,16,2,32,40]{5,4,2,3,1,0:T(8,128)(2,1)S(1)} %copy.66) | data formatting | bytes 1966080 | tf_op jit(solution)/shard_map/all_to_all | solution.py:68
  75.7 4.4 %fusion.31 = bf16[4,3,16,2,640]{4,2,3,1,0:T(8,128)(2,1)S(1)} fusion(bf16[4,3,16,2,1280]{4,2,3,1,0:T(8,128)(2,1)} %all_to_all.32, bf16[1,4,1280,640]{3,2,1,0:T(8,128)(2,1)} %param.10, f32[4,640]{1,0:T(4,128)S(1)} %fusion.45), kind=kOutput, calls=%fused_computation.40 | convolution fusion | flops 629637120 | bytes 8038400 | tf_op jit(solution)/shard_map/sfvrl,sln->sfvrn/dot_general | solution.py:69
  80.0 0.8 copy-done.1
  80.8 5.0 %fusion.10 = bf16[4,3,16,2,1280]{4,2,3,1,0:T(8,128)(2,1)S(1)} fusion(bf16[4,3,16,2,640]{4,2,3,1,0:T(8,128)(2,1)S(1)} %fusion.31, bf16[1,4,1280,640]{3,2,1,0:T(8,128)(2,1)} %param.10), kind=kOutput, calls=%fused_computation.22 | convolution fusion | flops 629637120 | bytes 8028160 | tf_op jit(solution)/shard_map/sln,sfvrn->sfvrl/dot_general | solution.py:71
  85.8 12.3 %copy.67 = bf16[4,3,16,2,1280]{2,3,1,0,4:T(2,128)(2,1)} copy(bf16[4,3,16,2,1280]{4,2,3,1,0:T(8,128)(2,1)S(1)} %fusion.10) | data formatting | bytes 1966080 | tf_op jit(solution)/shard_map/convert_element_type | solution.py:73
  98.1 10.9 %reshape.299 = bf16[32,2,7680]{2,1,0:T(2,128)(2,1)} reshape(bf16[1280,4,3,2,16]{4,3,2,1,0:T(2,128)(2,1)} %bitcast.103) | data formatting | bytes 1966080
  109.0 8.5 %all-to-all-start.1 = ((bf16[32,2,7680]{2,1,0:T(2,128)(2,1)}), bf16[32,2,7680]{2,1,0:T(2,128)(2,1)S(1)}, u32[]{:S(2)}, u32[]{:S(2)}) async-start(bf16[32,2,7680]{2,1,0:T(2,128)(2,1)} %reshape.299), calls=%async_computation.1 | async-start | bytes 1966080 | tf_op jit(solution)/shard_map/all_to_all | solution.py:72
  117.5 0.1 copy.72
  117.6 0.1 div.41
  117.8 0.1 rem.53
  117.9 0.1 copy.70
  118.0 0.1 ne.87
  118.1 0.1 select_reduce_fusion
  118.2 7.0 %multiply_convert_fusion.1 = (bf16[128,1,20,128]{3,0,1,2:T(8,128)(2,1)}, bf16[128,1,20,128]{3,0,1,2:T(8,128)(2,1)}) fusion(f32[128]{0:T(128)S(1)} %compare_select_fusion.3, s32[20,128]{1,0:T(8,128)S(1)} %multiply_add_fusion, s32[128]{0:T(128)S(1)} %get-tuple-element.12), kind=kLoop, calls=%fused_computation.34 | loop fusion | flops 4587520 | bytes 1321984 | tf_op jit(solution)/shard_map/convert.4
  125.2 15.2 %all-to-all-done.1 = bf16[32,2,7680]{2,1,0:T(2,128)(2,1)S(1)} async-done(((bf16[32,2,7680]{2,1,0:T(2,128)(2,1)}), bf16[32,2,7680]{2,1,0:T(2,128)(2,1)S(1)}, u32[]{:S(2)}, u32[]{:S(2)}) %all-to-all-start.1) | async-done | bytes 983072 | tf_op jit(solution)/shard_map/all_to_all | solution.py:72
  140.4 7.2 %reshape.300 = bf16[1280,4,3,2,16]{4,3,2,1,0:T(2,128)(2,1)} reshape(bf16[32,2,7680]{2,1,0:T(2,128)(2,1)S(1)} %all-to-all-done.1) | data formatting | bytes 1966080
  147.6 14.6 %copy.68 = bf16[4,3,16,2,32,40]{5,2,3,1,0,4:T(8,128)(2,1)S(1)} copy(bf16[4,3,16,2,32,40]{2,3,1,0,5,4:T(2,128)(2,1)} %bitcast.104) | data formatting | bytes 1966080 | tf_op jit(solution)/shard_map/all_to_all | solution.py:72
  162.3 3.8 %copy.69 = bf16[128,3,16,2,40]{0,4,3,2,1:T(8,128)(2,1)} copy(bf16[128,3,16,2,40]{4,2,3,1,0:T(8,128)(2,1)S(1)} %bitcast.106) | data formatting | bytes 1966080 | tf_op jit(solution)/shard_map/all_to_all | solution.py:72
  166.1 6.6 %fusion = bf16[40,20,3,16,128]{4,0,3,2,1:T(8,128)(2,1)} fusion(bf16[128,1,20,128]{3,0,1,2:T(8,128)(2,1)} %get-tuple-element.23, bf16[128,1,20,128]{3,0,1,2:T(8,128)(2,1)} %get-tuple-element.22, bf16[128,3,16,2,40]{0,4,3,2,1:T(8,128)(2,1)} %copy.69), kind=kOutput, calls=%fused_computation.3 | convolution fusion | flops 2524119040 | bytes 12124160 | tf_op jit(solution)/shard_map/sfvrt,srbp->tbfvp/dot_general | solution.py:81
  172.7 9.9 %copy.73 = bf16[40,20,3,16,128]{4,3,2,1,0:T(8,128)(2,1)} copy(bf16[40,20,3,16,128]{4,0,3,2,1:T(8,128)(2,1)} %fusion) | data formatting | bytes 19660800 | tf_op jit(solution)/shard_map/convert_element_type | solution.py:84
  182.7 5.5 %gather_fusion = bf16[64,3,16,128]{3,2,1,0:T(8,128)(2,1)} fusion(bf16[40,20,3,16,128]{4,3,2,1,0:T(8,128)(2,1)} %copy.73, s32[64]{0:T(128)S(1)} %fusion.52), kind=kCustom, calls=%fused_computation | custom fusion | bytes 1573376 | tf_op jit(solution)/shard_map/gather | solution.py:87
  188.1 8.6 %all-to-all-start.2 = ((bf16[64,3,16,128]{3,2,1,0:T(8,128)(2,1)}), bf16[64,3,16,128]{3,2,1,0:T(8,128)(2,1)S(1)}, u32[]{:S(2)}, u32[]{:S(2)}) async-start(bf16[64,3,16,128]{3,2,1,0:T(8,128)(2,1)} %gather_fusion), calls=%async_computation.2 | async-start | bytes 1572864 | tf_op jit(solution)/shard_map/all_to_all | solution.py:88
  196.8 0.1 copy.74
  196.9 0.1 reshape.284
  197.1 0.4 fusion.55
  197.4 19.1 %all-to-all-done.2 = bf16[64,3,16,128]{3,2,1,0:T(8,128)(2,1)S(1)} async-done(((bf16[64,3,16,128]{3,2,1,0:T(8,128)(2,1)}), bf16[64,3,16,128]{3,2,1,0:T(8,128)(2,1)S(1)}, u32[]{:S(2)}, u32[]{:S(2)}) %all-to-all-start.2) | async-done | bytes 786464 | tf_op jit(solution)/shard_map/all_to_all | solution.py:88
  216.5 11.8 %gather_fusion.1 = bf16[1024,3,16,128]{3,2,1,0:T(8,128)(2,1)} fusion(bf16[64,3,16,128]{3,2,1,0:T(8,128)(2,1)S(1)} %all-to-all-done.2, s32[1024]{0:T(1024)S(1)} %broadcast_clamp_fusion), kind=kCustom, calls=%fused_computation.1 | custom fusion | bytes 25169920 | tf_op jit(solution)/shard_map/gather | solution.py:89
  228.3 5.8 %fusion.54 = (bf16[256,1,3,16,128]{4,3,2,1,0:T(8,128)(2,1)S(1)}, bf16[256,1,3,16,128]{4,3,2,1,0:T(8,128)(2,1)S(1)}, bf16[256,1,3,16,128]{4,3,2,1,0:T(8,128)(2,1)S(1)}, bf16[256,1,3,16,128]{4,3,2,1,0:T(8,128)(2,1)S(1)}) fusion(bf16[256,4,3,16,128]{4,3,2,1,0:T(8,128)(2,1)} %bitcast.102), kind=kLoop, calls=%fused_computation.87 | loop fusion | bytes 25165824 | tf_op jit(solution)/shard_map/slice | solution.py:90
  234.1 2.6 %fusion.7 = f32[256,3,16,128]{3,0,1,2:T(8,128)S(1)} fusion(bf16[256,1,3,16,128]{4,3,2,1,0:T(8,128)(2,1)S(1)} %get-tuple-element.17, bf16[256,1,3,16,128]{4,3,2,1,0:T(8,128)(2,1)S(1)} %get-tuple-element.15, bf16[256,1,3,16,128]{4,3,2,1,0:T(8,128)(2,1)S(1)} %get-tuple-element.16, bf16[256,1,3,16,128]{4,3,2,1,0:T(8,128)(2,1)S(1)} %get-tuple-element.14, ...), kind=kLoop, calls=%fused_computation.12 | loop fusion | flops 17301504 | bytes 19398656 | tf_op jit(solution)/shard_map/add | solution.py:92
  236.8 2.6 %copy-done = f32[256,3,16,128]{3,0,1,2:T(8,128)} copy-done((f32[256,3,16,128]{3,0,1,2:T(8,128)}, f32[256,3,16,128]{3,0,1,2:T(8,128)S(1)}, u32[]{:S(2)}) %copy-start) | copy-done | bytes 6291480
  239.5 6.7 %collective-permute-start = (f32[256,3,128]{2,0,1:T(8,128)S(1)}, f32[256,3,128]{2,0,1:T(8,128)S(1)}, u32[]{:S(2)}, u32[]{:S(2)}) collective-permute-start(f32[256,3,128]{2,0,1:T(8,128)S(1)} %slice_bitcast_fusion), channel_id=1, source_target_pairs={{1,0},{2,1},{3,2},{4,3},{5,4},{6,5},{7,6},{9,8},{10,9},{11,10},{12... | collective-permute-start | bytes 1179656 | tf_op jit(solution)/shard_map/ppermute | solution.py:18
  246.2 1.2 copy.80
  247.4 5.2 %collective-permute-done = f32[256,3,128]{2,0,1:T(8,128)S(1)} collective-permute-done((f32[256,3,128]{2,0,1:T(8,128)S(1)}, f32[256,3,128]{2,0,1:T(8,128)S(1)}, u32[]{:S(2)}, u32[]{:S(2)}) %collective-permute-start) | collective-permute-done | bytes 393248 | tf_op jit(solution)/shard_map/ppermute | solution.py:18
  252.6 1.9 fusion.6
  254.5 3.7 %copy.81 = bf16[256,3,16,128]{3,2,1,0:T(8,128)(2,1)} copy(bf16[256,3,16,128]{3,0,1,2:T(8,128)(2,1)S(1)} %fusion.6) | data formatting | bytes 6291456
  (35 shorter events, 0.4 us)
Async XLA Ops:
  19.1 35.5 %all-to-all-start = ((bf16[32,2,7680]{2,1,0:T(2,128)(2,1)}), bf16[32,2,7680]{2,1,0:T(2,128)(2,1)}, u32[]{:S(2)}, u32[]{:S(2)}) async-start(bf16[32,2,7680]{2,1,0:T(2,128)(2,1)} %reshape.297), calls=%async_computation | async-start | bytes 1966080 | tf_op jit(solution)/shard_map/all_to_all | solution.py:68
  80.0 0.8 copy-start.1
  98.1 19.4 %copy-start.6 = (s32[1,32,2]{1,2,0:T(2,128)S(1)}, s32[1,32,2]{1,2,0:T(2,128)}, u32[]{:S(2)}) copy-start(s32[1,32,2]{1,2,0:T(2,128)} %param.12) | copy-start | bytes 772
  109.0 31.5 %all-to-all-start.1 = ((bf16[32,2,7680]{2,1,0:T(2,128)(2,1)}), bf16[32,2,7680]{2,1,0:T(2,128)(2,1)S(1)}, u32[]{:S(2)}, u32[]{:S(2)}) async-start(bf16[32,2,7680]{2,1,0:T(2,128)(2,1)} %reshape.299), calls=%async_computation.1 | async-start | bytes 1966080 | tf_op jit(solution)/shard_map/all_to_all | solution.py:72
  182.7 14.1 %copy-start.5 = (s32[256,4]{0,1:T(4,128)S(1)}, s32[256,4]{0,1:T(4,128)}, u32[]{:S(2)}) copy-start(s32[256,4]{0,1:T(4,128)} %param.13) | copy-start | bytes 12292
  182.7 14.4 %copy-start.3 = (f32[256,4,128]{2,1,0:T(4,128)S(1)}, f32[256,4,128]{2,1,0:T(4,128)}, u32[]{:S(2)}) copy-start(f32[256,4,128]{2,1,0:T(4,128)} %param.14) | copy-start | bytes 1572868
  188.1 28.4 %all-to-all-start.2 = ((bf16[64,3,16,128]{3,2,1,0:T(8,128)(2,1)}), bf16[64,3,16,128]{3,2,1,0:T(8,128)(2,1)S(1)}, u32[]{:S(2)}, u32[]{:S(2)}) async-start(bf16[64,3,16,128]{3,2,1,0:T(8,128)(2,1)} %gather_fusion), calls=%async_computation.2 | async-start | bytes 1572864 | tf_op jit(solution)/shard_map/all_to_all | solution.py:88
  234.1 12.0 %copy-start.4 = (f32[256,16]{0,1:T(8,128)S(1)}, f32[256,16]{0,1:T(8,128)}, u32[]{:S(2)}) copy-start(f32[256,16]{0,1:T(8,128)} %param.15) | copy-start | bytes 49156
  234.1 12.1 %copy-start.2 = (bf16[4,3,16,2,640]{4,2,3,1,0:T(8,128)(2,1)S(1)}, bf16[4,3,16,2,640]{4,2,3,1,0:T(8,128)(2,1)}, u32[]{:S(2)}) copy-start(bf16[4,3,16,2,640]{4,2,3,1,0:T(8,128)(2,1)} %copy-done.1) | copy-start | bytes 1474564
  236.8 2.7 %copy-start = (f32[256,3,16,128]{3,0,1,2:T(8,128)}, f32[256,3,16,128]{3,0,1,2:T(8,128)S(1)}, u32[]{:S(2)}) copy-start(f32[256,3,16,128]{3,0,1,2:T(8,128)S(1)} %fusion.7) | copy-start | bytes 18874372
  239.5 13.0 %collective-permute-start = (f32[256,3,128]{2,0,1:T(8,128)S(1)}, f32[256,3,128]{2,0,1:T(8,128)S(1)}, u32[]{:S(2)}, u32[]{:S(2)}) collective-permute-start(f32[256,3,128]{2,0,1:T(8,128)S(1)} %slice_bitcast_fusion), channel_id=1, source_target_pairs={{1,0},{2,1},{3,2},{4,3},{5,4},{6,5},{7,6},{9,8},{10,9},{11,10},{12... | collective-permute-start | bytes 1179656 | tf_op jit(solution)/shard_map/ppermute | solution.py:18
  246.2 6.3 %slice-start = ((s8[6291456]{0:T(1024)(128)(4,1)}), s8[4194304]{0:T(1024)(128)(4,1)S(1)}, s32[]{:S(2)}) async-start(s8[6291456]{0:T(1024)(128)(4,1)} %bitcast.100), calls=%async_computation.3 | async-start | bytes 8388608
  247.3 5.2 %slice-start.1 = ((s8[6291456]{0:T(1024)(128)(4,1)}), s8[2097152]{0:T(1024)(128)(4,1)S(1)}, s32[]{:S(2)}) async-start(s8[6291456]{0:T(1024)(128)(4,1)} %bitcast.100), calls=%async_computation.4 | async-start | bytes 4194304
  247.4 5.2 %slice-start.2 = ((f32[256,3,16,128]{3,0,1,2:T(8,128)}), f32[256,3,15,128]{3,0,1,2:T(8,128)S(1)}, s32[]{:S(2)}) async-start(f32[256,3,16,128]{3,0,1,2:T(8,128)} %copy-done), calls=%async_computation.5 | async-start | bytes 11796480 | tf_op jit(solution)/shard_map/slice | solution.py:97
where the time goes:
time: 260 us; the launch traced here: 258 us
  local copies, waits for them, and re-layouts  126 us (48%)
  waiting for transfers between devices  62.5 us (24%)
  starting transfers between devices  35.9 us (14%)
  matrix products  17.9 us (7%)
  other arithmetic  14.7 us (6%)
    unnamed x24, local copies, waits for them, and re-layouts  44.4 us
    all_to_all x1, waiting for transfers between devices, per_device(): lax.all_to_all(packed, 'lat', split_axis=0, concat_axis=4, tiled=True)  23 us
    all_to_all x1, waiting for transfers between devices, per_device(): lax.all_to_all(outgoing, 'lat', split_axis=0, concat_axis=0, tiled=True)  19.1 us
    all_to_all x2, local copies, waits for them, and re-layouts, per_device(): lax.all_to_all(back_rows.astype(jnp.bfloat16), 'lat', split_axis=4, conca...  18.4 us
    all_to_all x1, waiting for transfers between devices, per_device(): lax.all_to_all(back_rows.astype(jnp.bfloat16), 'lat', split_axis=4, conca...  15.2 us
    convert_element_type x1, local copies, waits for them, and re-layouts, per_device(): back_rows.astype(jnp.bfloat16)  12.3 us
    all_to_all x1, starting transfers between devices, per_device(): lax.all_to_all(packed, 'lat', split_axis=0, concat_axis=4, tiled=True)  12.2 us
    gather x1, local copies, waits for them, and re-layouts, per_device(): picked = received[stencil]  11.8 us
  transfers between devices with their start and end apart: 4, of which 4 were waited for; matrix products, arithmetic and copies ran while one was open for 4% of the time, Pallas kernels for 0%

commit v1 on v0

v1 whole, which is shorter than its diff:
```python
import math

import jax
import jax.numpy as jnp
from jax import lax
from jax.experimental import pallas as pl
from jax.experimental.pallas import tpu as pltpu
from jax.sharding import PartitionSpec as P

NLON = 2560
BLK = 128
BLOCKS_X = NLON // BLK
LANES = 128

diffusion = 3.0

NT = (((1,), (1,)), ((), ()))
NN = (((1,), (0,)), ((), ()))


def mxu(left, right, dims):
    return lax.dot_general(left, right, dims, preferred_element_type=jnp.float32)


def identity(size):
    rows = lax.broadcasted_iota(jnp.int32, (size, size), 0)
    columns = lax.broadcasted_iota(jnp.int32, (size, size), 1)
    return (rows == columns).astype(jnp.float32).astype(jnp.bfloat16)


def damping_curve(degrees):
    order_n = jnp.arange(degrees, dtype=jnp.float32)
    ratio = order_n * (order_n + 1.0) / float(degrees * (degrees - 1))
    return 1.0 / (1.0 + diffusion * ratio * ratio)


def pack_kernel(gauss, fourier, owned_by, slot_mask, message, scratch):
    lat_dev, fields, levels, columns = fourier.shape
    owners = owned_by.shape[0]
    chooser = owned_by[...]
    masks = [slot_mask[i : i + 1, :] for i in range(slot_mask.shape[0])]

    def one_latitude(t, carry):
        rows = fourier[t].reshape(fields * levels, columns).astype(jnp.float32)
        rows = (rows * gauss[t]).astype(jnp.bfloat16)
        parts = []
        for slot in range(len(masks) // 2):
            for field in range(fields):
                for part in range(2):
                    parts.append(rows[field * levels : (field + 1) * levels] * masks[2 * slot + part])
        spread = jnp.concatenate(parts, axis=0)
        chosen = mxu(chooser, spread, NT)
        for tile in range(scratch.shape[0]):
            scratch[tile, pl.ds(t, owners, stride=lat_dev), :] = chosen[:, tile * LANES : (tile + 1) * LANES]
        return carry

    lax.fori_loop(0, lat_dev, one_latitude, 0, unroll=4)
    for o in range(owners):
        for tile in range(scratch.shape[0]):
            message[o, :, tile * LANES : (tile + 1) * LANES] = scratch[
                tile, o * lat_dev : (o + 1) * lat_dev, :
            ].astype(jnp.bfloat16)


def spectral_kernel(row_of, arrived, tables, damping, spectral, message, turned, rows_at):
    step = pl.program_id(0)
    slots = damping.shape[0]
    per_slot = turned.shape[0] // slots
    half = per_slot // 2
    field_rows = half // 3
    latitudes = arrived.shape[0]

    @pl.when(step == 0)
    def _():
        unit = identity(LANES)
        for tile in range(arrived.shape[1] // LANES):
            columns = arrived[:, tile * LANES : (tile + 1) * LANES]
            turned[tile * LANES : (tile + 1) * LANES, :] = mxu(unit, columns, NT).astype(jnp.bfloat16)

    table = tables[0]
    own = turned[pl.ds(pl.multiple_of(step * per_slot, 16), per_slot), :]
    spectra = mxu(own, table, NN)
    damped = (spectra * damping[pl.ds(step, 1), :]).astype(jnp.bfloat16)
    spectral[0] = damped
    gap = jnp.zeros((LANES - half, damped.shape[1]), jnp.bfloat16)
    sides = []
    for part in range(2):
        for field in range(3):
            at = (2 * field + part) * field_rows
            sides.append(damped[at : at + field_rows])
        sides.append(gap)
    sides = jnp.concatenate(sides, axis=0)
    chunk = 256
    for at in range(0, latitudes, chunk):
        back = mxu(table[at : at + chunk], sides, NT)
        for part in range(2):
            rows_at[pl.ds(at * 2 * slots + step * 2 + part, chunk, stride=2 * slots), :] = back[
                :, part * LANES : (part + 1) * LANES
            ]

    @pl.when(step == slots - 1)
    def _():
        receivers, message_rows, message_lanes = message.shape
        lane = lax.broadcasted_iota(jnp.int32, (8, LANES), 1)
        tiles = message_lanes // LANES

        def one_receiver(r, carry):
            for pair in range(message_rows // 16):
                halves = []
                for side in range(2):
                    built = [None] * tiles
                    for e in range(8):
                        entry = r * message_rows + (pair * 2 + side) * 8 + e
                        at = pl.multiple_of(row_of[entry] * 8, 8)
                        row = rows_at[pl.ds(at, 8), :]
                        start = e * half
                        if start % LANES:
                            row = pltpu.roll(row, start % LANES, 1)
                        for tile in range(start // LANES, (start + half - 1) // LANES + 1):
                            first = start - tile * LANES
                            if built[tile] is None:
                                built[tile] = row
                            else:
                                built[tile] = jnp.where(lane >= first, row, built[tile])
                    halves.append(jnp.concatenate(built, axis=1))
                both = jnp.concatenate(halves, axis=0).astype(jnp.bfloat16)
                message[r, pair * 16 : (pair + 1) * 16, :] = both
            return carry

        lax.fori_loop(0, receivers, one_receiver, 0)


def block_kernel(column_of, received, zonal, blocks, lowest, lowest_scratch):
    owners, message_rows, message_lanes = received.shape
    unit = identity(LANES)
    half = message_lanes // 8
    groups = message_rows // 8
    entries = blocks.shape[0]
    for pair in range(groups // 2):
        wide = received[:, pair * 16 : (pair + 1) * 16, :].astype(jnp.float32)
        for side in range(2):
            group = pair * 2 + side
            own = wide[:, side * 8 : (side + 1) * 8, :].reshape(owners * 8, message_lanes).astype(jnp.bfloat16)
            turned = [
                mxu(unit, own[:, tile * LANES : (tile + 1) * LANES], NT).astype(jnp.bfloat16)
                for tile in range(message_lanes // LANES)
            ]
            turned = jnp.concatenate(turned, axis=0)
            for e in range(8):
                entry = group * 8 + e
                made = mxu(turned[e * half : (e + 1) * half], zonal[column_of[entry]], NN)
                blocks[entry] = made.astype(jnp.bfloat16)
                for field in range(3):
                    lowest_scratch[field * entries + entry : field * entries + entry + 1, :] = made[
                        field * 16 : field * 16 + 1, :
                    ]
    lowest[...] = lowest_scratch[...].astype(jnp.bfloat16)


def arrive_kernel(stencil, at_top, blocks, above, hweight, vweight, arrival, wide):
    entries = blocks.shape[0]
    step = pl.program_id(0)
    rows, fields, levels, _ = arrival.shape

    @pl.when(step == 0)
    def _():
        top = at_top[0] == 1

        def widen(entry, carry):
            block = blocks[entry].astype(jnp.float32)
            wide[entry, 0 : fields * levels, :] = block
            for field in range(fields):
                own_last = block[(field + 1) * levels - 1 : (field + 1) * levels, :]
                over = above[pl.ds(field * entries + entry, 1), :]
                wide[entry, pl.ds(fields * levels + field, 1), :] = jnp.where(top, own_last, over)
            return carry

        lax.fori_loop(0, entries, widen, 0, unroll=4)

    level = lax.broadcasted_iota(jnp.int32, (levels, LANES), 0)

    def one_row(a, carry):
        total = None
        for q in range(4):
            place = stencil[(step * rows + a) * 4 + q]
            term = hweight[a, pl.ds(q, 1), :] * wide[place]
            total = term if total is None else total + term
        upper = vweight[a]
        for field in range(fields):
            here = total[field * levels : (field + 1) * levels]
            over = jnp.where(
                level == levels - 1,
                total[fields * levels + field : fields * levels + field + 1],
                pltpu.roll(here, levels - 1, 0),
            )
            arrival[a, field] = ((1.0 - upper) * here + upper * over).astype(jnp.bfloat16)
        return carry

    lax.fori_loop(0, rows, one_row, 0, unroll=4)


def whole(memory):
    return pl.BlockSpec(memory_space=memory)


def per_device(fourier, gauss, legendre, owner, send_list, stencil, hweight, vweight):
    lat_count = lax.axis_size("lat")
    device_row = lax.axis_index("lat")
    lat_dev, fields, levels, columns = fourier.shape
    wave_total = columns // 2
    slot_most = legendre.shape[1]
    degrees = legendre.shape[3]
    latitudes = legendre.shape[2]
    slot_count = lat_count * slot_most
    capacity = send_list.shape[2]
    arrivals = stencil.shape[0]
    half = fields * levels
    per_slot = 2 * half
    message_lanes = slot_most * per_slot
    entries = lat_count * capacity

    owners = owner[:, 0]
    wave_index = jnp.arange(wave_total, dtype=jnp.int32)
    earlier = (owners[:, None] == owners[None, :]) & (wave_index[:, None] < wave_index[None, :])
    slot_rank = jnp.sum(earlier.astype(jnp.int32), axis=0)
    slot_of = owners * slot_most + slot_rank
    wave_number = wave_index * (degrees // wave_total)
    lists = lax.all_gather(send_list[0], "lat", axis=0)

    column_index = jnp.arange(columns, dtype=jnp.int32)
    owner_column = jnp.repeat(owners, 2)
    rank_column = jnp.repeat(slot_rank, 2)
    owned_by = (jnp.arange(lat_count, dtype=jnp.int32)[:, None] == owner_column[None, :]).astype(jnp.bfloat16)
    slot_mask = (
        jnp.arange(2 * slot_most, dtype=jnp.int32)[:, None] == (2 * rank_column + column_index % 2)[None, :]
    ).astype(jnp.bfloat16)
    vmem = whole(pltpu.VMEM)
    smem = whole(pltpu.SMEM)
    message_one = pl.pallas_call(
        pack_kernel,
        out_shape=jax.ShapeDtypeStruct((lat_count, lat_dev, message_lanes), jnp.bfloat16),
        in_specs=[smem, vmem, vmem, vmem],
        out_specs=vmem,
        scratch_shapes=[pltpu.VMEM((message_lanes // LANES, lat_count * lat_dev, LANES), jnp.float32)],
        compiler_params=pltpu.CompilerParams(vmem_limit_bytes=48 * 2**20),
        name="pack",
    )(gauss, fourier, owned_by, slot_mask)
    arrived = lax.all_to_all(message_one, "lat", split_axis=0, concat_axis=0, tiled=True)

    placed = (slot_of[:, None] == jnp.arange(slot_count, dtype=jnp.int32)[None, :]).astype(jnp.int32)
    owned = lax.dynamic_slice_in_dim(placed, device_row * slot_most, slot_most, 1)
    filled = jnp.sum(owned, axis=0) > 0
    slot_wave = jnp.sum(owned * wave_number[:, None], axis=0)
    degree_index = jnp.arange(degrees, dtype=jnp.int32)
    keep_mask = (filled[:, None] & (degree_index[None, :] >= slot_wave[:, None])).astype(jnp.float32)
    damping = keep_mask * damping_curve(degrees)[None, :]

    band_start = jnp.arange(lat_count, dtype=jnp.int32)[:, None, None] * lat_dev
    row_of = jnp.transpose(band_start + lists // BLOCKS_X, (1, 0, 2)).reshape(-1)
    message_shape = (lat_count, entries // 8 * slot_most * 2, 8 * half)
    spectral_rows, message_two = pl.pallas_call(
        spectral_kernel,
        grid_spec=pltpu.PrefetchScalarGridSpec(
            num_scalar_prefetch=1,
            grid=(slot_most,),
            in_specs=[
                pl.BlockSpec((latitudes, message_lanes), lambda s, _: (0, 0)),
                pl.BlockSpec((1, latitudes, degrees), lambda s, _: (s, 0, 0)),
                pl.BlockSpec((slot_most, degrees), lambda s, _: (0, 0)),
            ],
            out_specs=[
                pl.BlockSpec((1, per_slot, degrees), lambda s, _: (s, 0, 0)),
                pl.BlockSpec(message_shape, lambda s, _: (0, 0, 0)),
            ],
            scratch_shapes=[
                pltpu.VMEM((message_lanes, latitudes), jnp.bfloat16),
                pltpu.VMEM((latitudes * 2 * slot_most, LANES), jnp.float32),
            ],
        ),
        out_shape=[
            jax.ShapeDtypeStruct((slot_most, per_slot, degrees), jnp.bfloat16),
            jax.ShapeDtypeStruct(message_shape, jnp.bfloat16),
        ],
        compiler_params=pltpu.CompilerParams(vmem_limit_bytes=48 * 2**20),
        name="spectral",
    )(row_of, arrived.reshape(latitudes, message_lanes), legendre[0], damping)
    received = lax.all_to_all(message_two, "lat", split_axis=0, concat_axis=0, tiled=True)

    spectral = jnp.transpose(
        spectral_rows.reshape(slot_most, fields, 2, levels, degrees), (0, 1, 3, 2, 4)
    )
    slot_waves = jnp.sum(placed * wave_number[:, None], axis=0)
    present = (jnp.sum(placed, axis=0) > 0).astype(jnp.float32)
    points = jnp.arange(NLON, dtype=jnp.int32).reshape(BLOCKS_X, 1, 1, BLK)
    phases = slot_waves[None, :, None, None] * points % NLON
    angles = phases.astype(jnp.float32) * (2.0 * math.pi / NLON)
    norm_factor = present[None, :, None, None] / math.sqrt(wave_total)
    zonal = jnp.concatenate([jnp.cos(angles) * norm_factor, -jnp.sin(angles) * norm_factor], axis=2)
    zonal = zonal.astype(jnp.bfloat16).reshape(BLOCKS_X, slot_count * 2, BLK)
    own_lists = lax.dynamic_slice_in_dim(lists, device_row, 1, 1)
    column_of = (own_lists % BLOCKS_X).reshape(-1)
    blocks, lowest = pl.pallas_call(
        block_kernel,
        out_shape=[
            jax.ShapeDtypeStruct((entries, half, BLK), jnp.bfloat16),
            jax.ShapeDtypeStruct((fields * entries, BLK), jnp.bfloat16),
        ],
        in_specs=[smem, vmem, vmem],
        out_specs=[vmem, vmem],
        scratch_shapes=[pltpu.VMEM((fields * entries, BLK), jnp.float32)],
        compiler_params=pltpu.CompilerParams(vmem_limit_bytes=48 * 2**20),
        name="blocks",
    )(column_of, received, zonal)

    lev_count = lax.axis_size("lev")
    above = lax.ppermute(lowest, "lev", [(i, i - 1) for i in range(1, lev_count)])
    at_top = (lax.axis_index("lev") == lev_count - 1).astype(jnp.int32).reshape(1)
    vertical = jnp.broadcast_to(vweight[:, :, None], (arrivals, levels, BLK))
    step_rows = 32
    arrival = pl.pallas_call(
        arrive_kernel,
        grid_spec=pltpu.PrefetchScalarGridSpec(
            num_scalar_prefetch=2,
            grid=(arrivals // step_rows,),
            in_specs=[
                pl.BlockSpec((entries, half, BLK), lambda i, *_: (0, 0, 0)),
                pl.BlockSpec((fields * entries, BLK), lambda i, *_: (0, 0)),
                pl.BlockSpec((step_rows, 4, BLK), lambda i, *_: (i, 0, 0)),
                pl.BlockSpec((step_rows, levels, BLK), lambda i, *_: (i, 0, 0)),
            ],
            out_specs=pl.BlockSpec((step_rows, fields, levels, BLK), lambda i, *_: (i, 0, 0, 0)),
            scratch_shapes=[pltpu.VMEM((entries, half + 8, BLK), jnp.float32)],
        ),
        out_shape=jax.ShapeDtypeStruct((arrivals, fields, levels, BLK), jnp.bfloat16),
        compiler_params=pltpu.CompilerParams(vmem_limit_bytes=48 * 2**20),
        name="arrive",
    )(stencil.reshape(-1), at_top, blocks, above.astype(jnp.float32), hweight, vertical)
    return (spectral[None], arrival)


def solution(mesh):
    return jax.shard_map(
        per_device,
        mesh=mesh,
        in_specs=(
            P("lat", None, "lev", None),
            P("lat"),
            P("lat", None, None, None),
            P(),
            P("lat", None, None),
            P("lat", None),
            P("lat", None, None),
            P("lat", "lev"),
        ),
        out_specs=(P("lat", None, None, "lev", None, None), P("lat", None, "lev", None)),
        check_vma=False,
    )
```

time: 260 us -> 147 us (0.57)
  local copies, waits for them, and re-layouts: 126 us -> 8.06 us
  blocking collectives: 0 us -> 49.3 us
  waiting for transfers between devices: 62.5 us -> 18.9 us
  Pallas kernels: 0 us -> 25.7 us
  matrix products: 17.9 us -> 0 us
  other arithmetic: 14.7 us -> 8.01 us
    all_gather x0 -> x1, blocking collectives: none -> 49.3 us  [per_device(): lists = lax.all_gather(send_list[0], 'lat', axis=0)]
    unnamed x24 -> x20, local copies, waits for them, and re-layouts: 44.4 us -> 2.81 us
    all_to_all x3 -> x2, waiting for transfers between devices: 57.4 us -> 17.5 us  [the longest x1 17.5 us: per_device(): lax.all_to_all(message_two, 'lat', split_axis=0, concat_axis=0, tiled=True)]
    convert_element_type x4 -> x0, local copies, waits for them, and re-layouts: 30.3 us -> none  [the longest x1 12.3 us: per_device(): back_rows.astype(jnp.bfloat16)]
    all_to_all x5 -> x0, local copies, waits for them, and re-layouts: 27.2 us -> none  [the longest x2 18.4 us: per_device(): lax.all_to_all(back_rows.astype(jnp.bfloat16), 'lat', split_axis=4, conca...]
    pallas_call x0 -> x4, Pallas kernels: none -> 25.7 us  [the longest x1 12.6 us: per_device(): pl.pallas_call(spectral_kernel, grid_spec=pltpu.PrefetchScalarGridSpec(nu...]
    dot_general x4 -> x0, matrix products: 17.9 us -> none  [the longest x1 6.64 us: per_device(): jnp.einsum('sfvrt,srbp->tbfvp', returned, zonal_table, preferred_element_...]
    gather x2 -> x0, local copies, waits for them, and re-layouts: 17.2 us -> none  [the longest x1 11.8 us: per_device(): picked = received[stencil]]
  transfers between devices with their start and end apart: 4 -> 3, of which waited for: 4 -> 2; matrix products, arithmetic and copies ran while one was open for 4% -> 7% of each run, Pallas kernels for 0% -> 0%
where the time goes in v1:
time: 147 us; the launch traced here: 146 us
  blocking collectives  49.3 us (34%)
  starting transfers between devices  35.2 us (24%)
  Pallas kernels  25.7 us (17%)
  waiting for transfers between devices  18.9 us (13%)
  local copies, waits for them, and re-layouts  8.06 us (5%)
  other arithmetic  8.01 us (5%)
    all_gather x1, blocking collectives, per_device(): lists = lax.all_gather(send_list[0], 'lat', axis=0)  49.3 us
    all_to_all x1, waiting for transfers between devices, per_device(): lax.all_to_all(message_two, 'lat', split_axis=0, concat_axis=0, tiled=True)  17.5 us
    ppermute x1, starting transfers between devices, per_device(): lax.ppermute(lowest, 'lev', [(i, i - 1) for i in range(1, lev_count)])  15.8 us
    pallas_call x1, Pallas kernels, per_device(): pl.pallas_call(spectral_kernel, grid_spec=pltpu.PrefetchScalarGridSpec(nu...  12.6 us
    all_to_all x1, starting transfers between devices, per_device(): lax.all_to_all(message_one, 'lat', split_axis=0, concat_axis=0, tiled=True)  12 us
    all_to_all x1, starting transfers between devices, per_device(): lax.all_to_all(message_two, 'lat', split_axis=0, concat_axis=0, tiled=True)  7.44 us
    pallas_call x1, Pallas kernels, per_device(): pl.pallas_call(arrive_kernel, grid_spec=pltpu.PrefetchScalarGridSpec(num_...  6.29 us
    another operation x1, other arithmetic  5.84 us
  transfers between devices with their start and end apart: 3, of which 2 were waited for; matrix products, arithmetic and copies ran while one was open for 7% of the time, Pallas kernels for 0%

profile of v1, /device:TPU:1, one launch (start us, length us, event | category | flops | bytes accessed | tf_op | source)
XLA Modules:
  0.0 146.0 jit_solution(3806899251435071611)
XLA Ops:
  0.6 0.8 convert_reduce_fusion
  1.5 0.1 broadcast_in_dim.9
  1.5 0.1 mul.174
  1.7 0.7 broadcast_in_dim.8
  2.4 0.1 eq.66
  2.6 0.0 copy-start.3
  2.6 1.0 copy-done.3
  3.6 0.0 copy-start.4
  3.6 0.7 copy-done.4
  4.3 4.3 %pack.1 = bf16[32,40,384]{2,1,0:T(8,128)(2,1)} custom-call(f32[40]{0:T(128)S(1)} %copy-done.4, bf16[40,3,16,128]{3,2,1,0:T(8,128)(2,1)S(1)} %copy-done.3, bf16[32,128]{1,0:T(8,128)(2,1)S(1)} %fusion.9.owned_by, bf16[8,128]{1,0:T(8,128)(2,1)S(1)} %fusion.12.slot_mask), custom_call_target="tpu_custom_call" | custom-call | tf_op jit(solution)/shard_map/pack/pallas_call | solution.py:239
  8.5 0.0 copy-start.7
  8.5 12.0 %all-to-all-start = ((bf16[32,40,384]{2,1,0:T(8,128)(2,1)}), bf16[32,40,384]{2,1,0:T(8,128)(2,1)S(1)}, u32[]{:S(2)}, u32[]{:S(2)}) async-start(bf16[32,40,384]{2,1,0:T(8,128)(2,1)} %pack.1), calls=%async_computation | async-start | bytes 1966080 | tf_op jit(solution)/shard_map/all_to_all | solution.py:248
  20.6 0.0 copy-done.7
  20.6 49.3 %all_gather.3 = s32[32,32,2]{1,2,0:T(2,128)S(1)} all-gather(s32[1,32,2]{1,2,0:T(2,128)S(1)} %copy-done.7), channel_id=1, replica_groups=mesh['lat'=32,'lev'=8] {'lat'}, dimensions={0}, use_global_device_ids=true | all-gather | bytes 8448 | tf_op jit(solution)/shard_map/all_gather | solution.py:228
  69.8 0.1 add_bitcast_fusion
  69.9 0.5 copy.26
  70.5 0.3 reshape.164.row_of
  70.8 0.0 copy-done.8
  70.8 0.2 dynamic-slice_reduce_fusion
  71.0 0.1 fusion.11.damping
  71.1 0.0 all-to-all-done
  71.1 12.6 %spectral.1 = (bf16[4,96,640]{2,1,0:T(8,128)(2,1)S(1)}, bf16[32,64,384]{2,1,0:T(8,128)(2,1)}) custom-call(s32[2048]{0:T(1024)S(1)} %reshape.164.row_of, bf16[1280,384]{1,0:T(8,128)(2,1)S(1)} %bitcast.20, bf16[4,1280,640]{2,1,0:T(8,128)(2,1)} %bitcast.22, f32[4,640]{1,0:T(4,128)S(1)} %fusion.11.damping), custom_call_target="tpu_custom_call" | custom-call | tf_op jit(solution)/shard_map/spectral/pallas_call | solution.py:261
  83.7 7.4 %all-to-all-start.1 = ((bf16[32,64,384]{2,1,0:T(8,128)(2,1)}), bf16[32,64,384]{2,1,0:T(8,128)(2,1)S(1)}, u32[]{:S(2)}, u32[]{:S(2)}) async-start(bf16[32,64,384]{2,1,0:T(8,128)(2,1)} %get-tuple-element.7), calls=%async_computation.1 | async-start | bytes 3145728 | tf_op jit(solution)/shard_map/all_to_all | solution.py:287
  91.1 0.7 fusion.6
  91.8 0.1 reshape.170.column_of
  91.9 0.1 select_reduce_fusion
  92.1 5.8 %multiply_convert_fusion.1 = (bf16[20,128,1,128]{3,1,2,0:T(8,128)(2,1)S(1)}, bf16[20,128,1,128]{3,1,2,0:T(8,128)(2,1)S(1)}) fusion(f32[128]{0:T(128)S(1)} %compare_select_fusion, s32[20,128]{1,0:T(8,128)S(1)} %multiply_add_fusion, s32[128]{0:T(128)S(1)} %get-tuple-element.12), kind=kLoop, calls=%fused_computation.5 | loop fusion | flops 4587520 | bytes 1321984 | tf_op jit(solution)/shard_map/convert.1
  97.9 0.1 pad_maximum_fusion
  98.0 1.4 copy.31
  99.4 17.5 %all-to-all-done.1.received = bf16[32,64,384]{2,1,0:T(8,128)(2,1)S(1)} async-done(((bf16[32,64,384]{2,1,0:T(8,128)(2,1)}), bf16[32,64,384]{2,1,0:T(8,128)(2,1)S(1)}, u32[]{:S(2)}, u32[]{:S(2)}) %all-to-all-start.1) | async-done | bytes 1572896 | tf_op jit(solution)/shard_map/all_to_all | solution.py:287
  116.9 0.0 copy-start.6
  116.9 2.5 %blocks.1 = (bf16[64,48,128]{2,1,0:T(8,128)(2,1)S(1)}, bf16[192,128]{1,0:T(8,128)(2,1)S(1)}) custom-call(s32[64]{0:T(128)S(1)} %reshape.170.column_of, bf16[32,64,384]{2,1,0:T(8,128)(2,1)S(1)} %all-to-all-done.1.received, bf16[20,256,128]{2,1,0:T(8,128)(2,1)S(1)} %bitcast.19), custom_call_target="tpu_custom_call" | custom-call | tf_op jit(solution)/shard_map/blocks/pallas_call | solution.py:302
  119.4 0.0 copy-start
  119.5 0.9 copy-done
  120.3 15.8 %collective-permute-start = (bf16[192,128]{1,0:T(8,128)(2,1)S(1)}, bf16[192,128]{1,0:T(8,128)(2,1)S(1)}, u32[]{:S(2)}, u32[]{:S(2)}) collective-permute-start(bf16[192,128]{1,0:T(8,128)(2,1)S(1)} %get-tuple-element.9), channel_id=1, source_target_pairs={{1,0},{2,1},{3,2},{4,3},{5,4},{6,5},{7,6},{9,8},{10,9},{11,10},{12... | collective-permute-start | bytes 147464 | tf_op jit(solution)/shard_map/ppermute | solution.py:316
  136.1 0.0 copy-done.6
  136.1 0.1 copy.28
  136.2 0.1 reshape.167.stencil
  136.4 0.0 copy-done.5
  136.4 0.1 copy.32
  136.5 1.2 copy.36
  137.6 0.0 copy-start.1
  137.6 0.0 copy-start.2
  137.6 1.4 collective-permute-done
  139.0 0.6 broadcast_in_dim.11.vweight
  139.6 0.0 copy-done.1
  139.7 0.0 copy-done.2
  139.7 6.3 %arrive.1 = bf16[256,3,16,128]{3,2,1,0:T(8,128)(2,1)} custom-call(s32[1024]{0:T(1024)S(1)} %reshape.167.stencil, s32[1]{0:T(128)} %bitcast.9.at_top, bf16[64,48,128]{2,1,0:T(8,128)(2,1)S(1)} %copy-done.1, f32[192,128]{1,0:T(8,128)S(1)} %convert_element_type.45.above, f32[256,4,128]{2,1,0:T(4,128)S(1)} %copy-done.2, f32[256,16,128]{2,1,0:T(8,128)S(1)} %broadcast_in_dim.11.vweight), custom_call_target="tpu_custom_call" | custom-call | tf_op jit(solution)/shard_map/arrive/pallas_call | solution.py:320
  (15 shorter events, 0.1 us)
Async XLA Ops:
  2.6 1.0 copy-start.3
  3.6 0.7 copy-start.4
  8.5 12.0 %copy-start.7 = (s32[1,32,2]{1,2,0:T(2,128)S(1)}, s32[1,32,2]{1,2,0:T(2,128)}, u32[]{:S(2)}) copy-start(s32[1,32,2]{1,2,0:T(2,128)} %param.12) | copy-start | bytes 772
  8.5 62.2 %copy-start.8 = (s32[64,1]{0,1:T(1,128)S(1)}, s32[64,1]{0,1:T(1,128)}, u32[]{:S(2)}) copy-start(s32[64,1]{0,1:T(1,128)} %param.11) | copy-start | bytes 772
  8.5 62.5 %all-to-all-start = ((bf16[32,40,384]{2,1,0:T(8,128)(2,1)}), bf16[32,40,384]{2,1,0:T(8,128)(2,1)S(1)}, u32[]{:S(2)}, u32[]{:S(2)}) async-start(bf16[32,40,384]{2,1,0:T(8,128)(2,1)} %pack.1), calls=%async_computation | async-start | bytes 1966080 | tf_op jit(solution)/shard_map/all_to_all | solution.py:248
  83.7 33.2 %all-to-all-start.1 = ((bf16[32,64,384]{2,1,0:T(8,128)(2,1)}), bf16[32,64,384]{2,1,0:T(8,128)(2,1)S(1)}, u32[]{:S(2)}, u32[]{:S(2)}) async-start(bf16[32,64,384]{2,1,0:T(8,128)(2,1)} %get-tuple-element.7), calls=%async_computation.1 | async-start | bytes 3145728 | tf_op jit(solution)/shard_map/all_to_all | solution.py:287
  116.9 19.2 %copy-start.6 = (s32[256,4]{0,1:T(4,128)S(1)}, s32[256,4]{0,1:T(4,128)}, u32[]{:S(2)}) copy-start(s32[256,4]{0,1:T(4,128)} %param.13) | copy-start | bytes 12292
  116.9 19.5 %copy-start.5 = (f32[256,16]{0,1:T(8,128)S(1)}, f32[256,16]{0,1:T(8,128)}, u32[]{:S(2)}) copy-start(f32[256,16]{0,1:T(8,128)} %param.15) | copy-start | bytes 49156
  119.4 0.9 copy-start
  120.3 18.7 %collective-permute-start = (bf16[192,128]{1,0:T(8,128)(2,1)S(1)}, bf16[192,128]{1,0:T(8,128)(2,1)S(1)}, u32[]{:S(2)}, u32[]{:S(2)}) collective-permute-start(bf16[192,128]{1,0:T(8,128)(2,1)S(1)} %get-tuple-element.9), channel_id=1, source_target_pairs={{1,0},{2,1},{3,2},{4,3},{5,4},{6,5},{7,6},{9,8},{10,9},{11,10},{12... | collective-permute-start | bytes 147464 | tf_op jit(solution)/shard_map/ppermute | solution.py:316
  137.6 2.0 %copy-start.1 = (bf16[64,48,128]{2,1,0:T(8,128)(2,1)S(1)}, bf16[64,48,128]{2,1,0:T(8,128)(2,1)}, u32[]{:S(2)}) copy-start(bf16[64,48,128]{2,1,0:T(8,128)(2,1)} %copy-done) | copy-start | bytes 2359300
  137.6 2.0 %copy-start.2 = (f32[256,4,128]{2,1,0:T(4,128)S(1)}, f32[256,4,128]{2,1,0:T(4,128)}, u32[]{:S(2)}) copy-start(f32[256,4,128]{2,1,0:T(4,128)} %hweight.1) | copy-start | bytes 1572868

commit v2 on v1

--- a/solution.py
+++ b/solution.py
@@ -34,7 +34,7 @@
     return 1.0 / (1.0 + diffusion * ratio * ratio)
 
 
-def pack_kernel(gauss, fourier, owned_by, slot_mask, message, scratch):
+def pack_kernel(gauss, fourier, owned_by, slot_mask, listed, message, scratch):
     lat_dev, fields, levels, columns = fourier.shape
     owners = owned_by.shape[0]
     chooser = owned_by[...]
@@ -55,27 +55,39 @@
         return carry
 
     lax.fori_loop(0, lat_dev, one_latitude, 0, unroll=4)
+    extra = jnp.broadcast_to(listed[...], (8, LANES))
     for o in range(owners):
+        parts = []
         for tile in range(scratch.shape[0]):
-            message[o, :, tile * LANES : (tile + 1) * LANES] = scratch[
-                tile, o * lat_dev : (o + 1) * lat_dev, :
-            ].astype(jnp.bfloat16)
-
-
-def spectral_kernel(row_of, arrived, tables, damping, spectral, message, turned, rows_at):
+            parts.append(scratch[tile, o * lat_dev : (o + 1) * lat_dev, :])
+        parts.append(extra)
+        message[o] = jnp.concatenate(parts, axis=0).astype(jnp.bfloat16)
+
+
+def spectral_kernel(arrived, tables, damping, spectral, message, turned, rows_at, listed, row_of, listed_sem):
     step = pl.program_id(0)
     slots = damping.shape[0]
+    bands = arrived.shape[0]
+    tiles = turned.shape[0] // LANES
+    lat_dev = (arrived.shape[1] - 8) // tiles
+    lists = pltpu.make_async_copy(listed, row_of, listed_sem)
     per_slot = turned.shape[0] // slots
     half = per_slot // 2
     field_rows = half // 3
-    latitudes = arrived.shape[0]
+    latitudes = bands * lat_dev
 
     @pl.when(step == 0)
     def _():
+        wide = arrived[...].astype(jnp.float32)
+        band = lax.broadcasted_iota(jnp.int32, (bands, LANES), 0)
+        listed[...] = (wide[:, tiles * lat_dev, :].astype(jnp.int32) + band * lat_dev) * 8
+        lists.start()
         unit = identity(LANES)
-        for tile in range(arrived.shape[1] // LANES):
-            columns = arrived[:, tile * LANES : (tile + 1) * LANES]
-            turned[tile * LANES : (tile + 1) * LANES, :] = mxu(unit, columns, NT).astype(jnp.bfloat16)
+        for tile in range(tiles):
+            columns = wide[:, tile * lat_dev : (tile + 1) * lat_dev, :].reshape(latitudes, LANES)
+            turned[tile * LANES : (tile + 1) * LANES, :] = mxu(unit, columns.astype(jnp.bfloat16), NT).astype(
+                jnp.bfloat16
+            )
 
     table = tables[0]
     own = turned[pl.ds(pl.multiple_of(step * per_slot, 16), per_slot), :]
@@ -100,18 +112,19 @@
 
     @pl.when(step == slots - 1)
     def _():
+        lists.wait()
         receivers, message_rows, message_lanes = message.shape
         lane = lax.broadcasted_iota(jnp.int32, (8, LANES), 1)
-        tiles = message_lanes // LANES
+        wide_tiles = message_lanes // LANES
 
         def one_receiver(r, carry):
             for pair in range(message_rows // 16):
                 halves = []
                 for side in range(2):
-                    built = [None] * tiles
+                    built = [None] * wide_tiles
                     for e in range(8):
-                        entry = r * message_rows + (pair * 2 + side) * 8 + e
-                        at = pl.multiple_of(row_of[entry] * 8, 8)
+                        entry = (pair * 2 + side) * 8 + e
+                        at = pl.multiple_of(row_of[entry // 2, 2 * r + entry % 2], 8)
                         row = rows_at[pl.ds(at, 8), :]
                         start = e * half
                         if start % LANES:
@@ -217,6 +230,7 @@
     half = fields * levels
     per_slot = 2 * half
     message_lanes = slot_most * per_slot
+    tiles = message_lanes // LANES
     entries = lat_count * capacity
 
     owners = owner[:, 0]
@@ -225,7 +239,8 @@
     slot_rank = jnp.sum(earlier.astype(jnp.int32), axis=0)
     slot_of = owners * slot_most + slot_rank
     wave_number = wave_index * (degrees // wave_total)
-    lists = lax.all_gather(send_list[0], "lat", axis=0)
+    ids = send_list[0].reshape(1, entries)
+    listed = jnp.concatenate([ids // BLOCKS_X, ids % BLOCKS_X], axis=1).astype(jnp.float32)
 
     column_index = jnp.arange(columns, dtype=jnp.int32)
     owner_column = jnp.repeat(owners, 2)
@@ -238,13 +253,13 @@
     smem = whole(pltpu.SMEM)
     message_one = pl.pallas_call(
         pack_kernel,
-        out_shape=jax.ShapeDtypeStruct((lat_count, lat_dev, message_lanes), jnp.bfloat16),
-        in_specs=[smem, vmem, vmem, vmem],
+        out_shape=jax.ShapeDtypeStruct((lat_count, tiles * lat_dev + 8, LANES), jnp.bfloat16),
+        in_specs=[smem, vmem, vmem, vmem, vmem],
         out_specs=vmem,
-        scratch_shapes=[pltpu.VMEM((message_lanes // LANES, lat_count * lat_dev, LANES), jnp.float32)],
+        scratch_shapes=[pltpu.VMEM((tiles, lat_count * lat_dev, LANES), jnp.float32)],
         compiler_params=pltpu.CompilerParams(vmem_limit_bytes=48 * 2**20),
         name="pack",
-    )(gauss, fourier, owned_by, slot_mask)
+    )(gauss, fourier, owned_by, slot_mask, listed)
     arrived = lax.all_to_all(message_one, "lat", split_axis=0, concat_axis=0, tiled=True)
 
     placed = (slot_of[:, None] == jnp.arange(slot_count, dtype=jnp.int32)[None, :]).astype(jnp.int32)
@@ -255,35 +270,33 @@
     keep_mask = (filled[:, None] & (degree_index[None, :] >= slot_wave[:, None])).astype(jnp.float32)
     damping = keep_mask * damping_curve(degrees)[None, :]
 
-    band_start = jnp.arange(lat_count, dtype=jnp.int32)[:, None, None] * lat_dev
-    row_of = jnp.transpose(band_start + lists // BLOCKS_X, (1, 0, 2)).reshape(-1)
     message_shape = (lat_count, entries // 8 * slot_most * 2, 8 * half)
     spectral_rows, message_two = pl.pallas_call(
         spectral_kernel,
-        grid_spec=pltpu.PrefetchScalarGridSpec(
-            num_scalar_prefetch=1,
-            grid=(slot_most,),
-            in_specs=[
-                pl.BlockSpec((latitudes, message_lanes), lambda s, _: (0, 0)),
-                pl.BlockSpec((1, latitudes, degrees), lambda s, _: (s, 0, 0)),
-                pl.BlockSpec((slot_most, degrees), lambda s, _: (0, 0)),
-            ],
-            out_specs=[
-                pl.BlockSpec((1, per_slot, degrees), lambda s, _: (s, 0, 0)),
-                pl.BlockSpec(message_shape, lambda s, _: (0, 0, 0)),
-            ],
-            scratch_shapes=[
-                pltpu.VMEM((message_lanes, latitudes), jnp.bfloat16),
-                pltpu.VMEM((latitudes * 2 * slot_most, LANES), jnp.float32),
-            ],
-        ),
+        grid=(slot_most,),
+        in_specs=[
+            pl.BlockSpec(arrived.shape, lambda s: (0, 0, 0)),
+            pl.BlockSpec((1, latitudes, degrees), lambda s: (s, 0, 0)),
+            pl.BlockSpec((slot_most, degrees), lambda s: (0, 0)),
+        ],
+        out_specs=[
+            pl.BlockSpec((1, per_slot, degrees), lambda s: (s, 0, 0)),
+            pl.BlockSpec(message_shape, lambda s: (0, 0, 0)),
+        ],
+        scratch_shapes=[
+            pltpu.VMEM((message_lanes, latitudes), jnp.bfloat16),
+            pltpu.VMEM((latitudes * 2 * slot_most, LANES), jnp.float32),
+            pltpu.VMEM((lat_count, LANES), jnp.int32),
+            pltpu.SMEM((lat_count, LANES), jnp.int32),
+            pltpu.SemaphoreType.DMA,
+        ],
         out_shape=[
             jax.ShapeDtypeStruct((slot_most, per_slot, degrees), jnp.bfloat16),
             jax.ShapeDtypeStruct(message_shape, jnp.bfloat16),
         ],
         compiler_params=pltpu.CompilerParams(vmem_limit_bytes=48 * 2**20),
         name="spectral",
-    )(row_of, arrived.reshape(latitudes, message_lanes), legendre[0], damping)
+    )(arrived, legendre[0], damping)
     received = lax.all_to_all(message_two, "lat", split_axis=0, concat_axis=0, tiled=True)
 
     spectral = jnp.transpose(
@@ -297,8 +310,9 @@
     norm_factor = present[None, :, None, None] / math.sqrt(wave_total)
     zonal = jnp.concatenate([jnp.cos(angles) * norm_factor, -jnp.sin(angles) * norm_factor], axis=2)
     zonal = zonal.astype(jnp.bfloat16).reshape(BLOCKS_X, slot_count * 2, BLK)
-    own_lists = lax.dynamic_slice_in_dim(lists, device_row, 1, 1)
-    column_of = (own_lists % BLOCKS_X).reshape(-1)
+    all_columns = arrived[:, tiles * lat_dev, entries:]
+    column_of = lax.dynamic_slice_in_dim(all_columns, device_row * capacity, capacity, 1)
+    column_of = column_of.astype(jnp.int32).reshape(-1)
     blocks, lowest = pl.pallas_call(
         block_kernel,
         out_shape=[

time: 147 us -> 124 us (0.84)
  blocking collectives: 49.3 us -> 0 us
  waiting for transfers between devices: 18.9 us -> 53.9 us
  starting transfers between devices: 35.2 us -> 26.1 us
    all_gather x1 -> x0, blocking collectives: 49.3 us -> none  [per_device(): lists = lax.all_gather(send_list[0], 'lat', axis=0)]
    all_to_all x1, waiting for transfers between devices: 0.01 us -> 24.3 us  [per_device(): lax.all_to_all(message_one, 'lat', split_axis=0, concat_axis=0, tiled=True)]
    all_to_all x1, waiting for transfers between devices: 17.5 us -> 28.2 us  [per_device(): lax.all_to_all(message_two, 'lat', split_axis=0, concat_axis=0, tiled=True)]
    ppermute x1, starting transfers between devices: 15.8 us -> 5.47 us  [per_device(): lax.ppermute(lowest, 'lev', [(i, i - 1) for i in range(1, lev_count)])]
  transfers between devices with their start and end apart: 3 -> 3, of which waited for: 2 -> 3; matrix products, arithmetic and copies ran while one was open for 7% -> 8% of each run, Pallas kernels for 0% -> 0%
where the time goes in v2:
time: 124 us
  waiting for transfers between devices  53.9 us (43%)
  starting transfers between devices  26.1 us (21%)
  Pallas kernels  25.5 us (21%)
  other arithmetic  8.79 us (7%)
  local copies, waits for them, and re-layouts  8.77 us (7%)
    all_to_all x1, waiting for transfers between devices, per_device(): lax.all_to_all(message_two, 'lat', split_axis=0, concat_axis=0, tiled=True)  28.2 us
    all_to_all x1, waiting for transfers between devices, per_device(): lax.all_to_all(message_one, 'lat', split_axis=0, concat_axis=0, tiled=True)  24.3 us
    pallas_call x1, Pallas kernels, per_device(): pl.pallas_call(spectral_kernel, grid=(slot_most,), in_specs=[pl.BlockSpec...  12.4 us
    all_to_all x1, starting transfers between devices, per_device(): lax.all_to_all(message_one, 'lat', split_axis=0, concat_axis=0, tiled=True)  12 us
    all_to_all x1, starting transfers between devices, per_device(): lax.all_to_all(message_two, 'lat', split_axis=0, concat_axis=0, tiled=True)  8.6 us
    pallas_call x1, Pallas kernels, per_device(): pl.pallas_call(arrive_kernel, grid_spec=pltpu.PrefetchScalarGridSpec(num_...  6.29 us
    another operation x1, other arithmetic  5.84 us
    ppermute x1, starting transfers between devices, per_device(): lax.ppermute(lowest, 'lev', [(i, i - 1) for i in range(1, lev_count)])  5.47 us
  transfers between devices with their start and end apart: 3, of which 3 were waited for; matrix products, arithmetic and copies ran while one was open for 8% of the time, Pallas kernels for 0%

profile of v2, /device:TPU:1, one launch (start us, length us, event | category | flops | bytes accessed | tf_op | source)
XLA Modules:
  0.0 123.8 jit_solution(16320694799140914769)
XLA Ops:
  0.6 0.7 sign_compare_fusion
  1.3 0.7 broadcast_divide_fusion
  2.0 0.8 convert_reduce_fusion
  2.8 0.1 copy.29
  2.9 0.1 ne.112
  3.1 0.1 copy.31
  3.1 0.1 div.38
  3.3 0.1 copy.30
  3.3 0.1 rem.68
  3.4 0.1 broadcast_in_dim.9
  3.5 0.1 mul.164
  3.7 0.7 broadcast_in_dim.8
  4.4 0.1 eq.66
  4.6 0.1 add_convert_fusion.listed
  4.7 1.0 copy-done.4
  5.7 0.7 copy-done.5
  6.4 4.3 %pack.1 = bf16[32,128,128]{2,1,0:T(8,128)(2,1)} custom-call(f32[40]{0:T(128)S(1)} %copy-done.5, bf16[40,3,16,128]{3,2,1,0:T(8,128)(2,1)S(1)} %copy-done.4, bf16[32,128]{1,0:T(8,128)(2,1)S(1)} %fusion.8.owned_by, bf16[8,128]{1,0:T(8,128)(2,1)S(1)} %fusion.11.slot_mask, f32[1,128]{1,0:T(1,128)S(1)} %add_convert_fusion.listed), custom_call_target="tpu_custom_call" | custom-call | tf_op jit(solution)/shard_map/pack/pallas_call | solution.py:254
  10.6 12.0 %all-to-all-start = ((bf16[32,128,128]{2,1,0:T(8,128)(2,1)}), bf16[32,128,128]{2,1,0:T(8,128)(2,1)S(1)}, u32[]{:S(2)}, u32[]{:S(2)}) async-start(bf16[32,128,128]{2,1,0:T(8,128)(2,1)} %pack.1), calls=%async_computation | async-start | bytes 2097152 | tf_op jit(solution)/shard_map/all_to_all | solution.py:263
  22.7 0.0 copy-done.8
  22.7 0.2 dynamic-slice_reduce_fusion
  22.9 0.1 fusion.10.damping
  22.9 24.3 %all-to-all-done.arrived = bf16[32,128,128]{2,1,0:T(8,128)(2,1)S(1)} async-done(((bf16[32,128,128]{2,1,0:T(8,128)(2,1)}), bf16[32,128,128]{2,1,0:T(8,128)(2,1)S(1)}, u32[]{:S(2)}, u32[]{:S(2)}) %all-to-all-start) | async-done | bytes 1048608 | tf_op jit(solution)/shard_map/all_to_all | solution.py:263
  47.3 12.4 %spectral.1 = (bf16[4,96,640]{2,1,0:T(8,128)(2,1)S(1)}, bf16[32,64,384]{2,1,0:T(8,128)(2,1)}) custom-call(bf16[32,128,128]{2,1,0:T(8,128)(2,1)S(1)} %all-to-all-done.arrived, bf16[4,1280,640]{2,1,0:T(8,128)(2,1)} %bitcast.22, f32[4,640]{1,0:T(4,128)S(1)} %fusion.10.damping), custom_call_target="tpu_custom_call" | custom-call | tf_op jit(solution)/shard_map/spectral/pallas_call | solution.py:274
  59.6 0.0 copy-done
  59.6 8.6 %all-to-all-start.1 = ((bf16[32,64,384]{2,1,0:T(8,128)(2,1)}), bf16[32,64,384]{2,1,0:T(8,128)(2,1)S(1)}, u32[]{:S(2)}, u32[]{:S(2)}) async-start(bf16[32,64,384]{2,1,0:T(8,128)(2,1)} %get-tuple-element.7), calls=%async_computation.1 | async-start | bytes 3145728 | tf_op jit(solution)/shard_map/all_to_all | solution.py:300
  68.2 0.1 select_reduce_fusion
  68.4 5.8 %multiply_convert_fusion.1 = (bf16[20,128,1,128]{3,1,2,0:T(8,128)(2,1)S(1)}, bf16[20,128,1,128]{3,1,2,0:T(8,128)(2,1)S(1)}) fusion(f32[128]{0:T(128)S(1)} %compare_select_fusion, s32[20,128]{1,0:T(8,128)S(1)} %multiply_add_fusion, s32[128]{0:T(128)S(1)} %get-tuple-element.12), kind=kLoop, calls=%fused_computation.5 | loop fusion | flops 4587520 | bytes 1321984 | tf_op jit(solution)/shard_map/convert.2
  74.2 0.1 pad_maximum_fusion
  74.3 1.4 %copy.36 = bf16[20,128,2,128]{3,2,1,0:T(2,128)(2,1)S(1)} copy(bf16[20,128,2,128]{3,1,2,0:T(8,128)(2,1)S(1)} %pad_maximum_fusion) | data formatting | bytes 2621440 | tf_op jit(solution)/shard_map/concatenate | solution.py:311
  75.7 0.9 slice.4
  76.6 0.1 convert_reduce_fusion.1
  76.8 0.1 reshape.229.column_of
  76.9 28.2 %all-to-all-done.1.received = bf16[32,64,384]{2,1,0:T(8,128)(2,1)S(1)} async-done(((bf16[32,64,384]{2,1,0:T(8,128)(2,1)}), bf16[32,64,384]{2,1,0:T(8,128)(2,1)S(1)}, u32[]{:S(2)}, u32[]{:S(2)}) %all-to-all-start.1) | async-done | bytes 1572896 | tf_op jit(solution)/shard_map/all_to_all | solution.py:300
  105.0 2.5 %blocks.1 = (bf16[64,48,128]{2,1,0:T(8,128)(2,1)S(1)}, bf16[192,128]{1,0:T(8,128)(2,1)S(1)}) custom-call(s32[64]{0:T(128)S(1)} %reshape.229.column_of, bf16[32,64,384]{2,1,0:T(8,128)(2,1)S(1)} %all-to-all-done.1.received, bf16[20,256,128]{2,1,0:T(8,128)(2,1)S(1)} %bitcast.20), custom_call_target="tpu_custom_call" | custom-call | tf_op jit(solution)/shard_map/blocks/pallas_call | solution.py:316
  107.6 0.0 copy-start.1
  107.6 0.9 copy-done.1
  108.5 5.5 %collective-permute-start = (bf16[192,128]{1,0:T(8,128)(2,1)S(1)}, bf16[192,128]{1,0:T(8,128)(2,1)S(1)}, u32[]{:S(2)}, u32[]{:S(2)}) collective-permute-start(bf16[192,128]{1,0:T(8,128)(2,1)S(1)} %get-tuple-element.9), channel_id=1, source_target_pairs={{1,0},{2,1},{3,2},{4,3},{5,4},{6,5},{7,6},{9,8},{10,9},{11,10},{12... | collective-permute-start | bytes 147464 | tf_op jit(solution)/shard_map/ppermute | solution.py:330
  114.0 0.0 copy-done.7
  114.0 0.1 copy.33
  114.1 0.1 reshape.221.stencil
  114.2 0.0 copy-done.6
  114.2 0.1 copy.37
  114.3 1.2 copy.41
  115.5 1.4 %collective-permute-done = bf16[192,128]{1,0:T(8,128)(2,1)S(1)} collective-permute-done((bf16[192,128]{1,0:T(8,128)(2,1)S(1)}, bf16[192,128]{1,0:T(8,128)(2,1)S(1)}, u32[]{:S(2)}, u32[]{:S(2)}) %collective-permute-start) | collective-permute-done | bytes 49184 | tf_op jit(solution)/shard_map/ppermute | solution.py:330
  116.9 0.6 broadcast_in_dim.11.vweight
  117.5 0.0 copy-done.2
  117.5 0.0 copy-done.3
  117.5 6.3 %arrive.1 = bf16[256,3,16,128]{3,2,1,0:T(8,128)(2,1)} custom-call(s32[1024]{0:T(1024)S(1)} %reshape.221.stencil, s32[1]{0:T(128)} %bitcast.9.at_top, bf16[64,48,128]{2,1,0:T(8,128)(2,1)S(1)} %copy-done.2, f32[192,128]{1,0:T(8,128)S(1)} %convert_element_type.58.above, f32[256,4,128]{2,1,0:T(4,128)S(1)} %copy-done.3, f32[256,16,128]{2,1,0:T(8,128)S(1)} %broadcast_in_dim.11.vweight), custom_call_target="tpu_custom_call" | custom-call | tf_op jit(solution)/shard_map/arrive/pallas_call | solution.py:334
  (21 shorter events, 0.1 us)
Async XLA Ops:
  4.7 1.0 copy-start.4
  5.7 0.7 copy-start.5
  10.6 12.0 %copy-start.8 = (s32[64,1]{0,1:T(1,128)S(1)}, s32[64,1]{0,1:T(1,128)}, u32[]{:S(2)}) copy-start(s32[64,1]{0,1:T(1,128)} %param.11) | copy-start | bytes 772
  10.6 36.6 %all-to-all-start = ((bf16[32,128,128]{2,1,0:T(8,128)(2,1)}), bf16[32,128,128]{2,1,0:T(8,128)(2,1)S(1)}, u32[]{:S(2)}, u32[]{:S(2)}) async-start(bf16[32,128,128]{2,1,0:T(8,128)(2,1)} %pack.1), calls=%async_computation | async-start | bytes 2097152 | tf_op jit(solution)/shard_map/all_to_all | solution.py:263
  47.3 12.4 %copy-start = (bf16[32,128,128]{2,1,0:T(8,128)(2,1)}, bf16[32,128,128]{2,1,0:T(8,128)(2,1)S(1)}, u32[]{:S(2)}) copy-start(bf16[32,128,128]{2,1,0:T(8,128)(2,1)S(1)} %all-to-all-done.arrived) | copy-start | bytes 3145732
  59.6 45.4 %all-to-all-start.1 = ((bf16[32,64,384]{2,1,0:T(8,128)(2,1)}), bf16[32,64,384]{2,1,0:T(8,128)(2,1)S(1)}, u32[]{:S(2)}, u32[]{:S(2)}) async-start(bf16[32,64,384]{2,1,0:T(8,128)(2,1)} %get-tuple-element.7), calls=%async_computation.1 | async-start | bytes 3145728 | tf_op jit(solution)/shard_map/all_to_all | solution.py:300
  105.0 8.9 %copy-start.7 = (s32[256,4]{0,1:T(4,128)S(1)}, s32[256,4]{0,1:T(4,128)}, u32[]{:S(2)}) copy-start(s32[256,4]{0,1:T(4,128)} %param.13) | copy-start | bytes 12292
  105.0 9.2 %copy-start.6 = (f32[256,16]{0,1:T(8,128)S(1)}, f32[256,16]{0,1:T(8,128)}, u32[]{:S(2)}) copy-start(f32[256,16]{0,1:T(8,128)} %param.15) | copy-start | bytes 49156
  107.6 0.9 copy-start.1
  108.5 8.4 %collective-permute-start = (bf16[192,128]{1,0:T(8,128)(2,1)S(1)}, bf16[192,128]{1,0:T(8,128)(2,1)S(1)}, u32[]{:S(2)}, u32[]{:S(2)}) collective-permute-start(bf16[192,128]{1,0:T(8,128)(2,1)S(1)} %get-tuple-element.9), channel_id=1, source_target_pairs={{1,0},{2,1},{3,2},{4,3},{5,4},{6,5},{7,6},{9,8},{10,9},{11,10},{12... | collective-permute-start | bytes 147464 | tf_op jit(solution)/shard_map/ppermute | solution.py:330
  115.5 2.0 %copy-start.2 = (bf16[64,48,128]{2,1,0:T(8,128)(2,1)S(1)}, bf16[64,48,128]{2,1,0:T(8,128)(2,1)}, u32[]{:S(2)}) copy-start(bf16[64,48,128]{2,1,0:T(8,128)(2,1)} %copy-done.1) | copy-start | bytes 2359300
  115.5 2.0 %copy-start.3 = (f32[256,4,128]{2,1,0:T(4,128)S(1)}, f32[256,4,128]{2,1,0:T(4,128)}, u32[]{:S(2)}) copy-start(f32[256,4,128]{2,1,0:T(4,128)} %hweight.1) | copy-start | bytes 1572868

commit v3 on v2

v3 whole, which is shorter than its diff:
```python
import math

import jax
import jax.numpy as jnp
from jax import lax
from jax.experimental import pallas as pl
from jax.experimental.pallas import tpu as pltpu
from jax.sharding import PartitionSpec as P

NLON = 2560
BLK = 128
BLOCKS_X = NLON // BLK
LANES = 128

diffusion = 3.0

NT = (((1,), (1,)), ((), ()))
NN = (((1,), (0,)), ((), ()))


def mxu(left, right, dims):
    return lax.dot_general(left, right, dims, preferred_element_type=jnp.float32)


def identity(size):
    rows = lax.broadcasted_iota(jnp.int32, (size, size), 0)
    columns = lax.broadcasted_iota(jnp.int32, (size, size), 1)
    return (rows == columns).astype(jnp.float32).astype(jnp.bfloat16)


def damping_curve(degrees):
    order_n = jnp.arange(degrees, dtype=jnp.float32)
    ratio = order_n * (order_n + 1.0) / float(degrees * (degrees - 1))
    return 1.0 / (1.0 + diffusion * ratio * ratio)


def pack_kernel(owner, send_ids, gauss, fourier, message, scratch, owned_by, slot_mask, weight):
    step = pl.program_id(0)
    chunk, fields, levels, columns = fourier.shape
    owners = owned_by.shape[0]
    lat_dev = weight.shape[0]
    tiles = scratch.shape[0]

    @pl.when(step == 0)
    def _():
        waves = owner.shape[1]
        wave_at = lax.broadcasted_iota(jnp.int32, (waves, columns), 0)
        column = lax.broadcasted_iota(jnp.int32, (waves, columns), 1)
        square_row = lax.broadcasted_iota(jnp.int32, (waves, waves), 0)
        square_column = lax.broadcasted_iota(jnp.int32, (waves, waves), 1)
        listed = jnp.broadcast_to(owner[...], (waves, waves))
        upright = jnp.sum(jnp.where(square_row == square_column, listed, 0), axis=1, keepdims=True)
        upright = jnp.broadcast_to(upright, (waves, columns))
        column_owner = jnp.sum(jnp.where(wave_at == column // 2, upright, 0), axis=0, keepdims=True)
        earlier = (upright == jnp.broadcast_to(column_owner, (waves, columns))) & (wave_at < column // 2)
        column_rank = jnp.sum(jnp.where(earlier, 1, 0), axis=0, keepdims=True)
        owner_at = lax.broadcasted_iota(jnp.int32, (owners, columns), 0)
        owned_by[...] = jnp.where(owner_at == column_owner, 1.0, 0.0).astype(jnp.bfloat16)
        parts_at = lax.broadcasted_iota(jnp.int32, (16, columns), 0)
        part_column = lax.broadcasted_iota(jnp.int32, (16, columns), 1)
        in_slot = parts_at == 2 * column_rank + part_column % 2
        slot_mask[...] = jnp.where(in_slot, 1.0, 0.0).astype(jnp.bfloat16)
        turn_row = lax.broadcasted_iota(jnp.int32, (lat_dev, lat_dev), 0)
        turn_column = lax.broadcasted_iota(jnp.int32, (lat_dev, lat_dev), 1)
        weights = jnp.where(turn_row == turn_column, jnp.broadcast_to(gauss[...], (lat_dev, lat_dev)), 0.0)
        weight[...] = jnp.broadcast_to(jnp.sum(weights, axis=1, keepdims=True), weight.shape)

    chooser = owned_by[...]
    masks = [slot_mask[i : i + 1, :] for i in range(2 * (tiles * LANES) // (2 * fields * levels))]
    for k in range(chunk):
        t = step * chunk + k
        rows = fourier[k].reshape(fields * levels, columns).astype(jnp.float32)
        rows = (rows * weight[pl.ds(t, 1), :]).astype(jnp.bfloat16)
        parts = []
        for slot in range(len(masks) // 2):
            for field in range(fields):
                for part in range(2):
                    parts.append(rows[field * levels : (field + 1) * levels] * masks[2 * slot + part])
        spread = jnp.concatenate(parts, axis=0)
        chosen = mxu(chooser, spread, NT)
        for tile in range(tiles):
            scratch[tile, pl.ds(t, owners, stride=lat_dev), :] = chosen[:, tile * LANES : (tile + 1) * LANES]

    @pl.when(step == pl.num_programs(0) - 1)
    def _():
        ids = send_ids[...].astype(jnp.float32)
        in_row = jnp.floor((ids + 0.5) * (1.0 / BLOCKS_X))
        in_column = ids - in_row * BLOCKS_X
        sides = [in_row[k : k + 1] for k in range(ids.shape[0])] + [in_column[k : k + 1] for k in range(ids.shape[0])]
        extra = jnp.broadcast_to(jnp.concatenate(sides, axis=1), (8, LANES))
        for o in range(owners):
            parts = [scratch[tile, o * lat_dev : (o + 1) * lat_dev, :] for tile in range(tiles)]
            message[o] = jnp.concatenate(parts + [extra], axis=0).astype(jnp.bfloat16)


def spectral_kernel(arrived, tables, damping, spectral, message, turned, rows_at, listed, row_of, listed_sem):
    slots, per_slot, degrees = spectral.shape
    half = per_slot // 2
    field_rows = half // 3
    bands = arrived.shape[0]
    tiles = turned.shape[0] // LANES
    lat_dev = (arrived.shape[1] - 8) // tiles
    latitudes = bands * lat_dev
    receivers, message_rows, message_lanes = message.shape
    lists = pltpu.make_async_copy(listed, row_of, listed_sem)

    wide = arrived[...].astype(jnp.float32)
    band = lax.broadcasted_iota(jnp.int32, (bands, LANES), 0)
    listed[...] = (wide[:, tiles * lat_dev, :].astype(jnp.int32) + band * lat_dev) * 8
    lists.start()
    unit = identity(LANES)
    for tile in range(tiles):
        columns = wide[:, tile * lat_dev : (tile + 1) * lat_dev, :].reshape(latitudes, LANES)
        turned[tile * LANES : (tile + 1) * LANES, :] = mxu(unit, columns.astype(jnp.bfloat16), NT).astype(jnp.bfloat16)

    gap = jnp.zeros((LANES - half, degrees), jnp.bfloat16)
    chunk = 256
    for slot in range(slots):
        own = turned[slot * per_slot : (slot + 1) * per_slot, :]
        spectra = mxu(own, tables[slot], NN)
        damped = (spectra * damping[slot : slot + 1, :]).astype(jnp.bfloat16)
        spectral[slot] = damped
        sides = []
        for part in range(2):
            for field in range(3):
                at = (2 * field + part) * field_rows
                sides.append(damped[at : at + field_rows])
            sides.append(gap)
        sides = jnp.concatenate(sides, axis=0)
        for at in range(0, latitudes, chunk):
            back = mxu(tables[slot, at : at + chunk, :], sides, NT)
            for part in range(2):
                rows_at[pl.ds(at * 2 * slots + slot * 2 + part, chunk, stride=2 * slots), :] = back[
                    :, part * LANES : (part + 1) * LANES
                ]

    lists.wait()
    lane = lax.broadcasted_iota(jnp.int32, (8, LANES), 1)
    wide_tiles = message_lanes // LANES

    def one_receiver(r, carry):
        for pair in range(message_rows // 16):
            halves = []
            for side in range(2):
                built = [None] * wide_tiles
                for e in range(8):
                    entry = (pair * 2 + side) * 8 + e
                    at = pl.multiple_of(row_of[entry // 2, receivers * (entry % 2) + r], 8)
                    row = rows_at[pl.ds(at, 8), :]
                    start = e * half
                    if start % LANES:
                        row = pltpu.roll(row, start % LANES, 1)
                    for tile in range(start // LANES, (start + half - 1) // LANES + 1):
                        first = start - tile * LANES
                        if built[tile] is None:
                            built[tile] = row
                        else:
                            built[tile] = jnp.where(lane >= first, row, built[tile])
                halves.append(jnp.concatenate(built, axis=1))
            both = jnp.concatenate(halves, axis=0).astype(jnp.bfloat16)
            message[r, pair * 16 : (pair + 1) * 16, :] = both
        return carry

    lax.fori_loop(0, receivers, one_receiver, 0, unroll=4)


def block_kernel(column_of, received, zonal, blocks, lowest, lowest_scratch):
    owners, message_rows, message_lanes = received.shape
    unit = identity(LANES)
    half = message_lanes // 8
    groups = message_rows // 8
    entries = blocks.shape[0]
    for pair in range(groups // 2):
        wide = received[:, pair * 16 : (pair + 1) * 16, :].astype(jnp.float32)
        for side in range(2):
            group = pair * 2 + side
            own = wide[:, side * 8 : (side + 1) * 8, :].reshape(owners * 8, message_lanes).astype(jnp.bfloat16)
            turned = [
                mxu(unit, own[:, tile * LANES : (tile + 1) * LANES], NT).astype(jnp.bfloat16)
                for tile in range(message_lanes // LANES)
            ]
            turned = jnp.concatenate(turned, axis=0)
            for e in range(8):
                entry = group * 8 + e
                made = mxu(turned[e * half : (e + 1) * half], zonal[column_of[entry]], NN)
                blocks[entry] = made.astype(jnp.bfloat16)
                for field in range(3):
                    lowest_scratch[field * entries + entry : field * entries + entry + 1, :] = made[
                        field * 16 : field * 16 + 1, :
                    ]
    lowest[...] = lowest_scratch[...].astype(jnp.bfloat16)


def arrive_kernel(stencil, at_top, blocks, above, hweight, vweight, arrival, wide, over_rows):
    entries = blocks.shape[0]
    step = pl.program_id(0)
    rows, fields, levels, _ = arrival.shape

    @pl.when(step == 0)
    def _():
        top = at_top[0] == 1
        over_rows[...] = above[...].astype(jnp.float32)

        def widen(entry, carry):
            block = blocks[entry].astype(jnp.float32)
            wide[entry, 0 : fields * levels, :] = block
            for field in range(fields):
                own_last = block[(field + 1) * levels - 1 : (field + 1) * levels, :]
                over = over_rows[pl.ds(field * entries + entry, 1), :]
                wide[entry, pl.ds(fields * levels + field, 1), :] = jnp.where(top, own_last, over)
            return carry

        lax.fori_loop(0, entries, widen, 0, unroll=4)

    level = lax.broadcasted_iota(jnp.int32, (levels, LANES), 0)

    def one_row(a, carry):
        total = None
        for q in range(4):
            place = stencil[(step * rows + a) * 4 + q]
            term = hweight[a, pl.ds(q, 1), :] * wide[place]
            total = term if total is None else total + term
        upper = vweight[a]
        for field in range(fields):
            here = total[field * levels : (field + 1) * levels]
            over = jnp.where(
                level == levels - 1,
                total[fields * levels + field : fields * levels + field + 1],
                pltpu.roll(here, levels - 1, 0),
            )
            arrival[a, field] = ((1.0 - upper) * here + upper * over).astype(jnp.bfloat16)
        return carry

    lax.fori_loop(0, rows, one_row, 0, unroll=4)


def whole(memory):
    return pl.BlockSpec(memory_space=memory)


def per_device(fourier, gauss, legendre, owner, send_list, stencil, hweight, vweight):
    lat_count = lax.axis_size("lat")
    device_row = lax.axis_index("lat")
    lat_dev, fields, levels, columns = fourier.shape
    wave_total = columns // 2
    slot_most = legendre.shape[1]
    degrees = legendre.shape[3]
    latitudes = legendre.shape[2]
    slot_count = lat_count * slot_most
    capacity = send_list.shape[2]
    arrivals = stencil.shape[0]
    half = fields * levels
    per_slot = 2 * half
    message_lanes = slot_most * per_slot
    tiles = message_lanes // LANES
    entries = lat_count * capacity

    owners = owner[:, 0]
    wave_index = jnp.arange(wave_total, dtype=jnp.int32)
    earlier = (owners[:, None] == owners[None, :]) & (wave_index[:, None] < wave_index[None, :])
    slot_rank = jnp.sum(earlier.astype(jnp.int32), axis=0)
    slot_of = owners * slot_most + slot_rank
    wave_number = wave_index * (degrees // wave_total)
    vmem = whole(pltpu.VMEM)
    smem = whole(pltpu.SMEM)
    chunk = 8
    message_one = pl.pallas_call(
        pack_kernel,
        grid=(lat_dev // chunk,),
        out_shape=jax.ShapeDtypeStruct((lat_count, tiles * lat_dev + 8, LANES), jnp.bfloat16),
        in_specs=[
            pl.BlockSpec((1, wave_total), lambda i: (0, 0)),
            pl.BlockSpec((capacity, lat_count), lambda i: (0, 0)),
            pl.BlockSpec((1, lat_dev), lambda i: (0, 0)),
            pl.BlockSpec((chunk, fields, levels, columns), lambda i: (i, 0, 0, 0)),
        ],
        out_specs=pl.BlockSpec((lat_count, tiles * lat_dev + 8, LANES), lambda i: (0, 0, 0)),
        scratch_shapes=[
            pltpu.VMEM((tiles, lat_count * lat_dev, LANES), jnp.float32),
            pltpu.VMEM((lat_count, columns), jnp.bfloat16),
            pltpu.VMEM((16, columns), jnp.bfloat16),
            pltpu.VMEM((lat_dev, columns), jnp.float32),
        ],
        compiler_params=pltpu.CompilerParams(vmem_limit_bytes=16 * 2**20),
        name="pack",
    )(owner.reshape(1, wave_total), send_list[0].T, gauss.reshape(1, lat_dev), fourier)
    arrived = lax.all_to_all(message_one, "lat", split_axis=0, concat_axis=0, tiled=True)

    placed = (slot_of[:, None] == jnp.arange(slot_count, dtype=jnp.int32)[None, :]).astype(jnp.int32)
    owned = lax.dynamic_slice_in_dim(placed, device_row * slot_most, slot_most, 1)
    filled = jnp.sum(owned, axis=0) > 0
    slot_wave = jnp.sum(owned * wave_number[:, None], axis=0)
    degree_index = jnp.arange(degrees, dtype=jnp.int32)
    keep_mask = (filled[:, None] & (degree_index[None, :] >= slot_wave[:, None])).astype(jnp.float32)
    damping = keep_mask * damping_curve(degrees)[None, :]

    message_shape = (lat_count, entries // 8 * slot_most * 2, 8 * half)
    spectral_rows, message_two = pl.pallas_call(
        spectral_kernel,
        in_specs=[vmem, vmem, vmem],
        out_specs=[vmem, vmem],
        scratch_shapes=[
            pltpu.VMEM((message_lanes, latitudes), jnp.bfloat16),
            pltpu.VMEM((latitudes * 2 * slot_most, LANES), jnp.float32),
            pltpu.VMEM((lat_count, LANES), jnp.int32),
            pltpu.SMEM((lat_count, LANES), jnp.int32),
            pltpu.SemaphoreType.DMA,
        ],
        out_shape=[
            jax.ShapeDtypeStruct((slot_most, per_slot, degrees), jnp.bfloat16),
            jax.ShapeDtypeStruct(message_shape, jnp.bfloat16),
        ],
        compiler_params=pltpu.CompilerParams(vmem_limit_bytes=24 * 2**20),
        name="spectral",
    )(arrived, legendre[0], damping)
    received = lax.all_to_all(message_two, "lat", split_axis=0, concat_axis=0, tiled=True)

    spectral = jnp.transpose(
        spectral_rows.reshape(slot_most, fields, 2, levels, degrees), (0, 1, 3, 2, 4)
    )
    slot_waves = jnp.sum(placed * wave_number[:, None], axis=0)
    present = (jnp.sum(placed, axis=0) > 0).astype(jnp.float32)
    points = jnp.arange(NLON, dtype=jnp.int32).reshape(BLOCKS_X, 1, 1, BLK)
    phases = slot_waves[None, :, None, None] * points % NLON
    angles = phases.astype(jnp.float32) * (2.0 * math.pi / NLON)
    norm_factor = present[None, :, None, None] / math.sqrt(wave_total)
    zonal = jnp.concatenate([jnp.cos(angles) * norm_factor, -jnp.sin(angles) * norm_factor], axis=2)
    zonal = zonal.astype(jnp.bfloat16).reshape(BLOCKS_X, slot_count * 2, BLK)
    all_columns = arrived[:, tiles * lat_dev, entries:].reshape(lat_count, capacity, lat_count)
    column_of = lax.dynamic_index_in_dim(all_columns, device_row, 2, keepdims=False)
    column_of = column_of.astype(jnp.int32).reshape(-1)
    lev_count = lax.axis_size("lev")
    at_top = (lax.axis_index("lev") == lev_count - 1).astype(jnp.int32).reshape(1)
    vertical = jnp.broadcast_to(vweight[:, :, None], (arrivals, levels, BLK))
    corners = stencil.reshape(-1)
    received, vertical, corners, at_top = lax.optimization_barrier((received, vertical, corners, at_top))
    blocks, lowest = pl.pallas_call(
        block_kernel,
        out_shape=[
            jax.ShapeDtypeStruct((entries, half, BLK), jnp.bfloat16),
            jax.ShapeDtypeStruct((fields * entries, BLK), jnp.bfloat16),
        ],
        in_specs=[smem, vmem, vmem],
        out_specs=[vmem, vmem],
        scratch_shapes=[pltpu.VMEM((fields * entries, BLK), jnp.float32)],
        compiler_params=pltpu.CompilerParams(vmem_limit_bytes=16 * 2**20),
        name="blocks",
    )(column_of, received, zonal)

    above = lax.ppermute(lowest, "lev", [(i, i - 1) for i in range(1, lev_count)])
    step_rows = 32
    arrival = pl.pallas_call(
        arrive_kernel,
        grid_spec=pltpu.PrefetchScalarGridSpec(
            num_scalar_prefetch=2,
            grid=(arrivals // step_rows,),
            in_specs=[
                pl.BlockSpec((entries, half, BLK), lambda i, *_: (0, 0, 0)),
                pl.BlockSpec((fields * entries, BLK), lambda i, *_: (0, 0)),
                pl.BlockSpec((step_rows, 4, BLK), lambda i, *_: (i, 0, 0)),
                pl.BlockSpec((step_rows, levels, BLK), lambda i, *_: (i, 0, 0)),
            ],
            out_specs=pl.BlockSpec((step_rows, fields, levels, BLK), lambda i, *_: (i, 0, 0, 0)),
            scratch_shapes=[
                pltpu.VMEM((entries, half + 8, BLK), jnp.float32),
                pltpu.VMEM((fields * entries, BLK), jnp.float32),
            ],
        ),
        out_shape=jax.ShapeDtypeStruct((arrivals, fields, levels, BLK), jnp.bfloat16),
        compiler_params=pltpu.CompilerParams(vmem_limit_bytes=16 * 2**20),
        name="arrive",
    )(corners, at_top, blocks, above, hweight, vertical)
    return (spectral[None], arrival)


def solution(mesh):
    return jax.shard_map(
        per_device,
        mesh=mesh,
        in_specs=(
            P("lat", None, "lev", None),
            P("lat"),
            P("lat", None, None, None),
            P(),
            P("lat", None, None),
            P("lat", None),
            P("lat", None, None),
            P("lat", "lev"),
        ),
        out_specs=(P("lat", None, None, "lev", None, None), P("lat", None, "lev", None)),
        check_vma=False,
    )
```

time: 124 us -> 119 us (0.960)
  Pallas kernels: 25.5 us -> 20.8 us
  local copies, waits for them, and re-layouts: 8.77 us -> 10.9 us
  other arithmetic: 8.79 us -> 7.14 us
    pallas_call x2, Pallas kernels: 16.6 us -> 11.9 us  [the longest x1 8.63 us: per_device(): pl.pallas_call(spectral_kernel, in_specs=[vmem, vmem, vmem], out_specs=[v...]
    unnamed x20 -> x22, local copies, waits for them, and re-layouts: 2.82 us -> 6.51 us
  transfers between devices with their start and end apart: 3 -> 3, of which waited for: 3 -> 3; matrix products, arithmetic and copies ran while one was open for 8% -> 9% of each run, Pallas kernels for 0% -> 0%
where the time goes in v3:
time: 119 us
  waiting for transfers between devices  53.1 us (45%)
  starting transfers between devices  26.1 us (22%)
  Pallas kernels  20.8 us (17%)
  local copies, waits for them, and re-layouts  10.9 us (9%)
  other arithmetic  7.14 us (6%)
    all_to_all x1, waiting for transfers between devices, per_device(): lax.all_to_all(message_two, 'lat', split_axis=0, concat_axis=0, tiled=True)  27.1 us
    all_to_all x1, waiting for transfers between devices, per_device(): lax.all_to_all(message_one, 'lat', split_axis=0, concat_axis=0, tiled=True)  24.2 us
    all_to_all x1, starting transfers between devices, per_device(): lax.all_to_all(message_one, 'lat', split_axis=0, concat_axis=0, tiled=True)  12 us
    pallas_call x1, Pallas kernels, per_device(): pl.pallas_call(spectral_kernel, in_specs=[vmem, vmem, vmem], out_specs=[v...  8.63 us
    all_to_all x1, starting transfers between devices, per_device(): lax.all_to_all(message_two, 'lat', split_axis=0, concat_axis=0, tiled=True)  8.59 us
    unnamed x22, local copies, waits for them, and re-layouts  6.51 us
    pallas_call x1, Pallas kernels, per_device(): pl.pallas_call(arrive_kernel, grid_spec=pltpu.PrefetchScalarGridSpec(num_...  6.31 us
    another operation x1, other arithmetic  5.84 us
  transfers between devices with their start and end apart: 3, of which 3 were waited for; matrix products, arithmetic and copies ran while one was open for 9% of the time, Pallas kernels for 0%

profile of v3, /device:TPU:1, one launch (start us, length us, event | category | flops | bytes accessed | tf_op | source)
XLA Modules:
  0.0 118.8 jit_solution(4635762934072254967)
XLA Ops:
  0.6 0.0 copy-start.3
  0.6 1.0 copy-done.3
  1.7 0.0 copy-start.4
  1.7 0.7 copy-done.4
  2.3 0.0 copy-start.5
  2.3 0.7 copy-done.5
  3.0 0.0 copy-start.6
  3.0 0.7 copy-done.6
  3.7 3.3 %pack.1 = bf16[32,128,128]{2,1,0:T(8,128)(2,1)} custom-call(s32[1,64]{1,0:T(1,128)S(1)} %bitcast.26, s32[2,32]{1,0:T(2,128)S(1)} %bitcast.24, f32[1,40]{1,0:T(1,128)S(1)} %bitcast.25, bf16[40,3,16,128]{3,2,1,0:T(8,128)(2,1)S(1)} %copy-done.3), custom_call_target="tpu_custom_call" | custom-call | tf_op jit(solution)/shard_map/pack/pallas_call | solution.py:267
  6.9 0.0 copy-start.7
  6.9 12.0 %all-to-all-start = ((bf16[32,128,128]{2,1,0:T(8,128)(2,1)}), bf16[32,128,128]{2,1,0:T(8,128)(2,1)S(1)}, u32[]{:S(2)}, u32[]{:S(2)}) async-start(bf16[32,128,128]{2,1,0:T(8,128)(2,1)} %pack.1), calls=%async_computation | async-start | bytes 2097152 | tf_op jit(solution)/shard_map/all_to_all | solution.py:287
  19.0 0.0 copy-done.7
  19.0 0.1 convert_reduce_fusion.1
  19.1 0.2 dynamic-slice_reduce_fusion
  19.3 0.1 fusion.9.damping
  19.3 24.2 %all-to-all-done.arrived = bf16[32,128,128]{2,1,0:T(8,128)(2,1)S(1)} async-done(((bf16[32,128,128]{2,1,0:T(8,128)(2,1)}), bf16[32,128,128]{2,1,0:T(8,128)(2,1)S(1)}, u32[]{:S(2)}, u32[]{:S(2)}) %all-to-all-start) | async-done | bytes 1048608 | tf_op jit(solution)/shard_map/all_to_all | solution.py:287
  43.6 0.0 copy-start.1
  43.6 0.0 copy-start
  43.6 3.2 %copy-done = bf16[1,4,1280,640]{3,2,1,0:T(8,128)(2,1)S(1)} copy-done((bf16[1,4,1280,640]{3,2,1,0:T(8,128)(2,1)S(1)}, bf16[1,4,1280,640]{3,2,1,0:T(8,128)(2,1)}, u32[]{:S(2)}) %copy-start) | copy-done | bytes 6553624
  46.8 8.6 %spectral.1 = (bf16[4,96,640]{2,1,0:T(8,128)(2,1)S(1)}, bf16[32,64,384]{2,1,0:T(8,128)(2,1)}) custom-call(bf16[32,128,128]{2,1,0:T(8,128)(2,1)S(1)} %all-to-all-done.arrived, bf16[4,1280,640]{2,1,0:T(8,128)(2,1)S(1)} %bitcast.21, f32[4,640]{1,0:T(4,128)S(1)} %fusion.9.damping), custom_call_target="tpu_custom_call" | custom-call | tf_op jit(solution)/shard_map/spectral/pallas_call | solution.py:298
  55.4 0.0 copy-done.1
  55.5 0.0 copy-start.9
  55.5 0.0 copy-start.8
  55.5 8.6 %all-to-all-start.1 = ((bf16[32,64,384]{2,1,0:T(8,128)(2,1)}), bf16[32,64,384]{2,1,0:T(8,128)(2,1)S(1)}, u32[]{:S(2)}, u32[]{:S(2)}) async-start(bf16[32,64,384]{2,1,0:T(8,128)(2,1)} %get-tuple-element.11), calls=%async_computation.1 | async-start | bytes 3145728 | tf_op jit(solution)/shard_map/all_to_all | solution.py:316
  64.1 0.0 copy-done.9
  64.1 0.1 copy.23
  64.2 0.1 reshape.145.stencil
  64.4 0.0 copy-done.8
  64.4 0.1 copy.22
  64.5 0.1 select_reduce_fusion
  64.6 5.8 %multiply_convert_fusion.1 = (bf16[20,128,1,128]{3,1,2,0:T(8,128)(2,1)S(1)}, bf16[20,128,1,128]{3,1,2,0:T(8,128)(2,1)S(1)}) fusion(f32[128]{0:T(128)S(1)} %compare_select_fusion, s32[20,128]{1,0:T(8,128)S(1)} %multiply_add_fusion, s32[128]{0:T(128)S(1)} %get-tuple-element.20), kind=kLoop, calls=%fused_computation.5 | loop fusion | flops 4587520 | bytes 1321984 | tf_op jit(solution)/shard_map/convert.2
  70.4 0.1 pad_maximum_fusion
  70.6 1.4 %copy.26 = bf16[20,128,2,128]{3,2,1,0:T(2,128)(2,1)S(1)} copy(bf16[20,128,2,128]{3,1,2,0:T(8,128)(2,1)S(1)} %pad_maximum_fusion) | data formatting | bytes 2621440 | tf_op jit(solution)/shard_map/concatenate | solution.py:327
  71.9 1.0 slice_reduce_fusion
  72.9 0.1 reshape_squeeze.3
  73.0 0.7 convert_reduce_fusion
  73.7 0.1 reshape.153.column_of
  73.8 27.1 %all-to-all-done.1.received = bf16[32,64,384]{2,1,0:T(8,128)(2,1)S(1)} async-done(((bf16[32,64,384]{2,1,0:T(8,128)(2,1)}), bf16[32,64,384]{2,1,0:T(8,128)(2,1)S(1)}, u32[]{:S(2)}, u32[]{:S(2)}) %all-to-all-start.1) | async-done | bytes 1572896 | tf_op jit(solution)/shard_map/all_to_all | solution.py:316
  100.9 0.6 broadcast_in_dim.5.vweight
  101.5 0.0 copy-start.2
  101.5 2.5 %blocks.1 = (bf16[64,48,128]{2,1,0:T(8,128)(2,1)S(1)}, bf16[192,128]{1,0:T(8,128)(2,1)S(1)}) custom-call(s32[64]{0:T(128)S(1)} %reshape.153.column_of, bf16[32,64,384]{2,1,0:T(8,128)(2,1)S(1)} %all-to-all-done.1.received, bf16[20,256,128]{2,1,0:T(8,128)(2,1)S(1)} %bitcast.22), custom_call_target="tpu_custom_call" | custom-call | tf_op jit(solution)/shard_map/blocks/pallas_call | solution.py:337
  104.0 5.5 %collective-permute-start = (bf16[192,128]{1,0:T(8,128)(2,1)S(1)}, bf16[192,128]{1,0:T(8,128)(2,1)S(1)}, u32[]{:S(2)}, u32[]{:S(2)}) collective-permute-start(bf16[192,128]{1,0:T(8,128)(2,1)S(1)} %get-tuple-element.16), channel_id=1, source_target_pairs={{1,0},{2,1},{3,2},{4,3},{5,4},{6,5},{7,6},{9,8},{10,9},{11,10},{12... | collective-permute-start | bytes 147464 | tf_op jit(solution)/shard_map/ppermute | solution.py:350
  109.5 1.2 copy.30
  110.7 1.8 %collective-permute-done.above = bf16[192,128]{1,0:T(8,128)(2,1)S(1)} collective-permute-done((bf16[192,128]{1,0:T(8,128)(2,1)S(1)}, bf16[192,128]{1,0:T(8,128)(2,1)S(1)}, u32[]{:S(2)}, u32[]{:S(2)}) %collective-permute-start) | collective-permute-done | bytes 49184 | tf_op jit(solution)/shard_map/ppermute | solution.py:350
  112.5 0.0 copy-done.2
  112.5 6.3 %arrive.1 = bf16[256,3,16,128]{3,2,1,0:T(8,128)(2,1)} custom-call(s32[1024]{0:T(1024)S(1)} %reshape.145.stencil, s32[1]{0:T(128)} %bitcast.11.at_top, bf16[64,48,128]{2,1,0:T(8,128)(2,1)S(1)} %get-tuple-element.15.blocks, bf16[192,128]{1,0:T(8,128)(2,1)S(1)} %collective-permute-done.above, f32[256,4,128]{2,1,0:T(4,128)S(1)} %copy-done.2, ...), custom_call_target="tpu_custom_call" | custom-call | tf_op jit(solution)/shard_map/arrive/pallas_call | solution.py:352
  (7 shorter events, 0.1 us)
Async XLA Ops:
  0.6 1.0 copy-start.3
  1.7 0.7 copy-start.4
  2.3 0.7 copy-start.5
  3.0 0.7 copy-start.6
  6.9 12.0 %copy-start.7 = (s32[64,1]{0,1:T(1,128)S(1)}, s32[64,1]{0,1:T(1,128)}, u32[]{:S(2)}) copy-start(s32[64,1]{0,1:T(1,128)} %param.11) | copy-start | bytes 772
  6.9 36.6 %all-to-all-start = ((bf16[32,128,128]{2,1,0:T(8,128)(2,1)}), bf16[32,128,128]{2,1,0:T(8,128)(2,1)S(1)}, u32[]{:S(2)}, u32[]{:S(2)}) async-start(bf16[32,128,128]{2,1,0:T(8,128)(2,1)} %pack.1), calls=%async_computation | async-start | bytes 2097152 | tf_op jit(solution)/shard_map/all_to_all | solution.py:287
  43.6 11.9 %copy-start.1 = (bf16[32,128,128]{2,1,0:T(8,128)(2,1)}, bf16[32,128,128]{2,1,0:T(8,128)(2,1)S(1)}, u32[]{:S(2)}) copy-start(bf16[32,128,128]{2,1,0:T(8,128)(2,1)S(1)} %all-to-all-done.arrived) | copy-start | bytes 3145732
  43.6 3.2 %copy-start = (bf16[1,4,1280,640]{3,2,1,0:T(8,128)(2,1)S(1)}, bf16[1,4,1280,640]{3,2,1,0:T(8,128)(2,1)}, u32[]{:S(2)}) copy-start(bf16[1,4,1280,640]{3,2,1,0:T(8,128)(2,1)} %param.10) | copy-start | bytes 19660804
  55.5 8.6 %copy-start.9 = (s32[256,4]{0,1:T(4,128)S(1)}, s32[256,4]{0,1:T(4,128)}, u32[]{:S(2)}) copy-start(s32[256,4]{0,1:T(4,128)} %param.13) | copy-start | bytes 12292
  55.5 8.9 %copy-start.8 = (f32[256,16]{0,1:T(8,128)S(1)}, f32[256,16]{0,1:T(8,128)}, u32[]{:S(2)}) copy-start(f32[256,16]{0,1:T(8,128)} %param.15) | copy-start | bytes 49156
  55.5 45.4 %all-to-all-start.1 = ((bf16[32,64,384]{2,1,0:T(8,128)(2,1)}), bf16[32,64,384]{2,1,0:T(8,128)(2,1)S(1)}, u32[]{:S(2)}, u32[]{:S(2)}) async-start(bf16[32,64,384]{2,1,0:T(8,128)(2,1)} %get-tuple-element.11), calls=%async_computation.1 | async-start | bytes 3145728 | tf_op jit(solution)/shard_map/all_to_all | solution.py:316
  101.5 11.0 %copy-start.2 = (f32[256,4,128]{2,1,0:T(4,128)S(1)}, f32[256,4,128]{2,1,0:T(4,128)}, u32[]{:S(2)}) copy-start(f32[256,4,128]{2,1,0:T(4,128)} %hweight.1) | copy-start | bytes 1572868
  104.0 8.4 %collective-permute-start = (bf16[192,128]{1,0:T(8,128)(2,1)S(1)}, bf16[192,128]{1,0:T(8,128)(2,1)S(1)}, u32[]{:S(2)}, u32[]{:S(2)}) collective-permute-start(bf16[192,128]{1,0:T(8,128)(2,1)S(1)} %get-tuple-element.16), channel_id=1, source_target_pairs={{1,0},{2,1},{3,2},{4,3},{5,4},{6,5},{7,6},{9,8},{10,9},{11,10},{12... | collective-permute-start | bytes 147464 | tf_op jit(solution)/shard_map/ppermute | solution.py:350

commit v4 on v3

v4 whole, which is shorter than its diff:
```python
import math

import jax
import jax.numpy as jnp
from jax import lax
from jax.experimental import pallas as pl
from jax.experimental.pallas import tpu as pltpu
from jax.sharding import PartitionSpec as P

NLON = 2560
BLK = 128
BLOCKS_X = NLON // BLK
LANES = 128
GRANT = 56 * 2**20

diffusion = 3.0

NT = (((1,), (1,)), ((), ()))
NN = (((1,), (0,)), ((), ()))


def mxu(left, right, dims):
    return lax.dot_general(left, right, dims, preferred_element_type=jnp.float32)


def identity(size):
    rows = lax.broadcasted_iota(jnp.int32, (size, size), 0)
    columns = lax.broadcasted_iota(jnp.int32, (size, size), 1)
    return (rows == columns).astype(jnp.float32).astype(jnp.bfloat16)


def damping_curve(degrees):
    order_n = jnp.arange(degrees, dtype=jnp.float32)
    ratio = order_n * (order_n + 1.0) / float(degrees * (degrees - 1))
    return 1.0 / (1.0 + diffusion * ratio * ratio)


def pack_kernel(
    owner_in, ids_in, gauss_in, fourier_in, message, owner, send_ids, gauss, fourier, packed, scratch, weight, in_sem, out_sem
):
    lat_dev, fields, levels, columns = fourier.shape
    owners = packed.shape[0]
    tiles = scratch.shape[0]
    slots = (tiles * LANES) // (2 * fields * levels)
    chunk = 8
    pieces = lat_dev // chunk
    small = [
        pltpu.make_async_copy(source, target, in_sem.at[pieces + i])
        for i, (source, target) in enumerate(((owner_in, owner), (ids_in, send_ids), (gauss_in, gauss)))
    ]
    large = [
        pltpu.make_async_copy(
            fourier_in.at[pl.ds(i * chunk, chunk)], fourier.at[pl.ds(i * chunk, chunk)], in_sem.at[i]
        )
        for i in range(pieces)
    ]
    for copy in small + large:
        copy.start()
    for copy in small:
        copy.wait()

    waves = owner.shape[1]
    wave_at = lax.broadcasted_iota(jnp.int32, (waves, columns), 0)
    column = lax.broadcasted_iota(jnp.int32, (waves, columns), 1)
    square_row = lax.broadcasted_iota(jnp.int32, (waves, waves), 0)
    square_column = lax.broadcasted_iota(jnp.int32, (waves, waves), 1)
    listed = jnp.broadcast_to(owner[...], (waves, waves))
    upright = jnp.sum(jnp.where(square_row == square_column, listed, 0), axis=1, keepdims=True)
    upright = jnp.broadcast_to(upright, (waves, columns))
    column_owner = jnp.sum(jnp.where(wave_at == column // 2, upright, 0), axis=0, keepdims=True)
    earlier = (upright == jnp.broadcast_to(column_owner, (waves, columns))) & (wave_at < column // 2)
    column_rank = jnp.sum(jnp.where(earlier, 1, 0), axis=0, keepdims=True)
    owner_at = lax.broadcasted_iota(jnp.int32, (owners, columns), 0)
    chooser = jnp.where(owner_at == column_owner, 1.0, 0.0).astype(jnp.bfloat16)
    part_of = 2 * column_rank + lax.broadcasted_iota(jnp.int32, (1, columns), 1) % 2
    masks = [
        jnp.broadcast_to(jnp.where(part_of == i, 1.0, 0.0), (levels, columns)).astype(jnp.bfloat16)
        for i in range(2 * slots)
    ]
    turn_row = lax.broadcasted_iota(jnp.int32, (lat_dev, lat_dev), 0)
    turn_column = lax.broadcasted_iota(jnp.int32, (lat_dev, lat_dev), 1)
    weights = jnp.where(turn_row == turn_column, jnp.broadcast_to(gauss[...], (lat_dev, lat_dev)), 0.0)
    weight[...] = jnp.broadcast_to(jnp.sum(weights, axis=1, keepdims=True), weight.shape)

    for t in range(lat_dev):
        if t % chunk == 0:
            large[t // chunk].wait()
        rows = fourier[t].reshape(fields * levels, columns).astype(jnp.float32)
        rows = (rows * weight[t : t + 1, :]).astype(jnp.bfloat16)
        parts = []
        for slot in range(slots):
            for field in range(fields):
                for part in range(2):
                    parts.append(rows[field * levels : (field + 1) * levels] * masks[2 * slot + part])
        spread = jnp.concatenate(parts, axis=0)
        chosen = mxu(chooser, spread, NT)
        for tile in range(tiles):
            scratch[tile, pl.ds(t, owners, stride=lat_dev), :] = chosen[:, tile * LANES : (tile + 1) * LANES]

    ids = send_ids[...].astype(jnp.float32)
    in_row = jnp.floor((ids + 0.5) * (1.0 / BLOCKS_X))
    in_column = ids - in_row * BLOCKS_X
    sides = [in_row[k : k + 1] for k in range(ids.shape[0])] + [in_column[k : k + 1] for k in range(ids.shape[0])]
    extra = jnp.broadcast_to(jnp.concatenate(sides, axis=1), (8, LANES))
    group = 8
    copies = []
    for o in range(owners):
        parts = [scratch[tile, o * lat_dev : (o + 1) * lat_dev, :] for tile in range(tiles)]
        packed[o] = jnp.concatenate(parts + [extra], axis=0).astype(jnp.bfloat16)
        if o % group == group - 1:
            first = o + 1 - group
            copies.append(
                pltpu.make_async_copy(
                    packed.at[pl.ds(first, group)], message.at[pl.ds(first, group)], out_sem.at[o // group]
                )
            )
            copies[-1].start()
    for copy in copies:
        copy.wait()


def spectral_kernel(
    arrived, tables_in, damping, spectral, message, tables, made, turned, rows_at, listed, row_of, listed_sem, in_sem, out_sem
):
    slots, per_slot, degrees = spectral.shape
    fetches = [pltpu.make_async_copy(tables_in.at[i], tables.at[i], in_sem.at[i]) for i in range(slots)]
    for fetch in fetches:
        fetch.start()
    half = per_slot // 2
    field_rows = half // 3
    bands = arrived.shape[0]
    tiles = turned.shape[0] // LANES
    lat_dev = (arrived.shape[1] - 8) // tiles
    latitudes = bands * lat_dev
    receivers, message_rows, message_lanes = message.shape
    lists = pltpu.make_async_copy(listed, row_of, listed_sem)

    wide = arrived[...].astype(jnp.float32)
    band = lax.broadcasted_iota(jnp.int32, (bands, LANES), 0)
    listed[...] = (wide[:, tiles * lat_dev, :].astype(jnp.int32) + band * lat_dev) * 8
    lists.start()
    unit = identity(LANES)
    for tile in range(tiles):
        columns = wide[:, tile * lat_dev : (tile + 1) * lat_dev, :].reshape(latitudes, LANES)
        turned[tile * LANES : (tile + 1) * LANES, :] = mxu(unit, columns.astype(jnp.bfloat16), NT).astype(jnp.bfloat16)

    gap = jnp.zeros((LANES - half, degrees), jnp.bfloat16)
    chunk = 256
    for slot in range(slots):
        own = turned[slot * per_slot : (slot + 1) * per_slot, :]
        fetches[slot].wait()
        spectra = mxu(own, tables[slot], NN)
        damped = (spectra * damping[slot : slot + 1, :]).astype(jnp.bfloat16)
        spectral[slot] = damped
        sides = []
        for part in range(2):
            for field in range(3):
                at = (2 * field + part) * field_rows
                sides.append(damped[at : at + field_rows])
            sides.append(gap)
        sides = jnp.concatenate(sides, axis=0)
        for at in range(0, latitudes, chunk):
            back = mxu(tables[slot, at : at + chunk, :], sides, NT)
            for part in range(2):
                rows_at[pl.ds(at * 2 * slots + slot * 2 + part, chunk, stride=2 * slots), :] = back[
                    :, part * LANES : (part + 1) * LANES
                ]

    lists.wait()
    lane = lax.broadcasted_iota(jnp.int32, (8, LANES), 1)
    wide_tiles = message_lanes // LANES

    group = 4
    groups = receivers // group

    def send(g):
        at = pl.multiple_of(g * group, group)
        return pltpu.make_async_copy(made.at[pl.ds(at, group)], message.at[pl.ds(at, group)], out_sem.at[g])

    def one_group(g, carry):
        for k in range(group):
            r = g * group + k
            for pair in range(message_rows // 16):
                halves = []
                for side in range(2):
                    built = [None] * wide_tiles
                    for e in range(8):
                        entry = (pair * 2 + side) * 8 + e
                        at = pl.multiple_of(row_of[entry // 2, receivers * (entry % 2) + r], 8)
                        row = rows_at[pl.ds(at, 8), :]
                        start = e * half
                        if start % LANES:
                            row = pltpu.roll(row, start % LANES, 1)
                        for tile in range(start // LANES, (start + half - 1) // LANES + 1):
                            first = start - tile * LANES
                            if built[tile] is None:
                                built[tile] = row
                            else:
                                built[tile] = jnp.where(lane >= first, row, built[tile])
                    halves.append(jnp.concatenate(built, axis=1))
                both = jnp.concatenate(halves, axis=0).astype(jnp.bfloat16)
                made[r, pair * 16 : (pair + 1) * 16, :] = both
        send(g).start()
        return carry

    lax.fori_loop(0, groups, one_group, 0)
    for g in range(groups):
        send(g).wait()


def block_kernel(column_of, received, zonal, blocks, lowest, lowest_scratch):
    owners, message_rows, message_lanes = received.shape
    unit = identity(LANES)
    half = message_lanes // 8
    groups = message_rows // 8
    entries = blocks.shape[0]
    for pair in range(groups // 2):
        wide = received[:, pair * 16 : (pair + 1) * 16, :].astype(jnp.float32)
        for side in range(2):
            group = pair * 2 + side
            own = wide[:, side * 8 : (side + 1) * 8, :].reshape(owners * 8, message_lanes).astype(jnp.bfloat16)
            turned = [
                mxu(unit, own[:, tile * LANES : (tile + 1) * LANES], NT).astype(jnp.bfloat16)
                for tile in range(message_lanes // LANES)
            ]
            turned = jnp.concatenate(turned, axis=0)
            for e in range(8):
                entry = group * 8 + e
                made = mxu(turned[e * half : (e + 1) * half], zonal[column_of[entry]], NN)
                blocks[entry] = made.astype(jnp.bfloat16)
                for field in range(3):
                    lowest_scratch[field * entries + entry : field * entries + entry + 1, :] = made[
                        field * 16 : field * 16 + 1, :
                    ]
    lowest[...] = lowest_scratch[...].astype(jnp.bfloat16)


def arrive_kernel(stencil, at_top, blocks, above, hweight, vweight, arrival, made, wide, over_rows, out_sem):
    entries = blocks.shape[0]
    rows, fields, levels, _ = made.shape
    top = at_top[0] == 1
    over_rows[...] = above[...].astype(jnp.float32)

    def widen(entry, carry):
        block = blocks[entry].astype(jnp.float32)
        wide[entry, 0 : fields * levels, :] = block
        for field in range(fields):
            own_last = block[(field + 1) * levels - 1 : (field + 1) * levels, :]
            over = over_rows[pl.ds(field * entries + entry, 1), :]
            wide[entry, pl.ds(fields * levels + field, 1), :] = jnp.where(top, own_last, over)
        return carry

    lax.fori_loop(0, entries, widen, 0, unroll=4)

    level = lax.broadcasted_iota(jnp.int32, (levels, LANES), 0)
    together = 8
    piece = 32
    pieces = rows // piece

    def send(i):
        at = pl.multiple_of(i * piece, piece)
        return pltpu.make_async_copy(made.at[pl.ds(at, piece)], arrival.at[pl.ds(at, piece)], out_sem.at[i])

    def some_rows(i, carry):
        first = i * together
        tile = pl.multiple_of((first // LANES) * LANES, LANES)
        uppers = pltpu.roll(vweight[:, pl.ds(tile, LANES)], (LANES - first % LANES) % LANES, 1)
        for k in range(together):
            a = first + k
            total = None
            for q in range(4):
                term = hweight[a, q : q + 1, :] * wide[stencil[q, a]]
                total = term if total is None else total + term
            upper = jnp.broadcast_to(uppers[:, k : k + 1], (levels, LANES))
            lower = 1.0 - upper
            for field in range(fields):
                here = total[field * levels : (field + 1) * levels]
                over = jnp.where(
                    level == levels - 1,
                    total[fields * levels + field : fields * levels + field + 1],
                    pltpu.roll(here, levels - 1, 0),
                )
                made[a, field] = (lower * here + upper * over).astype(jnp.bfloat16)

        @pl.when(i % (piece // together) == piece // together - 1)
        def _():
            send(i // (piece // together)).start()

        return carry

    lax.fori_loop(0, rows // together, some_rows, 0)
    for i in range(pieces):
        send(i).wait()


def whole(memory):
    return pl.BlockSpec(memory_space=memory)


def per_device(fourier, gauss, legendre, owner, send_list, stencil, hweight, vweight):
    lat_count = lax.axis_size("lat")
    device_row = lax.axis_index("lat")
    lat_dev, fields, levels, columns = fourier.shape
    wave_total = columns // 2
    slot_most = legendre.shape[1]
    degrees = legendre.shape[3]
    latitudes = legendre.shape[2]
    slot_count = lat_count * slot_most
    capacity = send_list.shape[2]
    arrivals = stencil.shape[0]
    half = fields * levels
    per_slot = 2 * half
    message_lanes = slot_most * per_slot
    tiles = message_lanes // LANES
    entries = lat_count * capacity

    owners = owner[:, 0]
    wave_index = jnp.arange(wave_total, dtype=jnp.int32)
    earlier = (owners[:, None] == owners[None, :]) & (wave_index[:, None] < wave_index[None, :])
    slot_rank = jnp.sum(earlier.astype(jnp.int32), axis=0)
    slot_of = owners * slot_most + slot_rank
    wave_number = wave_index * (degrees // wave_total)
    vmem = whole(pltpu.VMEM)
    smem = whole(pltpu.SMEM)
    hbm = whole(pl.ANY)
    message_one = pl.pallas_call(
        pack_kernel,
        out_shape=jax.ShapeDtypeStruct((lat_count, tiles * lat_dev + 8, LANES), jnp.bfloat16),
        in_specs=[hbm, hbm, hbm, hbm],
        out_specs=hbm,
        scratch_shapes=[
            pltpu.VMEM((1, wave_total), jnp.int32),
            pltpu.VMEM((capacity, lat_count), jnp.int32),
            pltpu.VMEM((1, lat_dev), jnp.float32),
            pltpu.VMEM(fourier.shape, jnp.bfloat16),
            pltpu.VMEM((lat_count, tiles * lat_dev + 8, LANES), jnp.bfloat16),
            pltpu.VMEM((tiles, lat_count * lat_dev, LANES), jnp.float32),
            pltpu.VMEM((lat_dev, columns), jnp.float32),
            pltpu.SemaphoreType.DMA((lat_dev // 8 + 3,)),
            pltpu.SemaphoreType.DMA((lat_count // 8,)),
        ],
        compiler_params=pltpu.CompilerParams(vmem_limit_bytes=GRANT),
        name="pack",
    )(owner.reshape(1, wave_total), send_list[0].T, gauss.reshape(1, lat_dev), fourier)
    arrived = lax.all_to_all(message_one, "lat", split_axis=0, concat_axis=0, tiled=True)

    placed = (slot_of[:, None] == jnp.arange(slot_count, dtype=jnp.int32)[None, :]).astype(jnp.int32)
    owned = lax.dynamic_slice_in_dim(placed, device_row * slot_most, slot_most, 1)
    filled = jnp.sum(owned, axis=0) > 0
    slot_wave = jnp.sum(owned * wave_number[:, None], axis=0)
    degree_index = jnp.arange(degrees, dtype=jnp.int32)
    keep_mask = (filled[:, None] & (degree_index[None, :] >= slot_wave[:, None])).astype(jnp.float32)
    damping = keep_mask * damping_curve(degrees)[None, :]

    message_shape = (lat_count, entries // 8 * slot_most * 2, 8 * half)
    spectral_rows, message_two = pl.pallas_call(
        spectral_kernel,
        in_specs=[vmem, hbm, vmem],
        out_specs=[vmem, hbm],
        scratch_shapes=[
            pltpu.VMEM((slot_most, latitudes, degrees), jnp.bfloat16),
            pltpu.VMEM(message_shape, jnp.bfloat16),
            pltpu.VMEM((message_lanes, latitudes), jnp.bfloat16),
            pltpu.VMEM((latitudes * 2 * slot_most, LANES), jnp.float32),
            pltpu.VMEM((lat_count, LANES), jnp.int32),
            pltpu.SMEM((lat_count, LANES), jnp.int32),
            pltpu.SemaphoreType.DMA,
            pltpu.SemaphoreType.DMA((slot_most,)),
            pltpu.SemaphoreType.DMA((lat_count // 4,)),
        ],
        out_shape=[
            jax.ShapeDtypeStruct((slot_most, per_slot, degrees), jnp.bfloat16),
            jax.ShapeDtypeStruct(message_shape, jnp.bfloat16),
        ],
        compiler_params=pltpu.CompilerParams(vmem_limit_bytes=GRANT),
        name="spectral",
    )(arrived, legendre[0], damping)
    received = lax.all_to_all(message_two, "lat", split_axis=0, concat_axis=0, tiled=True)

    spectral = jnp.transpose(
        spectral_rows.reshape(slot_most, fields, 2, levels, degrees), (0, 1, 3, 2, 4)
    )
    slot_waves = jnp.sum(placed * wave_number[:, None], axis=0)
    present = (jnp.sum(placed, axis=0) > 0).astype(jnp.float32)
    points = jnp.arange(NLON, dtype=jnp.int32).reshape(BLOCKS_X, 1, 1, BLK)
    phases = slot_waves[None, :, None, None] * points % NLON
    angles = phases.astype(jnp.float32) * (2.0 * math.pi / NLON)
    norm_factor = present[None, :, None, None] / math.sqrt(wave_total)
    zonal = jnp.concatenate([jnp.cos(angles) * norm_factor, -jnp.sin(angles) * norm_factor], axis=2)
    zonal = zonal.astype(jnp.bfloat16).reshape(BLOCKS_X, slot_count * 2, BLK)
    all_columns = arrived[:, tiles * lat_dev, entries:].reshape(lat_count, capacity, lat_count)
    column_of = lax.dynamic_index_in_dim(all_columns, device_row, 2, keepdims=False)
    column_of = column_of.astype(jnp.int32).reshape(-1)
    lev_count = lax.axis_size("lev")
    at_top = (lax.axis_index("lev") == lev_count - 1).astype(jnp.int32).reshape(1)
    vertical = vweight.T
    corners = stencil.T
    received, vertical, corners, at_top = lax.optimization_barrier((received, vertical, corners, at_top))
    blocks, lowest = pl.pallas_call(
        block_kernel,
        out_shape=[
            jax.ShapeDtypeStruct((entries, half, BLK), jnp.bfloat16),
            jax.ShapeDtypeStruct((fields * entries, BLK), jnp.bfloat16),
        ],
        in_specs=[smem, vmem, vmem],
        out_specs=[vmem, vmem],
        scratch_shapes=[pltpu.VMEM((fields * entries, BLK), jnp.float32)],
        compiler_params=pltpu.CompilerParams(vmem_limit_bytes=16 * 2**20),
        name="blocks",
    )(column_of, received, zonal)

    above = lax.ppermute(lowest, "lev", [(i, i - 1) for i in range(1, lev_count)])
    arrival = pl.pallas_call(
        arrive_kernel,
        out_shape=jax.ShapeDtypeStruct((arrivals, fields, levels, BLK), jnp.bfloat16),
        in_specs=[smem, smem, vmem, vmem, vmem, vmem],
        out_specs=hbm,
        scratch_shapes=[
            pltpu.VMEM((arrivals, fields, levels, BLK), jnp.bfloat16),
            pltpu.VMEM((entries, half + 8, BLK), jnp.float32),
            pltpu.VMEM((fields * entries, BLK), jnp.float32),
            pltpu.SemaphoreType.DMA((arrivals // 32,)),
        ],
        compiler_params=pltpu.CompilerParams(vmem_limit_bytes=16 * 2**20),
        name="arrive",
    )(corners, at_top, blocks, above, hweight, vertical)
    return (spectral[None], arrival)


def solution(mesh):
    return jax.shard_map(
        per_device,
        mesh=mesh,
        in_specs=(
            P("lat", None, "lev", None),
            P("lat"),
            P("lat", None, None, None),
            P(),
            P("lat", None, None),
            P("lat", None),
            P("lat", None, None),
            P("lat", "lev"),
        ),
        out_specs=(P("lat", None, None, "lev", None, None), P("lat", None, "lev", None)),
        check_vma=False,
    )
```

time: 119 us -> 118 us (level)
  local copies, waits for them, and re-layouts: 10.9 us -> 4.67 us
  Pallas kernels: 20.8 us -> 25.7 us
    unnamed x22 -> x12, local copies, waits for them, and re-layouts: 6.51 us -> 1.01 us
    pallas_call x3, Pallas kernels: 18.2 us -> 23.2 us  [the longest x1 11.6 us: per_device(): pl.pallas_call(spectral_kernel, in_specs=[vmem, hbm, vmem], out_specs=[vm...]
  transfers between devices with their start and end apart: 3 -> 3, of which waited for: 3 -> 3; matrix products, arithmetic and copies ran while one was open for 9% -> 10% of each run, Pallas kernels for 0% -> 0%
where the time goes in v4:
time: 118 us
  waiting for transfers between devices  52.9 us (45%)
  starting transfers between devices  25.9 us (22%)
  Pallas kernels  25.7 us (22%)
  other arithmetic  7.73 us (7%)
  local copies, waits for them, and re-layouts  4.67 us (4%)
    all_to_all x1, waiting for transfers between devices, per_device(): lax.all_to_all(message_two, 'lat', split_axis=0, concat_axis=0, tiled=True)  27.5 us
    all_to_all x1, waiting for transfers between devices, per_device(): lax.all_to_all(message_one, 'lat', split_axis=0, concat_axis=0, tiled=True)  23.6 us
    all_to_all x1, starting transfers between devices, per_device(): lax.all_to_all(message_one, 'lat', split_axis=0, concat_axis=0, tiled=True)  11.9 us
    pallas_call x1, Pallas kernels, per_device(): pl.pallas_call(spectral_kernel, in_specs=[vmem, hbm, vmem], out_specs=[vm...  11.6 us
    all_to_all x1, starting transfers between devices, per_device(): lax.all_to_all(message_two, 'lat', split_axis=0, concat_axis=0, tiled=True)  8.58 us
    pallas_call x1, Pallas kernels, per_device(): pl.pallas_call(arrive_kernel, out_shape=jax.ShapeDtypeStruct((arrivals, f...  7.45 us
    another operation x1, other arithmetic  5.84 us
    ppermute x1, starting transfers between devices, per_device(): lax.ppermute(lowest, 'lev', [(i, i - 1) for i in range(1, lev_count)])  5.46 us
  transfers between devices with their start and end apart: 3, of which 3 were waited for; matrix products, arithmetic and copies ran while one was open for 10% of the time, Pallas kernels for 0%

profile of v4, /device:TPU:1, one launch (start us, length us, event | category | flops | bytes accessed | tf_op | source)
XLA Modules:
  0.0 117.7 jit_solution(12732115794078105953)
XLA Ops:
  0.6 4.1 %pack.1 = bf16[32,128,128]{2,1,0:T(8,128)(2,1)} custom-call(s32[1,64]{1,0:T(1,128)} %bitcast.31, s32[2,32]{1,0:T(2,128)} %bitcast.29, f32[1,40]{1,0:T(1,128)} %bitcast.30, bf16[40,3,16,128]{3,2,1,0:T(8,128)(2,1)} %fourier_in.1), custom_call_target="tpu_custom_call" | custom-call | tf_op jit(solution)/shard_map/pack/pallas_call | solution.py:326
  4.7 0.0 copy-start.5
  4.7 11.9 %all-to-all-start = ((bf16[32,128,128]{2,1,0:T(8,128)(2,1)}), bf16[32,128,128]{2,1,0:T(8,128)(2,1)S(1)}, u32[]{:S(2)}, u32[]{:S(2)}) async-start(bf16[32,128,128]{2,1,0:T(8,128)(2,1)} %pack.1), calls=%async_computation | async-start | bytes 2097152 | tf_op jit(solution)/shard_map/all_to_all | solution.py:345
  16.6 0.0 copy-done.5
  16.7 0.1 convert_reduce_fusion.1
  16.8 0.2 dynamic-slice_reduce_fusion
  16.9 0.7 fusion.9.damping
  17.6 23.6 %all-to-all-done.arrived = bf16[32,128,128]{2,1,0:T(8,128)(2,1)S(1)} async-done(((bf16[32,128,128]{2,1,0:T(8,128)(2,1)}), bf16[32,128,128]{2,1,0:T(8,128)(2,1)S(1)}, u32[]{:S(2)}, u32[]{:S(2)}) %all-to-all-start) | async-done | bytes 1048608 | tf_op jit(solution)/shard_map/all_to_all | solution.py:345
  41.2 0.0 copy-start.3
  41.2 1.0 copy-done.3
  42.2 11.6 %spectral.1 = (bf16[4,96,640]{2,1,0:T(8,128)(2,1)}, bf16[32,64,384]{2,1,0:T(8,128)(2,1)}) custom-call(bf16[32,128,128]{2,1,0:T(8,128)(2,1)} %copy-done.3, bf16[4,1280,640]{2,1,0:T(8,128)(2,1)} %bitcast.26, f32[4,640]{1,0:T(4,128)} %fusion.9.damping), custom_call_target="tpu_custom_call" | custom-call | tf_op jit(solution)/shard_map/spectral/pallas_call | solution.py:356
  53.9 8.6 %all-to-all-start.1 = ((bf16[32,64,384]{2,1,0:T(8,128)(2,1)}), bf16[32,64,384]{2,1,0:T(8,128)(2,1)S(1)}, u32[]{:S(2)}, u32[]{:S(2)}) async-start(bf16[32,64,384]{2,1,0:T(8,128)(2,1)} %get-tuple-element.11), calls=%async_computation.1 | async-start | bytes 3145728 | tf_op jit(solution)/shard_map/all_to_all | solution.py:378
  62.5 0.1 select_reduce_fusion
  62.6 5.8 %multiply_convert_fusion.1 = (bf16[20,128,1,128]{3,1,2,0:T(8,128)(2,1)S(1)}, bf16[20,128,1,128]{3,1,2,0:T(8,128)(2,1)S(1)}) fusion(f32[128]{0:T(128)S(1)} %compare_select_fusion, s32[20,128]{1,0:T(8,128)S(1)} %multiply_add_fusion, s32[128]{0:T(128)S(1)} %get-tuple-element.20), kind=kLoop, calls=%fused_computation.5 | loop fusion | flops 4587520 | bytes 1321984 | tf_op jit(solution)/shard_map/convert.2
  68.4 0.1 pad_maximum_fusion
  68.6 1.4 %copy.19 = bf16[20,128,2,128]{3,2,1,0:T(2,128)(2,1)S(1)} copy(bf16[20,128,2,128]{3,1,2,0:T(8,128)(2,1)S(1)} %pad_maximum_fusion) | data formatting | bytes 2621440 | tf_op jit(solution)/shard_map/concatenate | solution.py:389
  69.9 1.0 slice_reduce_fusion
  70.9 0.1 reshape_squeeze.3
  71.0 0.7 convert_reduce_fusion
  71.7 0.1 reshape.148.column_of
  71.8 27.5 %all-to-all-done.1.received = bf16[32,64,384]{2,1,0:T(8,128)(2,1)S(1)} async-done(((bf16[32,64,384]{2,1,0:T(8,128)(2,1)}), bf16[32,64,384]{2,1,0:T(8,128)(2,1)S(1)}, u32[]{:S(2)}, u32[]{:S(2)}) %all-to-all-start.1) | async-done | bytes 1572896 | tf_op jit(solution)/shard_map/all_to_all | solution.py:378
  99.3 0.0 copy-start.4
  99.3 0.0 copy-start
  99.3 0.0 copy-start.1
  99.3 0.0 copy-start.2
  99.3 2.5 %blocks.1 = (bf16[64,48,128]{2,1,0:T(8,128)(2,1)S(1)}, bf16[192,128]{1,0:T(8,128)(2,1)S(1)}) custom-call(s32[64]{0:T(128)S(1)} %reshape.148.column_of, bf16[32,64,384]{2,1,0:T(8,128)(2,1)S(1)} %all-to-all-done.1.received, bf16[20,256,128]{2,1,0:T(8,128)(2,1)S(1)} %bitcast.23), custom_call_target="tpu_custom_call" | custom-call | tf_op jit(solution)/shard_map/blocks/pallas_call | solution.py:399
  101.9 5.5 %collective-permute-start = (bf16[192,128]{1,0:T(8,128)(2,1)S(1)}, bf16[192,128]{1,0:T(8,128)(2,1)S(1)}, u32[]{:S(2)}, u32[]{:S(2)}) collective-permute-start(bf16[192,128]{1,0:T(8,128)(2,1)S(1)} %get-tuple-element.16), channel_id=1, source_target_pairs={{1,0},{2,1},{3,2},{4,3},{5,4},{6,5},{7,6},{9,8},{10,9},{11,10},{12... | collective-permute-start | bytes 147464 | tf_op jit(solution)/shard_map/ppermute | solution.py:412
  107.3 0.0 copy-done.4
  107.3 1.2 copy.23
  108.5 1.8 %collective-permute-done.above = bf16[192,128]{1,0:T(8,128)(2,1)S(1)} collective-permute-done((bf16[192,128]{1,0:T(8,128)(2,1)S(1)}, bf16[192,128]{1,0:T(8,128)(2,1)S(1)}, u32[]{:S(2)}, u32[]{:S(2)}) %collective-permute-start) | collective-permute-done | bytes 49184 | tf_op jit(solution)/shard_map/ppermute | solution.py:412
  110.3 0.0 copy-done
  110.3 0.0 copy-done.1
  110.3 0.0 copy-done.2
  110.3 7.5 %arrive.1 = bf16[256,3,16,128]{3,2,1,0:T(8,128)(2,1)} custom-call(s32[4,256]{1,0:T(4,128)S(1)} %bitcast.25, s32[1]{0:T(128)} %bitcast.13.at_top, bf16[64,48,128]{2,1,0:T(8,128)(2,1)S(1)} %get-tuple-element.15.blocks, bf16[192,128]{1,0:T(8,128)(2,1)S(1)} %collective-permute-done.above, f32[256,4,128]{2,1,0:T(4,128)S(1)} %copy-done, f32[16,256]{1,0:T(8,128)S(1)} %bitcast.24), custom_call_target="tpu_custom_call" | custom-call | tf_op jit(solution)/shard_map/arrive/pallas_call | solution.py:413
  (7 shorter events, 0.1 us)
Async XLA Ops:
  4.7 11.9 %copy-start.5 = (s32[64,1]{0,1:T(1,128)S(1)}, s32[64,1]{0,1:T(1,128)}, u32[]{:S(2)}) copy-start(s32[64,1]{0,1:T(1,128)} %param.11) | copy-start | bytes 772
  4.7 36.5 %all-to-all-start = ((bf16[32,128,128]{2,1,0:T(8,128)(2,1)}), bf16[32,128,128]{2,1,0:T(8,128)(2,1)S(1)}, u32[]{:S(2)}, u32[]{:S(2)}) async-start(bf16[32,128,128]{2,1,0:T(8,128)(2,1)} %pack.1), calls=%async_computation | async-start | bytes 2097152 | tf_op jit(solution)/shard_map/all_to_all | solution.py:345
  41.2 1.0 copy-start.3
  53.9 45.4 %all-to-all-start.1 = ((bf16[32,64,384]{2,1,0:T(8,128)(2,1)}), bf16[32,64,384]{2,1,0:T(8,128)(2,1)S(1)}, u32[]{:S(2)}, u32[]{:S(2)}) async-start(bf16[32,64,384]{2,1,0:T(8,128)(2,1)} %get-tuple-element.11), calls=%async_computation.1 | async-start | bytes 3145728 | tf_op jit(solution)/shard_map/all_to_all | solution.py:378
  99.3 8.0 %copy-start.4 = (bf16[4,96,640]{2,1,0:T(8,128)(2,1)S(1)}, bf16[4,96,640]{2,1,0:T(8,128)(2,1)}, u32[]{:S(2)}) copy-start(bf16[4,96,640]{2,1,0:T(8,128)(2,1)} %get-tuple-element.10) | copy-start | bytes 1474564
  99.3 11.0 %copy-start = (f32[256,4,128]{2,1,0:T(4,128)S(1)}, f32[256,4,128]{2,1,0:T(4,128)}, u32[]{:S(2)}) copy-start(f32[256,4,128]{2,1,0:T(4,128)} %hweight.1) | copy-start | bytes 1572868
  99.3 11.0 %copy-start.1 = (f32[256,16]{0,1:T(8,128)S(1)}, f32[256,16]{0,1:T(8,128)}, u32[]{:S(2)}) copy-start(f32[256,16]{0,1:T(8,128)} %param.15) | copy-start | bytes 49156
  99.3 11.0 %copy-start.2 = (s32[256,4]{0,1:T(4,128)S(1)}, s32[256,4]{0,1:T(4,128)}, u32[]{:S(2)}) copy-start(s32[256,4]{0,1:T(4,128)} %param.13) | copy-start | bytes 12292
  101.9 8.4 %collective-permute-start = (bf16[192,128]{1,0:T(8,128)(2,1)S(1)}, bf16[192,128]{1,0:T(8,128)(2,1)S(1)}, u32[]{:S(2)}, u32[]{:S(2)}) collective-permute-start(bf16[192,128]{1,0:T(8,128)(2,1)S(1)} %get-tuple-element.16), channel_id=1, source_target_pairs={{1,0},{2,1},{3,2},{4,3},{5,4},{6,5},{7,6},{9,8},{10,9},{11,10},{12... | collective-permute-start | bytes 147464 | tf_op jit(solution)/shard_map/ppermute | solution.py:412

commit v5 on v4

--- a/solution.py
+++ b/solution.py
@@ -119,13 +119,18 @@
         copy.wait()
 
 
+def fetch_kernel(tables_in, tables, sem):
+    copies = [pltpu.make_async_copy(tables_in.at[i], tables.at[i], sem.at[i]) for i in range(tables.shape[0])]
+    for copy in copies:
+        copy.start()
+    for copy in copies:
+        copy.wait()
+
+
 def spectral_kernel(
-    arrived, tables_in, damping, spectral, message, tables, made, turned, rows_at, listed, row_of, listed_sem, in_sem, out_sem
+    arrived, tables, damping, spectral, message, made, turned, rows_at, listed, row_of, listed_sem, out_sem
 ):
     slots, per_slot, degrees = spectral.shape
-    fetches = [pltpu.make_async_copy(tables_in.at[i], tables.at[i], in_sem.at[i]) for i in range(slots)]
-    for fetch in fetches:
-        fetch.start()
     half = per_slot // 2
     field_rows = half // 3
     bands = arrived.shape[0]
@@ -148,7 +153,6 @@
     chunk = 256
     for slot in range(slots):
         own = turned[slot * per_slot : (slot + 1) * per_slot, :]
-        fetches[slot].wait()
         spectra = mxu(own, tables[slot], NN)
         damped = (spectra * damping[slot : slot + 1, :]).astype(jnp.bfloat16)
         spectral[slot] = damped
@@ -208,7 +212,7 @@
         send(g).wait()
 
 
-def block_kernel(column_of, received, zonal, blocks, lowest, lowest_scratch):
+def block_kernel(column_of, received, zonal, blocks, lowest, highest, lowest_scratch, highest_scratch):
     owners, message_rows, message_lanes = received.shape
     unit = identity(LANES)
     half = message_lanes // 8
@@ -232,63 +236,82 @@
                     lowest_scratch[field * entries + entry : field * entries + entry + 1, :] = made[
                         field * 16 : field * 16 + 1, :
                     ]
+                    highest_scratch[field * entries + entry : field * entries + entry + 1, :] = made[
+                        field * 16 + 15 : field * 16 + 16, :
+                    ]
     lowest[...] = lowest_scratch[...].astype(jnp.bfloat16)
-
-
-def arrive_kernel(stencil, at_top, blocks, above, hweight, vweight, arrival, made, wide, over_rows, out_sem):
+    highest[...] = highest_scratch[...].astype(jnp.bfloat16)
+
+
+def horizontal_kernel(stencil, blocks, hweight, horizontal, wide):
     entries = blocks.shape[0]
-    rows, fields, levels, _ = made.shape
-    top = at_top[0] == 1
-    over_rows[...] = above[...].astype(jnp.float32)
-
-    def widen(entry, carry):
-        block = blocks[entry].astype(jnp.float32)
-        wide[entry, 0 : fields * levels, :] = block
-        for field in range(fields):
-            own_last = block[(field + 1) * levels - 1 : (field + 1) * levels, :]
-            over = over_rows[pl.ds(field * entries + entry, 1), :]
-            wide[entry, pl.ds(fields * levels + field, 1), :] = jnp.where(top, own_last, over)
+    rows = horizontal.shape[0]
+    together = 8
+
+    def widen(i, carry):
+        for k in range(together):
+            wide[i * together + k] = blocks[i * together + k].astype(jnp.float32)
         return carry
 
-    lax.fori_loop(0, entries, widen, 0, unroll=4)
-
-    level = lax.broadcasted_iota(jnp.int32, (levels, LANES), 0)
-    together = 8
-    piece = 32
-    pieces = rows // piece
-
-    def send(i):
-        at = pl.multiple_of(i * piece, piece)
-        return pltpu.make_async_copy(made.at[pl.ds(at, piece)], arrival.at[pl.ds(at, piece)], out_sem.at[i])
+    lax.fori_loop(0, entries // together, widen, 0)
 
     def some_rows(i, carry):
-        first = i * together
-        tile = pl.multiple_of((first // LANES) * LANES, LANES)
-        uppers = pltpu.roll(vweight[:, pl.ds(tile, LANES)], (LANES - first % LANES) % LANES, 1)
         for k in range(together):
-            a = first + k
+            a = i * together + k
             total = None
             for q in range(4):
                 term = hweight[a, q : q + 1, :] * wide[stencil[q, a]]
                 total = term if total is None else total + term
+            horizontal[a] = total
+        return carry
+
+    lax.fori_loop(0, rows // together, some_rows, 0)
+
+
+def vertical_kernel(stencil, at_top, horizontal, highest, above, hweight, vweight, arrival, made, over_rows, wide, out_sem):
+    rows, fields, levels, _ = made.shape
+    entries = wide.shape[0]
+    top = at_top[0] == 1
+    over_rows[...] = jnp.where(top, highest[...].astype(jnp.float32), above[...].astype(jnp.float32))
+    together = 8
+
+    def widen(i, carry):
+        for k in range(together):
+            entry = i * together + k
+            for field in range(fields):
+                wide[entry, field : field + 1, :] = over_rows[pl.ds(field * entries + entry, 1), :]
+        return carry
+
+    lax.fori_loop(0, entries // together, widen, 0)
+
+    level = lax.broadcasted_iota(jnp.int32, (levels, LANES), 0)
+    piece = 32
+    pieces = rows // piece
+
+    def send(i):
+        at = pl.multiple_of(i * piece, piece)
+        return pltpu.make_async_copy(made.at[pl.ds(at, piece)], arrival.at[pl.ds(at, piece)], out_sem.at[i])
+
+    def some_rows(i, carry):
+        first = i * piece
+        tile = pl.multiple_of((first // LANES) * LANES, LANES)
+        uppers = pltpu.roll(vweight[:, pl.ds(tile, LANES)], (LANES - first % LANES) % LANES, 1)
+        for k in range(piece):
+            a = first + k
+            last = None
+            for q in range(4):
+                term = hweight[a, q : q + 1, :] * wide[stencil[q, a]]
+                last = term if last is None else last + term
             upper = jnp.broadcast_to(uppers[:, k : k + 1], (levels, LANES))
             lower = 1.0 - upper
             for field in range(fields):
-                here = total[field * levels : (field + 1) * levels]
-                over = jnp.where(
-                    level == levels - 1,
-                    total[fields * levels + field : fields * levels + field + 1],
-                    pltpu.roll(here, levels - 1, 0),
-                )
+                here = horizontal[a, field * levels : (field + 1) * levels, :]
+                over = jnp.where(level == levels - 1, last[field : field + 1], pltpu.roll(here, levels - 1, 0))
                 made[a, field] = (lower * here + upper * over).astype(jnp.bfloat16)
-
-        @pl.when(i % (piece // together) == piece // together - 1)
-        def _():
-            send(i // (piece // together)).start()
-
+        send(i).start()
         return carry
 
-    lax.fori_loop(0, rows // together, some_rows, 0)
+    lax.fori_loop(0, pieces, some_rows, 0)
     for i in range(pieces):
         send(i).wait()
 
@@ -353,28 +376,36 @@
     damping = keep_mask * damping_curve(degrees)[None, :]
 
     message_shape = (lat_count, entries // 8 * slot_most * 2, 8 * half)
+    tables = pl.pallas_call(
+        fetch_kernel,
+        out_shape=jax.ShapeDtypeStruct(legendre.shape[1:], legendre.dtype),
+        in_specs=[hbm],
+        out_specs=vmem,
+        scratch_shapes=[pltpu.SemaphoreType.DMA((slot_most,))],
+        compiler_params=pltpu.CompilerParams(vmem_limit_bytes=16 * 2**20),
+        cost_estimate=pl.CostEstimate(flops=0, bytes_accessed=2 * legendre.size * 2, transcendentals=0),
+        name="fetch",
+    )(legendre[0])
     spectral_rows, message_two = pl.pallas_call(
         spectral_kernel,
-        in_specs=[vmem, hbm, vmem],
+        in_specs=[vmem, vmem, vmem],
         out_specs=[vmem, hbm],
         scratch_shapes=[
-            pltpu.VMEM((slot_most, latitudes, degrees), jnp.bfloat16),
             pltpu.VMEM(message_shape, jnp.bfloat16),
             pltpu.VMEM((message_lanes, latitudes), jnp.bfloat16),
             pltpu.VMEM((latitudes * 2 * slot_most, LANES), jnp.float32),
             pltpu.VMEM((lat_count, LANES), jnp.int32),
             pltpu.SMEM((lat_count, LANES), jnp.int32),
             pltpu.SemaphoreType.DMA,
-            pltpu.SemaphoreType.DMA((slot_most,)),
             pltpu.SemaphoreType.DMA((lat_count // 4,)),
         ],
         out_shape=[
             jax.ShapeDtypeStruct((slot_most, per_slot, degrees), jnp.bfloat16),
             jax.ShapeDtypeStruct(message_shape, jnp.bfloat16),
         ],
-        compiler_params=pltpu.CompilerParams(vmem_limit_bytes=GRANT),
+        compiler_params=pltpu.CompilerParams(vmem_limit_bytes=24 * 2**20),
         name="spectral",
-    )(arrived, legendre[0], damping)
+    )(arrived, tables, damping)
     received = lax.all_to_all(message_two, "lat", split_axis=0, concat_axis=0, tiled=True)
 
     spectral = jnp.transpose(
@@ -396,34 +427,47 @@
     vertical = vweight.T
     corners = stencil.T
     received, vertical, corners, at_top = lax.optimization_barrier((received, vertical, corners, at_top))
-    blocks, lowest = pl.pallas_call(
+    blocks, lowest, highest = pl.pallas_call(
         block_kernel,
         out_shape=[
             jax.ShapeDtypeStruct((entries, half, BLK), jnp.bfloat16),
             jax.ShapeDtypeStruct((fields * entries, BLK), jnp.bfloat16),
+            jax.ShapeDtypeStruct((fields * entries, BLK), jnp.bfloat16),
         ],
         in_specs=[smem, vmem, vmem],
-        out_specs=[vmem, vmem],
-        scratch_shapes=[pltpu.VMEM((fields * entries, BLK), jnp.float32)],
+        out_specs=[vmem, vmem, vmem],
+        scratch_shapes=[pltpu.VMEM((fields * entries, BLK), jnp.float32)] * 2,
         compiler_params=pltpu.CompilerParams(vmem_limit_bytes=16 * 2**20),
         name="blocks",
     )(column_of, received, zonal)
 
     above = lax.ppermute(lowest, "lev", [(i, i - 1) for i in range(1, lev_count)])
+    horizontal = pl.pallas_call(
+        horizontal_kernel,
+        out_shape=jax.ShapeDtypeStruct((arrivals, half, BLK), jnp.float32),
+        in_specs=[smem, vmem, vmem],
+        out_specs=vmem,
+        scratch_shapes=[pltpu.VMEM((entries, half, BLK), jnp.float32)],
+        compiler_params=pltpu.CompilerParams(vmem_limit_bytes=16 * 2**20),
+        cost_estimate=pl.CostEstimate(
+            flops=8 * arrivals * half * BLK, bytes_accessed=4 * arrivals * half * BLK, transcendentals=0
+        ),
+        name="horizontal",
+    )(corners, blocks, hweight)
     arrival = pl.pallas_call(
-        arrive_kernel,
+        vertical_kernel,
         out_shape=jax.ShapeDtypeStruct((arrivals, fields, levels, BLK), jnp.bfloat16),
-        in_specs=[smem, smem, vmem, vmem, vmem, vmem],
+        in_specs=[smem, smem, vmem, vmem, vmem, vmem, vmem],
         out_specs=hbm,
         scratch_shapes=[
             pltpu.VMEM((arrivals, fields, levels, BLK), jnp.bfloat16),
-            pltpu.VMEM((entries, half + 8, BLK), jnp.float32),
             pltpu.VMEM((fields * entries, BLK), jnp.float32),
+            pltpu.VMEM((entries, 8, BLK), jnp.float32),
             pltpu.SemaphoreType.DMA((arrivals // 32,)),
         ],
         compiler_params=pltpu.CompilerParams(vmem_limit_bytes=16 * 2**20),
-        name="arrive",
-    )(corners, at_top, blocks, above, hweight, vertical)
+        name="vertical",
+    )(corners, at_top, horizontal, highest, above, hweight, vertical)
     return (spectral[None], arrival)
 
 

time: 118 us -> 115 us (0.975)
  waiting for transfers between devices: 52.9 us -> 45.3 us
  local copies, waits for them, and re-layouts: 4.67 us -> 12.1 us
  Pallas kernels: 25.7 us -> 22.8 us
    unnamed x12 -> x16, local copies, waits for them, and re-layouts: 1.01 us -> 8.46 us
    all_to_all x1, waiting for transfers between devices: 23.6 us -> 17.8 us  [per_device(): lax.all_to_all(message_one, 'lat', split_axis=0, concat_axis=0, tiled=True)]
    pallas_call x2 -> x4, Pallas kernels: 19.1 us -> 16.2 us  [the longest x1 8.27 us: per_device(): pl.pallas_call(spectral_kernel, in_specs=[vmem, vmem, vmem], out_specs=[v...]
    ppermute x1, waiting for transfers between devices: 1.79 us -> 0.01 us  [per_device(): lax.ppermute(lowest, 'lev', [(i, i - 1) for i in range(1, lev_count)])]
  transfers between devices with their start and end apart: 3 -> 3, of which waited for: 3 -> 2; matrix products, arithmetic and copies ran while one was open for 10% -> 9% of each run, Pallas kernels for 0% -> 3%
where the time goes in v5:
time: 115 us; the launch traced here: 114 us
  waiting for transfers between devices  45.3 us (39%)
  starting transfers between devices  25.9 us (23%)
  Pallas kernels  22.8 us (20%)
  local copies, waits for them, and re-layouts  12.1 us (11%)
  other arithmetic  7.14 us (6%)
    all_to_all x1, waiting for transfers between devices, per_device(): lax.all_to_all(message_two, 'lat', split_axis=0, concat_axis=0, tiled=True)  27.5 us
    all_to_all x1, waiting for transfers between devices, per_device(): lax.all_to_all(message_one, 'lat', split_axis=0, concat_axis=0, tiled=True)  17.8 us
    all_to_all x1, starting transfers between devices, per_device(): lax.all_to_all(message_one, 'lat', split_axis=0, concat_axis=0, tiled=True)  11.9 us
    all_to_all x1, starting transfers between devices, per_device(): lax.all_to_all(message_two, 'lat', split_axis=0, concat_axis=0, tiled=True)  8.59 us
    unnamed x16, local copies, waits for them, and re-layouts  8.46 us
    pallas_call x1, Pallas kernels, per_device(): pl.pallas_call(spectral_kernel, in_specs=[vmem, vmem, vmem], out_specs=[v...  8.27 us
    another operation x1, other arithmetic  5.84 us
    ppermute x1, starting transfers between devices, per_device(): lax.ppermute(lowest, 'lev', [(i, i - 1) for i in range(1, lev_count)])  5.47 us
  transfers between devices with their start and end apart: 3, of which 2 were waited for; matrix products, arithmetic and copies ran while one was open for 9% of the time, Pallas kernels for 3%

profile of v5, /device:TPU:1, one launch (start us, length us, event | category | flops | bytes accessed | tf_op | source)
XLA Modules:
  0.0 114.1 jit_solution(1185190685369166296)
XLA Ops:
  0.6 4.1 %pack.1 = bf16[32,128,128]{2,1,0:T(8,128)(2,1)} custom-call(s32[1,64]{1,0:T(1,128)} %bitcast.32, s32[2,32]{1,0:T(2,128)} %bitcast.30, f32[1,40]{1,0:T(1,128)} %bitcast.31, bf16[40,3,16,128]{3,2,1,0:T(8,128)(2,1)} %fourier_in.1), custom_call_target="tpu_custom_call" | custom-call | tf_op jit(solution)/shard_map/pack/pallas_call | solution.py:349
  4.7 11.9 %all-to-all-start = ((bf16[32,128,128]{2,1,0:T(8,128)(2,1)}), bf16[32,128,128]{2,1,0:T(8,128)(2,1)S(1)}, u32[]{:S(2)}, u32[]{:S(2)}) async-start(bf16[32,128,128]{2,1,0:T(8,128)(2,1)} %pack.1), calls=%async_computation | async-start | bytes 2097152 | tf_op jit(solution)/shard_map/all_to_all | solution.py:368
  16.6 0.0 copy-start.2
  16.6 2.9 %copy-done.2 = bf16[1,4,1280,640]{3,2,1,0:T(8,128)(2,1)S(1)} copy-done((bf16[1,4,1280,640]{3,2,1,0:T(8,128)(2,1)S(1)}, bf16[1,4,1280,640]{3,2,1,0:T(8,128)(2,1)}, u32[]{:S(2)}) %copy-start.2) | copy-done | bytes 6553624
  19.5 0.0 copy-start.7
  19.5 0.8 fetch.1.tables
  20.3 0.0 copy-start
  20.3 2.7 %copy-done = bf16[4,1280,640]{2,1,0:T(8,128)(2,1)} copy-done((bf16[4,1280,640]{2,1,0:T(8,128)(2,1)}, bf16[4,1280,640]{2,1,0:T(8,128)(2,1)S(1)}, u32[]{:S(2)}) %copy-start) | copy-done | bytes 6553624
  23.0 0.0 copy-done.7
  23.0 0.1 convert_reduce_fusion.1
  23.2 0.2 dynamic-slice_reduce_fusion
  23.3 0.1 fusion.9.damping
  23.4 17.8 %all-to-all-done.arrived = bf16[32,128,128]{2,1,0:T(8,128)(2,1)S(1)} async-done(((bf16[32,128,128]{2,1,0:T(8,128)(2,1)}), bf16[32,128,128]{2,1,0:T(8,128)(2,1)S(1)}, u32[]{:S(2)}, u32[]{:S(2)}) %all-to-all-start) | async-done | bytes 1048608 | tf_op jit(solution)/shard_map/all_to_all | solution.py:368
  41.2 0.0 copy-start.1
  41.2 2.9 %copy-done.1 = bf16[4,1280,640]{2,1,0:T(8,128)(2,1)S(1)} copy-done((bf16[4,1280,640]{2,1,0:T(8,128)(2,1)S(1)}, bf16[4,1280,640]{2,1,0:T(8,128)(2,1)}, u32[]{:S(2)}) %copy-start.1) | copy-done | bytes 6553624
  44.1 0.0 copy-start.3
  44.1 8.3 %spectral.1 = (bf16[4,96,640]{2,1,0:T(8,128)(2,1)S(1)}, bf16[32,64,384]{2,1,0:T(8,128)(2,1)}) custom-call(bf16[32,128,128]{2,1,0:T(8,128)(2,1)S(1)} %all-to-all-done.arrived, bf16[4,1280,640]{2,1,0:T(8,128)(2,1)S(1)} %copy-done.1, f32[4,640]{1,0:T(4,128)S(1)} %fusion.9.damping), custom_call_target="tpu_custom_call" | custom-call | tf_op jit(solution)/shard_map/spectral/pallas_call | solution.py:389
  52.4 0.0 copy-done.3
  52.4 8.6 %all-to-all-start.1 = ((bf16[32,64,384]{2,1,0:T(8,128)(2,1)}), bf16[32,64,384]{2,1,0:T(8,128)(2,1)S(1)}, u32[]{:S(2)}, u32[]{:S(2)}) async-start(bf16[32,64,384]{2,1,0:T(8,128)(2,1)} %get-tuple-element.12), calls=%async_computation.1 | async-start | bytes 3145728 | tf_op jit(solution)/shard_map/all_to_all | solution.py:409
  61.0 0.1 select_reduce_fusion
  61.1 5.8 %multiply_convert_fusion.1 = (bf16[20,128,1,128]{3,1,2,0:T(8,128)(2,1)S(1)}, bf16[20,128,1,128]{3,1,2,0:T(8,128)(2,1)S(1)}) fusion(f32[128]{0:T(128)S(1)} %compare_select_fusion, s32[20,128]{1,0:T(8,128)S(1)} %multiply_add_fusion, s32[128]{0:T(128)S(1)} %get-tuple-element.22), kind=kLoop, calls=%fused_computation.5 | loop fusion | flops 4587520 | bytes 1321984 | tf_op jit(solution)/shard_map/convert.2
  67.0 0.1 pad_maximum_fusion
  67.1 1.4 %copy.19 = bf16[20,128,2,128]{3,2,1,0:T(2,128)(2,1)S(1)} copy(bf16[20,128,2,128]{3,1,2,0:T(8,128)(2,1)S(1)} %pad_maximum_fusion) | data formatting | bytes 2621440 | tf_op jit(solution)/shard_map/concatenate | solution.py:420
  68.5 1.0 slice_reduce_fusion
  69.4 0.1 reshape_squeeze.3
  69.5 0.7 convert_reduce_fusion
  70.2 0.1 reshape.148.column_of
  70.3 27.5 %all-to-all-done.1.received = bf16[32,64,384]{2,1,0:T(8,128)(2,1)S(1)} async-done(((bf16[32,64,384]{2,1,0:T(8,128)(2,1)}), bf16[32,64,384]{2,1,0:T(8,128)(2,1)S(1)}, u32[]{:S(2)}, u32[]{:S(2)}) %all-to-all-start.1) | async-done | bytes 1572896 | tf_op jit(solution)/shard_map/all_to_all | solution.py:409
  97.8 0.0 copy-start.4
  97.8 0.0 copy-start.5
  97.8 2.5 %blocks.1 = (bf16[64,48,128]{2,1,0:T(8,128)(2,1)S(1)}, bf16[192,128]{1,0:T(8,128)(2,1)S(1)}, bf16[192,128]{1,0:T(8,128)(2,1)S(1)}) custom-call(s32[64]{0:T(128)S(1)} %reshape.148.column_of, bf16[32,64,384]{2,1,0:T(8,128)(2,1)S(1)} %all-to-all-done.1.received, bf16[20,256,128]{2,1,0:T(8,128)(2,1)S(1)} %bitcast.24), custom_call_target="tpu_custom_call" | custom-call | tf_op jit(solution)/shard_map/blocks/pallas_call | solution.py:430
  100.3 5.5 %collective-permute-start = (bf16[192,128]{1,0:T(8,128)(2,1)S(1)}, bf16[192,128]{1,0:T(8,128)(2,1)S(1)}, u32[]{:S(2)}, u32[]{:S(2)}) collective-permute-start(bf16[192,128]{1,0:T(8,128)(2,1)S(1)} %get-tuple-element.18), channel_id=1, source_target_pairs={{1,0},{2,1},{3,2},{4,3},{5,4},{6,5},{7,6},{9,8},{10,9},{11,10},{12... | collective-permute-start | bytes 147464 | tf_op jit(solution)/shard_map/ppermute | solution.py:444
  105.8 1.2 %copy.23 = bf16[4,3,2,16,640]{4,2,3,1,0:T(2,128)(2,1)} copy(bf16[4,3,2,16,640]{4,3,2,1,0:T(8,128)(2,1)S(1)} %bitcast.25) | data formatting | bytes 983040 | tf_op jit(solution)/shard_map/reshape | solution.py:412
  107.0 0.0 copy-done.4
  107.0 0.0 copy-done.5
  107.0 0.0 copy-start.6
  107.0 2.7 %horizontal.1 = f32[256,48,128]{2,1,0:T(8,128)S(1)} custom-call(s32[4,256]{1,0:T(4,128)S(1)} %bitcast.26, bf16[64,48,128]{2,1,0:T(8,128)(2,1)S(1)} %get-tuple-element.16.blocks, f32[256,4,128]{2,1,0:T(4,128)S(1)} %copy-done.4), custom_call_target="tpu_custom_call" | custom-call | flops 12582912 | bytes 6291456 | tf_op jit(solution)/shard_map/horizontal/pallas_call | solution.py:445
  109.7 0.0 collective-permute-done.above
  109.7 0.0 copy-done.6
  109.7 4.4 %vertical.1 = bf16[256,3,16,128]{3,2,1,0:T(8,128)(2,1)} custom-call(s32[4,256]{1,0:T(4,128)S(1)} %bitcast.27, s32[1]{0:T(128)} %bitcast.13.at_top, f32[256,48,128]{2,1,0:T(8,128)S(1)} %horizontal.1, bf16[192,128]{1,0:T(8,128)(2,1)S(1)} %get-tuple-element.17.highest, bf16[192,128]{1,0:T(8,128)(2,1)S(1)} %collective-permute-done.above, ...), custom_call_target="tpu_custom_call" | custom-call | tf_op jit(solution)/shard_map/vertical/pallas_call | solution.py:457
  (7 shorter events, 0.1 us)
Async XLA Ops:
  4.7 36.5 %all-to-all-start = ((bf16[32,128,128]{2,1,0:T(8,128)(2,1)}), bf16[32,128,128]{2,1,0:T(8,128)(2,1)S(1)}, u32[]{:S(2)}, u32[]{:S(2)}) async-start(bf16[32,128,128]{2,1,0:T(8,128)(2,1)} %pack.1), calls=%async_computation | async-start | bytes 2097152 | tf_op jit(solution)/shard_map/all_to_all | solution.py:368
  16.6 2.9 %copy-start.2 = (bf16[1,4,1280,640]{3,2,1,0:T(8,128)(2,1)S(1)}, bf16[1,4,1280,640]{3,2,1,0:T(8,128)(2,1)}, u32[]{:S(2)}) copy-start(bf16[1,4,1280,640]{3,2,1,0:T(8,128)(2,1)} %param.10) | copy-start | bytes 19660804
  19.5 3.6 %copy-start.7 = (s32[64,1]{0,1:T(1,128)S(1)}, s32[64,1]{0,1:T(1,128)}, u32[]{:S(2)}) copy-start(s32[64,1]{0,1:T(1,128)} %param.11) | copy-start | bytes 772
  20.3 2.7 %copy-start = (bf16[4,1280,640]{2,1,0:T(8,128)(2,1)}, bf16[4,1280,640]{2,1,0:T(8,128)(2,1)S(1)}, u32[]{:S(2)}) copy-start(bf16[4,1280,640]{2,1,0:T(8,128)(2,1)S(1)} %fetch.1.tables) | copy-start | bytes 19660804
  41.2 2.9 %copy-start.1 = (bf16[4,1280,640]{2,1,0:T(8,128)(2,1)S(1)}, bf16[4,1280,640]{2,1,0:T(8,128)(2,1)}, u32[]{:S(2)}) copy-start(bf16[4,1280,640]{2,1,0:T(8,128)(2,1)} %copy-done) | copy-start | bytes 19660804
  44.1 8.3 %copy-start.3 = (bf16[32,128,128]{2,1,0:T(8,128)(2,1)}, bf16[32,128,128]{2,1,0:T(8,128)(2,1)S(1)}, u32[]{:S(2)}) copy-start(bf16[32,128,128]{2,1,0:T(8,128)(2,1)S(1)} %all-to-all-done.arrived) | copy-start | bytes 3145732
  52.4 45.4 %all-to-all-start.1 = ((bf16[32,64,384]{2,1,0:T(8,128)(2,1)}), bf16[32,64,384]{2,1,0:T(8,128)(2,1)S(1)}, u32[]{:S(2)}, u32[]{:S(2)}) async-start(bf16[32,64,384]{2,1,0:T(8,128)(2,1)} %get-tuple-element.12), calls=%async_computation.1 | async-start | bytes 3145728 | tf_op jit(solution)/shard_map/all_to_all | solution.py:409
  97.8 9.2 %copy-start.4 = (f32[256,4,128]{2,1,0:T(4,128)S(1)}, f32[256,4,128]{2,1,0:T(4,128)}, u32[]{:S(2)}) copy-start(f32[256,4,128]{2,1,0:T(4,128)} %hweight.3) | copy-start | bytes 1572868
  97.8 9.2 %copy-start.5 = (s32[256,4]{0,1:T(4,128)S(1)}, s32[256,4]{0,1:T(4,128)}, u32[]{:S(2)}) copy-start(s32[256,4]{0,1:T(4,128)} %param.13) | copy-start | bytes 12292
  100.3 9.3 %collective-permute-start = (bf16[192,128]{1,0:T(8,128)(2,1)S(1)}, bf16[192,128]{1,0:T(8,128)(2,1)S(1)}, u32[]{:S(2)}, u32[]{:S(2)}) collective-permute-start(bf16[192,128]{1,0:T(8,128)(2,1)S(1)} %get-tuple-element.18), channel_id=1, source_target_pairs={{1,0},{2,1},{3,2},{4,3},{5,4},{6,5},{7,6},{9,8},{10,9},{11,10},{12... | collective-permute-start | bytes 147464 | tf_op jit(solution)/shard_map/ppermute | solution.py:444
  107.0 2.7 %copy-start.6 = (f32[256,16]{0,1:T(8,128)S(1)}, f32[256,16]{0,1:T(8,128)}, u32[]{:S(2)}) copy-start(f32[256,16]{0,1:T(8,128)} %param.15) | copy-start | bytes 49156

commit v6 on v5

--- a/solution.py
+++ b/solution.py
@@ -119,24 +119,25 @@
         copy.wait()
 
 
-def fetch_kernel(tables_in, tables, sem):
-    copies = [pltpu.make_async_copy(tables_in.at[i], tables.at[i], sem.at[i]) for i in range(tables.shape[0])]
-    for copy in copies:
-        copy.start()
-    for copy in copies:
-        copy.wait()
-
-
 def spectral_kernel(
-    arrived, tables, damping, spectral, message, made, turned, rows_at, listed, row_of, listed_sem, out_sem
+    arrived, tables_in, damping, spectral, message, tables, made, turned, rows_at, listed, row_of, listed_sem, in_sem, out_sem
 ):
     slots, per_slot, degrees = spectral.shape
+    latitudes = tables.shape[1]
+
+    def fetch(slot):
+        return pltpu.make_async_copy(tables_in.at[slot], tables.at[slot], in_sem.at[slot])
+
+    def fetch_one(slot, carry):
+        fetch(slot).start()
+        return carry
+
+    lax.fori_loop(0, slots, fetch_one, 0)
     half = per_slot // 2
     field_rows = half // 3
     bands = arrived.shape[0]
     tiles = turned.shape[0] // LANES
     lat_dev = (arrived.shape[1] - 8) // tiles
-    latitudes = bands * lat_dev
     receivers, message_rows, message_lanes = message.shape
     lists = pltpu.make_async_copy(listed, row_of, listed_sem)
 
@@ -151,10 +152,12 @@
 
     gap = jnp.zeros((LANES - half, degrees), jnp.bfloat16)
     chunk = 256
-    for slot in range(slots):
-        own = turned[slot * per_slot : (slot + 1) * per_slot, :]
+
+    def one_slot(slot, carry):
+        fetch(slot).wait()
+        own = turned[pl.ds(pl.multiple_of(slot * per_slot, 32), per_slot), :]
         spectra = mxu(own, tables[slot], NN)
-        damped = (spectra * damping[slot : slot + 1, :]).astype(jnp.bfloat16)
+        damped = (spectra * damping[pl.ds(slot, 1), :]).astype(jnp.bfloat16)
         spectral[slot] = damped
         sides = []
         for part in range(2):
@@ -169,6 +172,9 @@
                 rows_at[pl.ds(at * 2 * slots + slot * 2 + part, chunk, stride=2 * slots), :] = back[
                     :, part * LANES : (part + 1) * LANES
                 ]
+        return carry
+
+    lax.fori_loop(0, slots, one_slot, 0)
 
     lists.wait()
     lane = lax.broadcasted_iota(jnp.int32, (8, LANES), 1)
@@ -212,12 +218,16 @@
         send(g).wait()
 
 
-def block_kernel(column_of, received, zonal, blocks, lowest, highest, lowest_scratch, highest_scratch):
+def block_kernel(
+    column_of, received, zonal, vweight, blocks, lowest, highest, spread, lowest_scratch, highest_scratch
+):
     owners, message_rows, message_lanes = received.shape
     unit = identity(LANES)
     half = message_lanes // 8
     groups = message_rows // 8
     entries = blocks.shape[0]
+    rows, levels, _ = spread.shape
+    per_entry = rows // entries
     for pair in range(groups // 2):
         wide = received[:, pair * 16 : (pair + 1) * 16, :].astype(jnp.float32)
         for side in range(2):
@@ -232,6 +242,8 @@
                 entry = group * 8 + e
                 made = mxu(turned[e * half : (e + 1) * half], zonal[column_of[entry]], NN)
                 blocks[entry] = made.astype(jnp.bfloat16)
+                for a in range(entry * per_entry, (entry + 1) * per_entry):
+                    spread[a] = jnp.broadcast_to(vweight[:, a : a + 1], (levels, LANES))
                 for field in range(3):
                     lowest_scratch[field * entries + entry : field * entries + entry + 1, :] = made[
                         field * 16 : field * 16 + 1, :
@@ -268,7 +280,7 @@
     lax.fori_loop(0, rows // together, some_rows, 0)
 
 
-def vertical_kernel(stencil, at_top, horizontal, highest, above, hweight, vweight, arrival, made, over_rows, wide, out_sem):
+def vertical_kernel(stencil, at_top, horizontal, highest, above, hweight, spread, arrival, made, over_rows, wide, out_sem):
     rows, fields, levels, _ = made.shape
     entries = wide.shape[0]
     top = at_top[0] == 1
@@ -279,13 +291,13 @@
         for k in range(together):
             entry = i * together + k
             for field in range(fields):
-                wide[entry, field : field + 1, :] = over_rows[pl.ds(field * entries + entry, 1), :]
+                wide[entry, 7 - field : 8 - field, :] = over_rows[pl.ds(field * entries + entry, 1), :]
         return carry
 
     lax.fori_loop(0, entries // together, widen, 0)
 
-    level = lax.broadcasted_iota(jnp.int32, (levels, LANES), 0)
-    piece = 32
+    row = lax.broadcasted_iota(jnp.int32, (8, LANES), 0)
+    piece = 64
     pieces = rows // piece
 
     def send(i):
@@ -293,21 +305,22 @@
         return pltpu.make_async_copy(made.at[pl.ds(at, piece)], arrival.at[pl.ds(at, piece)], out_sem.at[i])
 
     def some_rows(i, carry):
-        first = i * piece
-        tile = pl.multiple_of((first // LANES) * LANES, LANES)
-        uppers = pltpu.roll(vweight[:, pl.ds(tile, LANES)], (LANES - first % LANES) % LANES, 1)
         for k in range(piece):
-            a = first + k
+            a = i * piece + k
             last = None
             for q in range(4):
                 term = hweight[a, q : q + 1, :] * wide[stencil[q, a]]
                 last = term if last is None else last + term
-            upper = jnp.broadcast_to(uppers[:, k : k + 1], (levels, LANES))
-            lower = 1.0 - upper
             for field in range(fields):
-                here = horizontal[a, field * levels : (field + 1) * levels, :]
-                over = jnp.where(level == levels - 1, last[field : field + 1], pltpu.roll(here, levels - 1, 0))
-                made[a, field] = (lower * here + upper * over).astype(jnp.bfloat16)
+                parts = []
+                over = last if field == 0 else pltpu.roll(last, field, 0)
+                for part in reversed(range(levels // 8)):
+                    here = horizontal[a, field * levels + part * 8 : field * levels + (part + 1) * 8, :]
+                    turned = pltpu.roll(here, 7, 0)
+                    up = jnp.where(row == 7, over, turned)
+                    parts.insert(0, here + spread[a, part * 8 : (part + 1) * 8, :] * (up - here))
+                    over = turned
+                made[a, field] = jnp.concatenate(parts, axis=0).astype(jnp.bfloat16)
         send(i).start()
         return carry
 
@@ -376,42 +389,35 @@
     damping = keep_mask * damping_curve(degrees)[None, :]
 
     message_shape = (lat_count, entries // 8 * slot_most * 2, 8 * half)
-    tables = pl.pallas_call(
-        fetch_kernel,
-        out_shape=jax.ShapeDtypeStruct(legendre.shape[1:], legendre.dtype),
-        in_specs=[hbm],
-        out_specs=vmem,
-        scratch_shapes=[pltpu.SemaphoreType.DMA((slot_most,))],
-        compiler_params=pltpu.CompilerParams(vmem_limit_bytes=16 * 2**20),
-        cost_estimate=pl.CostEstimate(flops=0, bytes_accessed=2 * legendre.size * 2, transcendentals=0),
-        name="fetch",
-    )(legendre[0])
     spectral_rows, message_two = pl.pallas_call(
         spectral_kernel,
-        in_specs=[vmem, vmem, vmem],
+        in_specs=[vmem, hbm, vmem],
         out_specs=[vmem, hbm],
         scratch_shapes=[
+            pltpu.VMEM((slot_most, latitudes, degrees), jnp.bfloat16),
             pltpu.VMEM(message_shape, jnp.bfloat16),
             pltpu.VMEM((message_lanes, latitudes), jnp.bfloat16),
             pltpu.VMEM((latitudes * 2 * slot_most, LANES), jnp.float32),
             pltpu.VMEM((lat_count, LANES), jnp.int32),
             pltpu.SMEM((lat_count, LANES), jnp.int32),
             pltpu.SemaphoreType.DMA,
+            pltpu.SemaphoreType.DMA((slot_most,)),
             pltpu.SemaphoreType.DMA((lat_count // 4,)),
         ],
         out_shape=[
             jax.ShapeDtypeStruct((slot_most, per_slot, degrees), jnp.bfloat16),
             jax.ShapeDtypeStruct(message_shape, jnp.bfloat16),
         ],
-        compiler_params=pltpu.CompilerParams(vmem_limit_bytes=24 * 2**20),
+        compiler_params=pltpu.CompilerParams(vmem_limit_bytes=50 * 2**20),
         name="spectral",
-    )(arrived, tables, damping)
+    )(arrived, legendre[0], damping)
     received = lax.all_to_all(message_two, "lat", split_axis=0, concat_axis=0, tiled=True)
 
     spectral = jnp.transpose(
         spectral_rows.reshape(slot_most, fields, 2, levels, degrees), (0, 1, 3, 2, 4)
     )
     slot_waves = jnp.sum(placed * wave_number[:, None], axis=0)
+    slot_waves, spectral = lax.optimization_barrier((slot_waves, spectral))
     present = (jnp.sum(placed, axis=0) > 0).astype(jnp.float32)
     points = jnp.arange(NLON, dtype=jnp.int32).reshape(BLOCKS_X, 1, 1, BLK)
     phases = slot_waves[None, :, None, None] * points % NLON
@@ -427,19 +433,20 @@
     vertical = vweight.T
     corners = stencil.T
     received, vertical, corners, at_top = lax.optimization_barrier((received, vertical, corners, at_top))
-    blocks, lowest, highest = pl.pallas_call(
+    blocks, lowest, highest, spread = pl.pallas_call(
         block_kernel,
         out_shape=[
             jax.ShapeDtypeStruct((entries, half, BLK), jnp.bfloat16),
             jax.ShapeDtypeStruct((fields * entries, BLK), jnp.bfloat16),
             jax.ShapeDtypeStruct((fields * entries, BLK), jnp.bfloat16),
+            jax.ShapeDtypeStruct((arrivals, levels, BLK), jnp.float32),
         ],
-        in_specs=[smem, vmem, vmem],
-        out_specs=[vmem, vmem, vmem],
+        in_specs=[smem, vmem, vmem, vmem],
+        out_specs=[vmem, vmem, vmem, vmem],
         scratch_shapes=[pltpu.VMEM((fields * entries, BLK), jnp.float32)] * 2,
         compiler_params=pltpu.CompilerParams(vmem_limit_bytes=16 * 2**20),
         name="blocks",
-    )(column_of, received, zonal)
+    )(column_of, received, zonal, vertical)
 
     above = lax.ppermute(lowest, "lev", [(i, i - 1) for i in range(1, lev_count)])
     horizontal = pl.pallas_call(
@@ -463,11 +470,11 @@
             pltpu.VMEM((arrivals, fields, levels, BLK), jnp.bfloat16),
             pltpu.VMEM((fields * entries, BLK), jnp.float32),
             pltpu.VMEM((entries, 8, BLK), jnp.float32),
-            pltpu.SemaphoreType.DMA((arrivals // 32,)),
+            pltpu.SemaphoreType.DMA((arrivals // 64,)),
         ],
         compiler_params=pltpu.CompilerParams(vmem_limit_bytes=16 * 2**20),
         name="vertical",
-    )(corners, at_top, horizontal, highest, above, hweight, vertical)
+    )(corners, at_top, horizontal, highest, above, hweight, spread)
     return (spectral[None], arrival)
 
 

time: 115 us -> 113 us (0.983)
  local copies, waits for them, and re-layouts: 12.1 us -> 3.99 us
  waiting for transfers between devices: 45.3 us -> 51.6 us
    unnamed x16 -> x10, local copies, waits for them, and re-layouts: 8.46 us -> 1.16 us
    all_to_all x1, waiting for transfers between devices: 17.8 us -> 24.2 us  [per_device(): lax.all_to_all(message_one, 'lat', split_axis=0, concat_axis=0, tiled=True)]
    pallas_call x2 -> x1, Pallas kernels: 9.08 us -> 10.9 us  [per_device(): pl.pallas_call(spectral_kernel, in_specs=[vmem, hbm, vmem], out_specs=[vm...]
  transfers between devices with their start and end apart: 3 -> 3, of which waited for: 2 -> 3; matrix products, arithmetic and copies ran while one was open for 9% -> 9% of each run, Pallas kernels for 3% -> 2%
where the time goes in v6:
time: 113 us
  waiting for transfers between devices  51.6 us (46%)
  starting transfers between devices  26 us (23%)
  Pallas kernels  23.7 us (21%)
  other arithmetic  7.12 us (6%)
  local copies, waits for them, and re-layouts  3.99 us (4%)
    all_to_all x1, waiting for transfers between devices, per_device(): lax.all_to_all(message_two, 'lat', split_axis=0, concat_axis=0, tiled=True)  27.1 us
    all_to_all x1, waiting for transfers between devices, per_device(): lax.all_to_all(message_one, 'lat', split_axis=0, concat_axis=0, tiled=True)  24.2 us
    all_to_all x1, starting transfers between devices, per_device(): lax.all_to_all(message_one, 'lat', split_axis=0, concat_axis=0, tiled=True)  11.9 us
    pallas_call x1, Pallas kernels, per_device(): pl.pallas_call(spectral_kernel, in_specs=[vmem, hbm, vmem], out_specs=[vm...  10.9 us
    all_to_all x1, starting transfers between devices, per_device(): lax.all_to_all(message_two, 'lat', split_axis=0, concat_axis=0, tiled=True)  8.58 us
    another operation x1, other arithmetic  5.81 us
    ppermute x1, starting transfers between devices, per_device(): lax.ppermute(lowest, 'lev', [(i, i - 1) for i in range(1, lev_count)])  5.49 us
    pallas_call x1, Pallas kernels, per_device(): pl.pallas_call(pack_kernel, out_shape=jax.ShapeDtypeStruct((lat_count, ti...  4.08 us
  transfers between devices with their start and end apart: 3, of which 3 were waited for; matrix products, arithmetic and copies ran while one was open for 9% of the time, Pallas kernels for 2%

profile of v6, /device:TPU:1, one launch (start us, length us, event | category | flops | bytes accessed | tf_op | source)
XLA Modules:
  0.0 113.2 jit_solution(14959447580999192064)
XLA Ops:
  0.6 4.1 %pack.1 = bf16[32,128,128]{2,1,0:T(8,128)(2,1)} custom-call(s32[1,64]{1,0:T(1,128)} %bitcast.31, s32[2,32]{1,0:T(2,128)} %bitcast.29, f32[1,40]{1,0:T(1,128)} %bitcast.30, bf16[40,3,16,128]{3,2,1,0:T(8,128)(2,1)} %fourier_in.1), custom_call_target="tpu_custom_call" | custom-call | tf_op jit(solution)/shard_map/pack/pallas_call | solution.py:362
  4.7 0.0 copy-start.4
  4.7 11.9 %all-to-all-start = ((bf16[32,128,128]{2,1,0:T(8,128)(2,1)}), bf16[32,128,128]{2,1,0:T(8,128)(2,1)S(1)}, u32[]{:S(2)}, u32[]{:S(2)}) async-start(bf16[32,128,128]{2,1,0:T(8,128)(2,1)} %pack.1), calls=%async_computation | async-start | bytes 2097152 | tf_op jit(solution)/shard_map/all_to_all | solution.py:381
  16.6 0.0 copy-done.4
  16.7 0.1 convert_reduce_fusion.1
  16.8 0.2 dynamic-slice_reduce_fusion
  16.9 0.1 fusion.9.damping
  17.0 24.2 %all-to-all-done.arrived = bf16[32,128,128]{2,1,0:T(8,128)(2,1)S(1)} async-done(((bf16[32,128,128]{2,1,0:T(8,128)(2,1)}), bf16[32,128,128]{2,1,0:T(8,128)(2,1)S(1)}, u32[]{:S(2)}, u32[]{:S(2)}) %all-to-all-start) | async-done | bytes 1048608 | tf_op jit(solution)/shard_map/all_to_all | solution.py:381
  41.2 10.9 %spectral.1 = (bf16[4,96,640]{2,1,0:T(8,128)(2,1)S(1)}, bf16[32,64,384]{2,1,0:T(8,128)(2,1)S(1)}) custom-call(bf16[32,128,128]{2,1,0:T(8,128)(2,1)S(1)} %all-to-all-done.arrived, bf16[4,1280,640]{2,1,0:T(8,128)(2,1)} %bitcast.27, f32[4,640]{1,0:T(4,128)S(1)} %fusion.9.damping), custom_call_target="tpu_custom_call" | custom-call | tf_op jit(solution)/shard_map/spectral/pallas_call | solution.py:392
  52.2 0.0 copy-start.1
  52.2 1.1 %copy-done.1 = bf16[32,64,384]{2,1,0:T(8,128)(2,1)} copy-done((bf16[32,64,384]{2,1,0:T(8,128)(2,1)}, bf16[32,64,384]{2,1,0:T(8,128)(2,1)S(1)}, u32[]{:S(2)}) %copy-start.1) | copy-done | bytes 1572888
  53.3 8.6 %all-to-all-start.1 = ((bf16[32,64,384]{2,1,0:T(8,128)(2,1)}), bf16[32,64,384]{2,1,0:T(8,128)(2,1)S(1)}, u32[]{:S(2)}, u32[]{:S(2)}) async-start(bf16[32,64,384]{2,1,0:T(8,128)(2,1)} %copy-done.1), calls=%async_computation.1 | async-start | bytes 3145728 | tf_op jit(solution)/shard_map/all_to_all | solution.py:414
  62.0 0.1 fusion.7
  62.1 0.1 slice_reduce_fusion
  62.2 0.1 reshape_squeeze.3
  62.3 0.7 convert_reduce_fusion
  63.0 0.1 reshape.145.column_of
  63.1 1.2 %copy.23 = bf16[4,3,2,16,640]{4,2,3,1,0:T(2,128)(2,1)} copy(bf16[4,3,2,16,640]{4,3,2,1,0:T(8,128)(2,1)S(1)} %bitcast.23) | data formatting | bytes 983040 | tf_op jit(solution)/shard_map/reshape | solution.py:417
  64.3 5.8 %multiply_convert_fusion.1 = (bf16[20,128,1,128]{3,1,2,0:T(8,128)(2,1)S(1)}, bf16[20,128,1,128]{3,1,2,0:T(8,128)(2,1)S(1)}) fusion(f32[128]{0:T(128)S(1)} %compare_select_fusion, s32[20,128]{1,0:T(8,128)S(1)} %multiply_add_fusion, s32[128]{0:T(128)S(1)} %get-tuple-element.20), kind=kLoop, calls=%fused_computation.5 | loop fusion | flops 4587520 | bytes 1321984 | tf_op jit(solution)/shard_map/convert.2
  70.1 0.1 pad_maximum_fusion
  70.2 0.0 copy-start.3
  70.2 1.4 %copy.19 = bf16[20,128,2,128]{3,2,1,0:T(2,128)(2,1)S(1)} copy(bf16[20,128,2,128]{3,1,2,0:T(8,128)(2,1)S(1)} %pad_maximum_fusion) | data formatting | bytes 2621440 | tf_op jit(solution)/shard_map/concatenate | solution.py:426
  71.6 27.1 %all-to-all-done.1.received = bf16[32,64,384]{2,1,0:T(8,128)(2,1)S(1)} async-done(((bf16[32,64,384]{2,1,0:T(8,128)(2,1)}), bf16[32,64,384]{2,1,0:T(8,128)(2,1)S(1)}, u32[]{:S(2)}, u32[]{:S(2)}) %all-to-all-start.1) | async-done | bytes 1572896 | tf_op jit(solution)/shard_map/all_to_all | solution.py:414
  98.7 0.0 copy-done.3
  98.7 0.0 copy-start
  98.7 0.0 copy-start.2
  98.7 2.5 %blocks.1 = (bf16[64,48,128]{2,1,0:T(8,128)(2,1)S(1)}, bf16[192,128]{1,0:T(8,128)(2,1)S(1)}, bf16[192,128]{1,0:T(8,128)(2,1)S(1)}, f32[256,16,128]{2,1,0:T(8,128)S(1)}) custom-call(s32[64]{0:T(128)S(1)} %reshape.145.column_of, bf16[32,64,384]{2,1,0:T(8,128)(2,1)S(1)} %all-to-all-done.1.received, bf16[20,256,128]{2,1,0:T(8,128)(2,1)S(1)} %bitcast.22, ...), custom_call_target="tpu_custom_call" | custom-call | tf_op jit(solution)/shard_map/blocks/pallas_call | solution.py:436
  101.3 5.5 %collective-permute-start = (bf16[192,128]{1,0:T(8,128)(2,1)S(1)}, bf16[192,128]{1,0:T(8,128)(2,1)S(1)}, u32[]{:S(2)}, u32[]{:S(2)}) collective-permute-start(bf16[192,128]{1,0:T(8,128)(2,1)S(1)} %get-tuple-element.24), channel_id=1, source_target_pairs={{1,0},{2,1},{3,2},{4,3},{5,4},{6,5},{7,6},{9,8},{10,9},{11,10},{12... | collective-permute-start | bytes 147464 | tf_op jit(solution)/shard_map/ppermute | solution.py:451
  106.8 0.0 copy-done
  106.8 0.0 copy-done.2
  106.8 2.7 %horizontal.1 = f32[256,48,128]{2,1,0:T(8,128)S(1)} custom-call(s32[4,256]{1,0:T(4,128)S(1)} %bitcast.24, bf16[64,48,128]{2,1,0:T(8,128)(2,1)S(1)} %get-tuple-element.22.blocks, f32[256,4,128]{2,1,0:T(4,128)S(1)} %copy-done), custom_call_target="tpu_custom_call" | custom-call | flops 12582912 | bytes 6291456 | tf_op jit(solution)/shard_map/horizontal/pallas_call | solution.py:452
  109.5 0.3 collective-permute-done.above
  109.7 3.4 %vertical.1 = bf16[256,3,16,128]{3,2,1,0:T(8,128)(2,1)} custom-call(s32[4,256]{1,0:T(4,128)S(1)} %bitcast.25, s32[1]{0:T(128)} %bitcast.13.at_top, f32[256,48,128]{2,1,0:T(8,128)S(1)} %horizontal.1, bf16[192,128]{1,0:T(8,128)(2,1)S(1)} %get-tuple-element.23.highest, bf16[192,128]{1,0:T(8,128)(2,1)S(1)} %collective-permute-done.above, ...), custom_call_target="tpu_custom_call" | custom-call | tf_op jit(solution)/shard_map/vertical/pallas_call | solution.py:464
  (7 shorter events, 0.1 us)
Async XLA Ops:
  4.7 11.9 %copy-start.4 = (s32[64,1]{0,1:T(1,128)S(1)}, s32[64,1]{0,1:T(1,128)}, u32[]{:S(2)}) copy-start(s32[64,1]{0,1:T(1,128)} %param.11) | copy-start | bytes 772
  4.7 36.5 %all-to-all-start = ((bf16[32,128,128]{2,1,0:T(8,128)(2,1)}), bf16[32,128,128]{2,1,0:T(8,128)(2,1)S(1)}, u32[]{:S(2)}, u32[]{:S(2)}) async-start(bf16[32,128,128]{2,1,0:T(8,128)(2,1)} %pack.1), calls=%async_computation | async-start | bytes 2097152 | tf_op jit(solution)/shard_map/all_to_all | solution.py:381
  52.2 1.1 %copy-start.1 = (bf16[32,64,384]{2,1,0:T(8,128)(2,1)}, bf16[32,64,384]{2,1,0:T(8,128)(2,1)S(1)}, u32[]{:S(2)}) copy-start(bf16[32,64,384]{2,1,0:T(8,128)(2,1)S(1)} %get-tuple-element.16) | copy-start | bytes 4718596
  53.3 45.4 %all-to-all-start.1 = ((bf16[32,64,384]{2,1,0:T(8,128)(2,1)}), bf16[32,64,384]{2,1,0:T(8,128)(2,1)S(1)}, u32[]{:S(2)}, u32[]{:S(2)}) async-start(bf16[32,64,384]{2,1,0:T(8,128)(2,1)} %copy-done.1), calls=%async_computation.1 | async-start | bytes 3145728 | tf_op jit(solution)/shard_map/all_to_all | solution.py:414
  70.2 28.5 %copy-start.3 = (f32[256,16]{0,1:T(8,128)S(1)}, f32[256,16]{0,1:T(8,128)}, u32[]{:S(2)}) copy-start(f32[256,16]{0,1:T(8,128)} %param.15) | copy-start | bytes 49156
  98.7 8.1 %copy-start = (f32[256,4,128]{2,1,0:T(4,128)S(1)}, f32[256,4,128]{2,1,0:T(4,128)}, u32[]{:S(2)}) copy-start(f32[256,4,128]{2,1,0:T(4,128)} %hweight.3) | copy-start | bytes 1572868
  98.7 8.1 %copy-start.2 = (s32[256,4]{0,1:T(4,128)S(1)}, s32[256,4]{0,1:T(4,128)}, u32[]{:S(2)}) copy-start(s32[256,4]{0,1:T(4,128)} %param.13) | copy-start | bytes 12292
  101.3 8.4 %collective-permute-start = (bf16[192,128]{1,0:T(8,128)(2,1)S(1)}, bf16[192,128]{1,0:T(8,128)(2,1)S(1)}, u32[]{:S(2)}, u32[]{:S(2)}) collective-permute-start(bf16[192,128]{1,0:T(8,128)(2,1)S(1)} %get-tuple-element.24), channel_id=1, source_target_pairs={{1,0},{2,1},{3,2},{4,3},{5,4},{6,5},{7,6},{9,8},{10,9},{11,10},{12... | collective-permute-start | bytes 147464 | tf_op jit(solution)/shard_map/ppermute | solution.py:451

commit v7 on v6

--- a/solution.py
+++ b/solution.py
@@ -408,7 +408,7 @@
             jax.ShapeDtypeStruct((slot_most, per_slot, degrees), jnp.bfloat16),
             jax.ShapeDtypeStruct(message_shape, jnp.bfloat16),
         ],
-        compiler_params=pltpu.CompilerParams(vmem_limit_bytes=50 * 2**20),
+        compiler_params=pltpu.CompilerParams(vmem_limit_bytes=52 * 2**20),
         name="spectral",
     )(arrived, legendre[0], damping)
     received = lax.all_to_all(message_two, "lat", split_axis=0, concat_axis=0, tiled=True)

time: 113 us -> 111 us (0.982)
  Pallas kernels: 23.7 us -> 21.9 us
  local copies, waits for them, and re-layouts: 3.99 us -> 2.86 us
    pallas_call x1, Pallas kernels: 10.9 us -> 9.16 us  [per_device(): pl.pallas_call(spectral_kernel, in_specs=[vmem, hbm, vmem], out_specs=[vm...]
    unnamed x10 -> x8, local copies, waits for them, and re-layouts: 1.16 us -> 0.02 us
where the time goes in v7:
time: 111 us; the launch traced here: 110 us
  waiting for transfers between devices  51.6 us (46%)
  starting transfers between devices  26 us (23%)
  Pallas kernels  21.9 us (20%)
  other arithmetic  7.12 us (6%)
  local copies, waits for them, and re-layouts  2.86 us (3%)
    all_to_all x1, waiting for transfers between devices, per_device(): lax.all_to_all(message_two, 'lat', split_axis=0, concat_axis=0, tiled=True)  27.1 us
    all_to_all x1, waiting for transfers between devices, per_device(): lax.all_to_all(message_one, 'lat', split_axis=0, concat_axis=0, tiled=True)  24.2 us
    all_to_all x1, starting transfers between devices, per_device(): lax.all_to_all(message_one, 'lat', split_axis=0, concat_axis=0, tiled=True)  11.9 us
    pallas_call x1, Pallas kernels, per_device(): pl.pallas_call(spectral_kernel, in_specs=[vmem, hbm, vmem], out_specs=[vm...  9.16 us
    all_to_all x1, starting transfers between devices, per_device(): lax.all_to_all(message_two, 'lat', split_axis=0, concat_axis=0, tiled=True)  8.59 us
    another operation x1, other arithmetic  5.81 us
    ppermute x1, starting transfers between devices, per_device(): lax.ppermute(lowest, 'lev', [(i, i - 1) for i in range(1, lev_count)])  5.49 us
    pallas_call x1, Pallas kernels, per_device(): pl.pallas_call(pack_kernel, out_shape=jax.ShapeDtypeStruct((lat_count, ti...  4.08 us
  transfers between devices with their start and end apart: 3, of which 3 were waited for; matrix products, arithmetic and copies ran while one was open for 9% of the time, Pallas kernels for 2%

profile of v7, /device:TPU:1, one launch (start us, length us, event | category | flops | bytes accessed | tf_op | source)
XLA Modules:
  0.0 110.2 jit_solution(5606981650126856339)
XLA Ops:
  0.6 4.1 %pack.1 = bf16[32,128,128]{2,1,0:T(8,128)(2,1)} custom-call(s32[1,64]{1,0:T(1,128)} %bitcast.31, s32[2,32]{1,0:T(2,128)} %bitcast.29, f32[1,40]{1,0:T(1,128)} %bitcast.30, bf16[40,3,16,128]{3,2,1,0:T(8,128)(2,1)} %fourier_in.1), custom_call_target="tpu_custom_call" | custom-call | tf_op jit(solution)/shard_map/pack/pallas_call | solution.py:362
  4.7 0.0 copy-start.3
  4.7 11.9 %all-to-all-start = ((bf16[32,128,128]{2,1,0:T(8,128)(2,1)}), bf16[32,128,128]{2,1,0:T(8,128)(2,1)S(1)}, u32[]{:S(2)}, u32[]{:S(2)}) async-start(bf16[32,128,128]{2,1,0:T(8,128)(2,1)} %pack.1), calls=%async_computation | async-start | bytes 2097152 | tf_op jit(solution)/shard_map/all_to_all | solution.py:381
  16.6 0.0 copy-done.3
  16.7 0.1 convert_reduce_fusion.1
  16.8 0.2 dynamic-slice_reduce_fusion
  16.9 0.1 fusion.9.damping
  17.0 24.2 %all-to-all-done.arrived = bf16[32,128,128]{2,1,0:T(8,128)(2,1)S(1)} async-done(((bf16[32,128,128]{2,1,0:T(8,128)(2,1)}), bf16[32,128,128]{2,1,0:T(8,128)(2,1)S(1)}, u32[]{:S(2)}, u32[]{:S(2)}) %all-to-all-start) | async-done | bytes 1048608 | tf_op jit(solution)/shard_map/all_to_all | solution.py:381
  41.2 9.2 %spectral.1 = (bf16[4,96,640]{2,1,0:T(8,128)(2,1)S(1)}, bf16[32,64,384]{2,1,0:T(8,128)(2,1)}) custom-call(bf16[32,128,128]{2,1,0:T(8,128)(2,1)S(1)} %all-to-all-done.arrived, bf16[4,1280,640]{2,1,0:T(8,128)(2,1)} %bitcast.27, f32[4,640]{1,0:T(4,128)S(1)} %fusion.9.damping), custom_call_target="tpu_custom_call" | custom-call | tf_op jit(solution)/shard_map/spectral/pallas_call | solution.py:392
  50.4 8.6 %all-to-all-start.1 = ((bf16[32,64,384]{2,1,0:T(8,128)(2,1)}), bf16[32,64,384]{2,1,0:T(8,128)(2,1)S(1)}, u32[]{:S(2)}, u32[]{:S(2)}) async-start(bf16[32,64,384]{2,1,0:T(8,128)(2,1)} %get-tuple-element.16), calls=%async_computation.1 | async-start | bytes 3145728 | tf_op jit(solution)/shard_map/all_to_all | solution.py:414
  59.0 0.1 fusion.7
  59.2 0.1 slice_reduce_fusion
  59.3 0.1 reshape_squeeze.3
  59.4 0.7 convert_reduce_fusion
  60.1 0.1 reshape.145.column_of
  60.2 1.2 %copy.23 = bf16[4,3,2,16,640]{4,2,3,1,0:T(2,128)(2,1)} copy(bf16[4,3,2,16,640]{4,3,2,1,0:T(8,128)(2,1)S(1)} %bitcast.23) | data formatting | bytes 983040 | tf_op jit(solution)/shard_map/reshape | solution.py:417
  61.3 5.8 %multiply_convert_fusion.1 = (bf16[20,128,1,128]{3,1,2,0:T(8,128)(2,1)S(1)}, bf16[20,128,1,128]{3,1,2,0:T(8,128)(2,1)S(1)}) fusion(f32[128]{0:T(128)S(1)} %compare_select_fusion, s32[20,128]{1,0:T(8,128)S(1)} %multiply_add_fusion, s32[128]{0:T(128)S(1)} %get-tuple-element.20), kind=kLoop, calls=%fused_computation.5 | loop fusion | flops 4587520 | bytes 1321984 | tf_op jit(solution)/shard_map/convert.2
  67.2 0.1 pad_maximum_fusion
  67.3 0.0 copy-start.2
  67.3 1.4 %copy.19 = bf16[20,128,2,128]{3,2,1,0:T(2,128)(2,1)S(1)} copy(bf16[20,128,2,128]{3,1,2,0:T(8,128)(2,1)S(1)} %pad_maximum_fusion) | data formatting | bytes 2621440 | tf_op jit(solution)/shard_map/concatenate | solution.py:426
  68.7 27.1 %all-to-all-done.1.received = bf16[32,64,384]{2,1,0:T(8,128)(2,1)S(1)} async-done(((bf16[32,64,384]{2,1,0:T(8,128)(2,1)}), bf16[32,64,384]{2,1,0:T(8,128)(2,1)S(1)}, u32[]{:S(2)}, u32[]{:S(2)}) %all-to-all-start.1) | async-done | bytes 1572896 | tf_op jit(solution)/shard_map/all_to_all | solution.py:414
  95.8 0.0 copy-done.2
  95.8 0.0 copy-start
  95.8 0.0 copy-start.1
  95.8 2.6 %blocks.1 = (bf16[64,48,128]{2,1,0:T(8,128)(2,1)S(1)}, bf16[192,128]{1,0:T(8,128)(2,1)S(1)}, bf16[192,128]{1,0:T(8,128)(2,1)S(1)}, f32[256,16,128]{2,1,0:T(8,128)S(1)}) custom-call(s32[64]{0:T(128)S(1)} %reshape.145.column_of, bf16[32,64,384]{2,1,0:T(8,128)(2,1)S(1)} %all-to-all-done.1.received, bf16[20,256,128]{2,1,0:T(8,128)(2,1)S(1)} %bitcast.22, ...), custom_call_target="tpu_custom_call" | custom-call | tf_op jit(solution)/shard_map/blocks/pallas_call | solution.py:436
  98.4 5.5 %collective-permute-start = (bf16[192,128]{1,0:T(8,128)(2,1)S(1)}, bf16[192,128]{1,0:T(8,128)(2,1)S(1)}, u32[]{:S(2)}, u32[]{:S(2)}) collective-permute-start(bf16[192,128]{1,0:T(8,128)(2,1)S(1)} %get-tuple-element.24), channel_id=1, source_target_pairs={{1,0},{2,1},{3,2},{4,3},{5,4},{6,5},{7,6},{9,8},{10,9},{11,10},{12... | collective-permute-start | bytes 147464 | tf_op jit(solution)/shard_map/ppermute | solution.py:451
  103.9 0.0 copy-done
  103.9 0.0 copy-done.1
  103.9 2.7 %horizontal.1 = f32[256,48,128]{2,1,0:T(8,128)S(1)} custom-call(s32[4,256]{1,0:T(4,128)S(1)} %bitcast.24, bf16[64,48,128]{2,1,0:T(8,128)(2,1)S(1)} %get-tuple-element.22.blocks, f32[256,4,128]{2,1,0:T(4,128)S(1)} %copy-done), custom_call_target="tpu_custom_call" | custom-call | flops 12582912 | bytes 6291456 | tf_op jit(solution)/shard_map/horizontal/pallas_call | solution.py:452
  106.6 0.2 collective-permute-done.above
  106.8 3.4 %vertical.1 = bf16[256,3,16,128]{3,2,1,0:T(8,128)(2,1)} custom-call(s32[4,256]{1,0:T(4,128)S(1)} %bitcast.25, s32[1]{0:T(128)} %bitcast.13.at_top, f32[256,48,128]{2,1,0:T(8,128)S(1)} %horizontal.1, bf16[192,128]{1,0:T(8,128)(2,1)S(1)} %get-tuple-element.23.highest, bf16[192,128]{1,0:T(8,128)(2,1)S(1)} %collective-permute-done.above, ...), custom_call_target="tpu_custom_call" | custom-call | tf_op jit(solution)/shard_map/vertical/pallas_call | solution.py:464
  (7 shorter events, 0.1 us)
Async XLA Ops:
  4.7 11.9 %copy-start.3 = (s32[64,1]{0,1:T(1,128)S(1)}, s32[64,1]{0,1:T(1,128)}, u32[]{:S(2)}) copy-start(s32[64,1]{0,1:T(1,128)} %param.11) | copy-start | bytes 772
  4.7 36.5 %all-to-all-start = ((bf16[32,128,128]{2,1,0:T(8,128)(2,1)}), bf16[32,128,128]{2,1,0:T(8,128)(2,1)S(1)}, u32[]{:S(2)}, u32[]{:S(2)}) async-start(bf16[32,128,128]{2,1,0:T(8,128)(2,1)} %pack.1), calls=%async_computation | async-start | bytes 2097152 | tf_op jit(solution)/shard_map/all_to_all | solution.py:381
  50.4 45.4 %all-to-all-start.1 = ((bf16[32,64,384]{2,1,0:T(8,128)(2,1)}), bf16[32,64,384]{2,1,0:T(8,128)(2,1)S(1)}, u32[]{:S(2)}, u32[]{:S(2)}) async-start(bf16[32,64,384]{2,1,0:T(8,128)(2,1)} %get-tuple-element.16), calls=%async_computation.1 | async-start | bytes 3145728 | tf_op jit(solution)/shard_map/all_to_all | solution.py:414
  67.3 28.5 %copy-start.2 = (f32[256,16]{0,1:T(8,128)S(1)}, f32[256,16]{0,1:T(8,128)}, u32[]{:S(2)}) copy-start(f32[256,16]{0,1:T(8,128)} %param.15) | copy-start | bytes 49156
  95.8 8.1 %copy-start = (f32[256,4,128]{2,1,0:T(4,128)S(1)}, f32[256,4,128]{2,1,0:T(4,128)}, u32[]{:S(2)}) copy-start(f32[256,4,128]{2,1,0:T(4,128)} %hweight.3) | copy-start | bytes 1572868
  95.8 8.1 %copy-start.1 = (s32[256,4]{0,1:T(4,128)S(1)}, s32[256,4]{0,1:T(4,128)}, u32[]{:S(2)}) copy-start(s32[256,4]{0,1:T(4,128)} %param.13) | copy-start | bytes 12292
  98.4 8.4 %collective-permute-start = (bf16[192,128]{1,0:T(8,128)(2,1)S(1)}, bf16[192,128]{1,0:T(8,128)(2,1)S(1)}, u32[]{:S(2)}, u32[]{:S(2)}) collective-permute-start(bf16[192,128]{1,0:T(8,128)(2,1)S(1)} %get-tuple-element.24), channel_id=1, source_target_pairs={{1,0},{2,1},{3,2},{4,3},{5,4},{6,5},{7,6},{9,8},{10,9},{11,10},{12... | collective-permute-start | bytes 147464 | tf_op jit(solution)/shard_map/ppermute | solution.py:451

commit v8 on v7

--- a/solution.py
+++ b/solution.py
@@ -103,20 +103,22 @@
     sides = [in_row[k : k + 1] for k in range(ids.shape[0])] + [in_column[k : k + 1] for k in range(ids.shape[0])]
     extra = jnp.broadcast_to(jnp.concatenate(sides, axis=1), (8, LANES))
     group = 8
-    copies = []
-    for o in range(owners):
-        parts = [scratch[tile, o * lat_dev : (o + 1) * lat_dev, :] for tile in range(tiles)]
-        packed[o] = jnp.concatenate(parts + [extra], axis=0).astype(jnp.bfloat16)
-        if o % group == group - 1:
-            first = o + 1 - group
-            copies.append(
-                pltpu.make_async_copy(
-                    packed.at[pl.ds(first, group)], message.at[pl.ds(first, group)], out_sem.at[o // group]
-                )
-            )
-            copies[-1].start()
-    for copy in copies:
-        copy.wait()
+
+    def send(g):
+        first = pl.multiple_of(g * group, group)
+        return pltpu.make_async_copy(packed.at[pl.ds(first, group)], message.at[pl.ds(first, group)], out_sem.at[g])
+
+    def finish(g, carry):
+        for k in range(group):
+            o = g * group + k
+            parts = [scratch[tile, pl.ds(pl.multiple_of(o * lat_dev, 8), lat_dev), :] for tile in range(tiles)]
+            packed[o] = jnp.concatenate(parts + [extra], axis=0).astype(jnp.bfloat16)
+        send(g).start()
+        return carry
+
+    lax.fori_loop(0, owners // group, finish, 0)
+    for g in range(owners // group):
+        send(g).wait()
 
 
 def spectral_kernel(
@@ -241,7 +243,8 @@
             for e in range(8):
                 entry = group * 8 + e
                 made = mxu(turned[e * half : (e + 1) * half], zonal[column_of[entry]], NN)
-                blocks[entry] = made.astype(jnp.bfloat16)
+                made = made.astype(jnp.bfloat16).astype(jnp.float32)
+                blocks[entry] = made
                 for a in range(entry * per_entry, (entry + 1) * per_entry):
                     spread[a] = jnp.broadcast_to(vweight[:, a : a + 1], (levels, LANES))
                 for field in range(3):
@@ -255,24 +258,16 @@
     highest[...] = highest_scratch[...].astype(jnp.bfloat16)
 
 
-def horizontal_kernel(stencil, blocks, hweight, horizontal, wide):
-    entries = blocks.shape[0]
+def horizontal_kernel(stencil, blocks, hweight, horizontal):
     rows = horizontal.shape[0]
-    together = 8
-
-    def widen(i, carry):
-        for k in range(together):
-            wide[i * together + k] = blocks[i * together + k].astype(jnp.float32)
-        return carry
-
-    lax.fori_loop(0, entries // together, widen, 0)
+    together = 32
 
     def some_rows(i, carry):
         for k in range(together):
             a = i * together + k
             total = None
             for q in range(4):
-                term = hweight[a, q : q + 1, :] * wide[stencil[q, a]]
+                term = hweight[a, q : q + 1, :] * blocks[stencil[q, a]]
                 total = term if total is None else total + term
             horizontal[a] = total
         return carry
@@ -297,7 +292,7 @@
     lax.fori_loop(0, entries // together, widen, 0)
 
     row = lax.broadcasted_iota(jnp.int32, (8, LANES), 0)
-    piece = 64
+    piece = 32
     pieces = rows // piece
 
     def send(i):
@@ -436,7 +431,7 @@
     blocks, lowest, highest, spread = pl.pallas_call(
         block_kernel,
         out_shape=[
-            jax.ShapeDtypeStruct((entries, half, BLK), jnp.bfloat16),
+            jax.ShapeDtypeStruct((entries, half, BLK), jnp.float32),
             jax.ShapeDtypeStruct((fields * entries, BLK), jnp.bfloat16),
             jax.ShapeDtypeStruct((fields * entries, BLK), jnp.bfloat16),
             jax.ShapeDtypeStruct((arrivals, levels, BLK), jnp.float32),
@@ -454,7 +449,6 @@
         out_shape=jax.ShapeDtypeStruct((arrivals, half, BLK), jnp.float32),
         in_specs=[smem, vmem, vmem],
         out_specs=vmem,
-        scratch_shapes=[pltpu.VMEM((entries, half, BLK), jnp.float32)],
         compiler_params=pltpu.CompilerParams(vmem_limit_bytes=16 * 2**20),
         cost_estimate=pl.CostEstimate(
             flops=8 * arrivals * half * BLK, bytes_accessed=4 * arrivals * half * BLK, transcendentals=0
@@ -470,7 +464,7 @@
             pltpu.VMEM((arrivals, fields, levels, BLK), jnp.bfloat16),
             pltpu.VMEM((fields * entries, BLK), jnp.float32),
             pltpu.VMEM((entries, 8, BLK), jnp.float32),
-            pltpu.SemaphoreType.DMA((arrivals // 64,)),
+            pltpu.SemaphoreType.DMA((arrivals // 32,)),
         ],
         compiler_params=pltpu.CompilerParams(vmem_limit_bytes=16 * 2**20),
         name="vertical",

time: 111 us -> 110 us (level)
  no operation moved by 1% of the time
where the time goes in v8:
time: 110 us
  waiting for transfers between devices  51.9 us (47%)
  starting transfers between devices  25.9 us (24%)
  Pallas kernels  21.5 us (20%)
  other arithmetic  7.12 us (6%)
  local copies, waits for them, and re-layouts  2.86 us (3%)
    all_to_all x1, waiting for transfers between devices, per_device(): lax.all_to_all(message_two, 'lat', split_axis=0, concat_axis=0, tiled=True)  27.2 us
    all_to_all x1, waiting for transfers between devices, per_device(): lax.all_to_all(message_one, 'lat', split_axis=0, concat_axis=0, tiled=True)  24.2 us
    all_to_all x1, starting transfers between devices, per_device(): lax.all_to_all(message_one, 'lat', split_axis=0, concat_axis=0, tiled=True)  11.9 us
    pallas_call x1, Pallas kernels, per_device(): pl.pallas_call(spectral_kernel, in_specs=[vmem, hbm, vmem], out_specs=[vm...  9.16 us
    all_to_all x1, starting transfers between devices, per_device(): lax.all_to_all(message_two, 'lat', split_axis=0, concat_axis=0, tiled=True)  8.59 us
    another operation x1, other arithmetic  5.81 us
    ppermute x1, starting transfers between devices, per_device(): lax.ppermute(lowest, 'lev', [(i, i - 1) for i in range(1, lev_count)])  5.47 us
    pallas_call x1, Pallas kernels, per_device(): pl.pallas_call(pack_kernel, out_shape=jax.ShapeDtypeStruct((lat_count, ti...  4.08 us
  transfers between devices with their start and end apart: 3, of which 3 were waited for; matrix products, arithmetic and copies ran while one was open for 9% of the time, Pallas kernels for 2%

profile of v8, /device:TPU:1, one launch (start us, length us, event | category | flops | bytes accessed | tf_op | source)
XLA Modules:
  0.0 110.1 jit_solution(11051185388606387426)
XLA Ops:
  0.6 4.1 %pack.1 = bf16[32,128,128]{2,1,0:T(8,128)(2,1)} custom-call(s32[1,64]{1,0:T(1,128)} %bitcast.31, s32[2,32]{1,0:T(2,128)} %bitcast.29, f32[1,40]{1,0:T(1,128)} %bitcast.30, bf16[40,3,16,128]{3,2,1,0:T(8,128)(2,1)} %fourier_in.1), custom_call_target="tpu_custom_call" | custom-call | tf_op jit(solution)/shard_map/pack/pallas_call | solution.py:357
  4.7 0.0 copy-start.3
  4.7 11.9 %all-to-all-start = ((bf16[32,128,128]{2,1,0:T(8,128)(2,1)}), bf16[32,128,128]{2,1,0:T(8,128)(2,1)S(1)}, u32[]{:S(2)}, u32[]{:S(2)}) async-start(bf16[32,128,128]{2,1,0:T(8,128)(2,1)} %pack.1), calls=%async_computation | async-start | bytes 2097152 | tf_op jit(solution)/shard_map/all_to_all | solution.py:376
  16.6 0.0 copy-done.3
  16.7 0.1 convert_reduce_fusion.1
  16.8 0.2 dynamic-slice_reduce_fusion
  16.9 0.1 fusion.9.damping
  17.0 24.2 %all-to-all-done.arrived = bf16[32,128,128]{2,1,0:T(8,128)(2,1)S(1)} async-done(((bf16[32,128,128]{2,1,0:T(8,128)(2,1)}), bf16[32,128,128]{2,1,0:T(8,128)(2,1)S(1)}, u32[]{:S(2)}, u32[]{:S(2)}) %all-to-all-start) | async-done | bytes 1048608 | tf_op jit(solution)/shard_map/all_to_all | solution.py:376
  41.2 9.2 %spectral.1 = (bf16[4,96,640]{2,1,0:T(8,128)(2,1)S(1)}, bf16[32,64,384]{2,1,0:T(8,128)(2,1)}) custom-call(bf16[32,128,128]{2,1,0:T(8,128)(2,1)S(1)} %all-to-all-done.arrived, bf16[4,1280,640]{2,1,0:T(8,128)(2,1)} %bitcast.27, f32[4,640]{1,0:T(4,128)S(1)} %fusion.9.damping), custom_call_target="tpu_custom_call" | custom-call | tf_op jit(solution)/shard_map/spectral/pallas_call | solution.py:387
  50.4 8.6 %all-to-all-start.1 = ((bf16[32,64,384]{2,1,0:T(8,128)(2,1)}), bf16[32,64,384]{2,1,0:T(8,128)(2,1)S(1)}, u32[]{:S(2)}, u32[]{:S(2)}) async-start(bf16[32,64,384]{2,1,0:T(8,128)(2,1)} %get-tuple-element.16), calls=%async_computation.1 | async-start | bytes 3145728 | tf_op jit(solution)/shard_map/all_to_all | solution.py:409
  59.0 0.1 fusion.7
  59.1 0.1 slice_reduce_fusion
  59.3 0.1 reshape_squeeze.3
  59.4 0.7 convert_reduce_fusion
  60.1 0.1 reshape.145.column_of
  60.2 1.2 %copy.23 = bf16[4,3,2,16,640]{4,2,3,1,0:T(2,128)(2,1)} copy(bf16[4,3,2,16,640]{4,3,2,1,0:T(8,128)(2,1)S(1)} %bitcast.23) | data formatting | bytes 983040 | tf_op jit(solution)/shard_map/reshape | solution.py:412
  61.3 5.8 %multiply_convert_fusion.1 = (bf16[20,128,1,128]{3,1,2,0:T(8,128)(2,1)S(1)}, bf16[20,128,1,128]{3,1,2,0:T(8,128)(2,1)S(1)}) fusion(f32[128]{0:T(128)S(1)} %compare_select_fusion, s32[20,128]{1,0:T(8,128)S(1)} %multiply_add_fusion, s32[128]{0:T(128)S(1)} %get-tuple-element.20), kind=kLoop, calls=%fused_computation.5 | loop fusion | flops 4587520 | bytes 1321984 | tf_op jit(solution)/shard_map/convert.2
  67.2 0.1 pad_maximum_fusion
  67.3 0.0 copy-start.1
  67.3 1.4 %copy.19 = bf16[20,128,2,128]{3,2,1,0:T(2,128)(2,1)S(1)} copy(bf16[20,128,2,128]{3,1,2,0:T(8,128)(2,1)S(1)} %pad_maximum_fusion) | data formatting | bytes 2621440 | tf_op jit(solution)/shard_map/concatenate | solution.py:421
  68.7 27.2 %all-to-all-done.1.received = bf16[32,64,384]{2,1,0:T(8,128)(2,1)S(1)} async-done(((bf16[32,64,384]{2,1,0:T(8,128)(2,1)}), bf16[32,64,384]{2,1,0:T(8,128)(2,1)S(1)}, u32[]{:S(2)}, u32[]{:S(2)}) %all-to-all-start.1) | async-done | bytes 1572896 | tf_op jit(solution)/shard_map/all_to_all | solution.py:409
  95.8 0.0 copy-done.1
  95.8 0.0 copy-start
  95.8 0.0 copy-start.2
  95.8 2.5 %blocks.1 = (f32[64,48,128]{2,1,0:T(8,128)S(1)}, bf16[192,128]{1,0:T(8,128)(2,1)S(1)}, bf16[192,128]{1,0:T(8,128)(2,1)S(1)}, f32[256,16,128]{2,1,0:T(8,128)S(1)}) custom-call(s32[64]{0:T(128)S(1)} %reshape.145.column_of, bf16[32,64,384]{2,1,0:T(8,128)(2,1)S(1)} %all-to-all-done.1.received, bf16[20,256,128]{2,1,0:T(8,128)(2,1)S(1)} %bitcast.22, ...), custom_call_target="tpu_custom_call" | custom-call | tf_op jit(solution)/shard_map/blocks/pallas_call | solution.py:431
  98.4 5.5 %collective-permute-start = (bf16[192,128]{1,0:T(8,128)(2,1)S(1)}, bf16[192,128]{1,0:T(8,128)(2,1)S(1)}, u32[]{:S(2)}, u32[]{:S(2)}) collective-permute-start(bf16[192,128]{1,0:T(8,128)(2,1)S(1)} %get-tuple-element.24), channel_id=1, source_target_pairs={{1,0},{2,1},{3,2},{4,3},{5,4},{6,5},{7,6},{9,8},{10,9},{11,10},{12... | collective-permute-start | bytes 147464 | tf_op jit(solution)/shard_map/ppermute | solution.py:446
  103.9 0.0 copy-done
  103.9 0.0 copy-done.2
  103.9 2.4 %horizontal.1 = f32[256,48,128]{2,1,0:T(8,128)S(1)} custom-call(s32[4,256]{1,0:T(4,128)S(1)} %bitcast.25, f32[64,48,128]{2,1,0:T(8,128)S(1)} %get-tuple-element.22.blocks, f32[256,4,128]{2,1,0:T(4,128)S(1)} %copy-done), custom_call_target="tpu_custom_call" | custom-call | flops 12582912 | bytes 6291456 | tf_op jit(solution)/shard_map/horizontal/pallas_call | solution.py:447
  106.3 0.5 collective-permute-done.above
  106.8 3.3 %vertical.1 = bf16[256,3,16,128]{3,2,1,0:T(8,128)(2,1)} custom-call(s32[4,256]{1,0:T(4,128)S(1)} %bitcast.26, s32[1]{0:T(128)} %bitcast.13.at_top, f32[256,48,128]{2,1,0:T(8,128)S(1)} %horizontal.1, bf16[192,128]{1,0:T(8,128)(2,1)S(1)} %get-tuple-element.23.highest, bf16[192,128]{1,0:T(8,128)(2,1)S(1)} %collective-permute-done.above, ...), custom_call_target="tpu_custom_call" | custom-call | tf_op jit(solution)/shard_map/vertical/pallas_call | solution.py:458
  (7 shorter events, 0.1 us)
Async XLA Ops:
  4.7 11.9 %copy-start.3 = (s32[64,1]{0,1:T(1,128)S(1)}, s32[64,1]{0,1:T(1,128)}, u32[]{:S(2)}) copy-start(s32[64,1]{0,1:T(1,128)} %param.11) | copy-start | bytes 772
  4.7 36.5 %all-to-all-start = ((bf16[32,128,128]{2,1,0:T(8,128)(2,1)}), bf16[32,128,128]{2,1,0:T(8,128)(2,1)S(1)}, u32[]{:S(2)}, u32[]{:S(2)}) async-start(bf16[32,128,128]{2,1,0:T(8,128)(2,1)} %pack.1), calls=%async_computation | async-start | bytes 2097152 | tf_op jit(solution)/shard_map/all_to_all | solution.py:376
  50.4 45.4 %all-to-all-start.1 = ((bf16[32,64,384]{2,1,0:T(8,128)(2,1)}), bf16[32,64,384]{2,1,0:T(8,128)(2,1)S(1)}, u32[]{:S(2)}, u32[]{:S(2)}) async-start(bf16[32,64,384]{2,1,0:T(8,128)(2,1)} %get-tuple-element.16), calls=%async_computation.1 | async-start | bytes 3145728 | tf_op jit(solution)/shard_map/all_to_all | solution.py:409
  67.3 28.5 %copy-start.1 = (f32[256,16]{0,1:T(8,128)S(1)}, f32[256,16]{0,1:T(8,128)}, u32[]{:S(2)}) copy-start(f32[256,16]{0,1:T(8,128)} %param.15) | copy-start | bytes 49156
  95.8 8.0 %copy-start = (f32[256,4,128]{2,1,0:T(4,128)S(1)}, f32[256,4,128]{2,1,0:T(4,128)}, u32[]{:S(2)}) copy-start(f32[256,4,128]{2,1,0:T(4,128)} %hweight.3) | copy-start | bytes 1572868
  95.8 8.0 %copy-start.2 = (s32[256,4]{0,1:T(4,128)S(1)}, s32[256,4]{0,1:T(4,128)}, u32[]{:S(2)}) copy-start(s32[256,4]{0,1:T(4,128)} %param.13) | copy-start | bytes 12292
  98.4 8.4 %collective-permute-start = (bf16[192,128]{1,0:T(8,128)(2,1)S(1)}, bf16[192,128]{1,0:T(8,128)(2,1)S(1)}, u32[]{:S(2)}, u32[]{:S(2)}) collective-permute-start(bf16[192,128]{1,0:T(8,128)(2,1)S(1)} %get-tuple-element.24), channel_id=1, source_target_pairs={{1,0},{2,1},{3,2},{4,3},{5,4},{6,5},{7,6},{9,8},{10,9},{11,10},{12... | collective-permute-start | bytes 147464 | tf_op jit(solution)/shard_map/ppermute | solution.py:446

commit v9 on v8

--- a/solution.py
+++ b/solution.py
@@ -82,20 +82,29 @@
     weights = jnp.where(turn_row == turn_column, jnp.broadcast_to(gauss[...], (lat_dev, lat_dev)), 0.0)
     weight[...] = jnp.broadcast_to(jnp.sum(weights, axis=1, keepdims=True), weight.shape)
 
-    for t in range(lat_dev):
-        if t % chunk == 0:
-            large[t // chunk].wait()
-        rows = fourier[t].reshape(fields * levels, columns).astype(jnp.float32)
-        rows = (rows * weight[t : t + 1, :]).astype(jnp.bfloat16)
-        parts = []
-        for slot in range(slots):
-            for field in range(fields):
-                for part in range(2):
-                    parts.append(rows[field * levels : (field + 1) * levels] * masks[2 * slot + part])
-        spread = jnp.concatenate(parts, axis=0)
-        chosen = mxu(chooser, spread, NT)
-        for tile in range(tiles):
-            scratch[tile, pl.ds(t, owners, stride=lat_dev), :] = chosen[:, tile * LANES : (tile + 1) * LANES]
+    none = jnp.zeros_like(chooser)
+    chooser = jnp.concatenate(
+        [jnp.concatenate([chooser, none], axis=1), jnp.concatenate([none, chooser], axis=1)], axis=0
+    )
+    for pair in range(0, lat_dev, 2):
+        if pair % chunk == 0:
+            large[pair // chunk].wait()
+        spread = []
+        for t in range(pair, pair + 2):
+            rows = fourier[t].reshape(fields * levels, columns).astype(jnp.float32)
+            rows = (rows * weight[t : t + 1, :]).astype(jnp.bfloat16)
+            parts = []
+            for slot in range(slots):
+                for field in range(fields):
+                    for part in range(2):
+                        parts.append(rows[field * levels : (field + 1) * levels] * masks[2 * slot + part])
+            spread.append(jnp.concatenate(parts, axis=0))
+        chosen = mxu(chooser, jnp.concatenate(spread, axis=1), NT)
+        for side in range(2):
+            for tile in range(tiles):
+                scratch[tile, pl.ds(pair + side, owners, stride=lat_dev), :] = chosen[
+                    side * owners : (side + 1) * owners, tile * LANES : (tile + 1) * LANES
+                ]
 
     ids = send_ids[...].astype(jnp.float32)
     in_row = jnp.floor((ids + 0.5) * (1.0 / BLOCKS_X))
@@ -121,20 +130,26 @@
         send(g).wait()
 
 
+def fetch_kernel(table_in, table, room, sem):
+    copy = pltpu.make_async_copy(table_in.at[0], table, sem)
+    copy.start()
+    copy.wait()
+
+
 def spectral_kernel(
-    arrived, tables_in, damping, spectral, message, tables, made, turned, rows_at, listed, row_of, listed_sem, in_sem, out_sem
+    arrived, first_table, tables_in, damping, _, spectral, message, tables, made, turned, rows_at, listed, row_of, listed_sem, in_sem, out_sem
 ):
     slots, per_slot, degrees = spectral.shape
     latitudes = tables.shape[1]
 
     def fetch(slot):
-        return pltpu.make_async_copy(tables_in.at[slot], tables.at[slot], in_sem.at[slot])
+        return pltpu.make_async_copy(tables_in.at[slot], tables.at[slot - 1], in_sem.at[slot - 1])
 
     def fetch_one(slot, carry):
         fetch(slot).start()
         return carry
 
-    lax.fori_loop(0, slots, fetch_one, 0)
+    lax.fori_loop(1, slots, fetch_one, 0)
     half = per_slot // 2
     field_rows = half // 3
     bands = arrived.shape[0]
@@ -155,10 +170,9 @@
     gap = jnp.zeros((LANES - half, degrees), jnp.bfloat16)
     chunk = 256
 
-    def one_slot(slot, carry):
-        fetch(slot).wait()
+    def one_slot(slot, table):
         own = turned[pl.ds(pl.multiple_of(slot * per_slot, 32), per_slot), :]
-        spectra = mxu(own, tables[slot], NN)
+        spectra = mxu(own, table[...], NN)
         damped = (spectra * damping[pl.ds(slot, 1), :]).astype(jnp.bfloat16)
         spectral[slot] = damped
         sides = []
@@ -169,14 +183,19 @@
             sides.append(gap)
         sides = jnp.concatenate(sides, axis=0)
         for at in range(0, latitudes, chunk):
-            back = mxu(tables[slot, at : at + chunk, :], sides, NT)
+            back = mxu(table[at : at + chunk, :], sides, NT)
             for part in range(2):
                 rows_at[pl.ds(at * 2 * slots + slot * 2 + part, chunk, stride=2 * slots), :] = back[
                     :, part * LANES : (part + 1) * LANES
                 ]
-        return carry
-
-    lax.fori_loop(0, slots, one_slot, 0)
+
+    def later_slot(slot, carry):
+        fetch(slot).wait()
+        one_slot(slot, tables.at[slot - 1])
+        return carry
+
+    one_slot(0, first_table)
+    lax.fori_loop(1, slots, later_slot, 0)
 
     lists.wait()
     lane = lax.broadcasted_iota(jnp.int32, (8, LANES), 1)
@@ -384,28 +403,42 @@
     damping = keep_mask * damping_curve(degrees)[None, :]
 
     message_shape = (lat_count, entries // 8 * slot_most * 2, 8 * half)
+    first_table, room = pl.pallas_call(
+        fetch_kernel,
+        out_shape=[
+            jax.ShapeDtypeStruct(legendre.shape[2:], legendre.dtype),
+            jax.ShapeDtypeStruct(message_shape, jnp.bfloat16),
+        ],
+        in_specs=[hbm],
+        out_specs=[vmem, hbm],
+        scratch_shapes=[pltpu.SemaphoreType.DMA],
+        compiler_params=pltpu.CompilerParams(vmem_limit_bytes=48 * 2**20),
+        cost_estimate=pl.CostEstimate(flops=0, bytes_accessed=legendre.size, transcendentals=0),
+        name="fetch",
+    )(legendre[0])
     spectral_rows, message_two = pl.pallas_call(
         spectral_kernel,
-        in_specs=[vmem, hbm, vmem],
+        in_specs=[vmem, vmem, hbm, vmem, hbm],
         out_specs=[vmem, hbm],
+        input_output_aliases={4: 1},
         scratch_shapes=[
-            pltpu.VMEM((slot_most, latitudes, degrees), jnp.bfloat16),
+            pltpu.VMEM((slot_most - 1, latitudes, degrees), jnp.bfloat16),
             pltpu.VMEM(message_shape, jnp.bfloat16),
             pltpu.VMEM((message_lanes, latitudes), jnp.bfloat16),
             pltpu.VMEM((latitudes * 2 * slot_most, LANES), jnp.float32),
             pltpu.VMEM((lat_count, LANES), jnp.int32),
             pltpu.SMEM((lat_count, LANES), jnp.int32),
             pltpu.SemaphoreType.DMA,
-            pltpu.SemaphoreType.DMA((slot_most,)),
+            pltpu.SemaphoreType.DMA((slot_most - 1,)),
             pltpu.SemaphoreType.DMA((lat_count // 4,)),
         ],
         out_shape=[
             jax.ShapeDtypeStruct((slot_most, per_slot, degrees), jnp.bfloat16),
             jax.ShapeDtypeStruct(message_shape, jnp.bfloat16),
         ],
-        compiler_params=pltpu.CompilerParams(vmem_limit_bytes=52 * 2**20),
+        compiler_params=pltpu.CompilerParams(vmem_limit_bytes=48 * 2**20),
         name="spectral",
-    )(arrived, legendre[0], damping)
+    )(arrived, first_table, legendre[0], damping, room)
     received = lax.all_to_all(message_two, "lat", split_axis=0, concat_axis=0, tiled=True)
 
     spectral = jnp.transpose(

time: 110 us -> 111 us (level)
  waiting for transfers between devices: 51.9 us -> 49.3 us
  local copies, waits for them, and re-layouts: 2.86 us -> 5.45 us
    all_to_all x1, waiting for transfers between devices: 24.2 us -> 21.6 us  [per_device(): lax.all_to_all(message_one, 'lat', split_axis=0, concat_axis=0, tiled=True)]
    unnamed x8 -> x12, local copies, waits for them, and re-layouts: 0.02 us -> 2.61 us
    pallas_call x1 -> x2, Pallas kernels: 9.16 us -> 9.55 us  [the longest x1 8.11 us: per_device(): pl.pallas_call(spectral_kernel, in_specs=[vmem, vmem, hbm, vmem, hbm], ou...]
  transfers between devices with their start and end apart: 3 -> 3, of which waited for: 3 -> 3; matrix products, arithmetic and copies ran while one was open for 9% -> 9% of each run, Pallas kernels for 2% -> 3%
where the time goes in v9:
time: 111 us; the launch traced here: 110 us
  waiting for transfers between devices  49.3 us (44%)
  starting transfers between devices  26 us (23%)
  Pallas kernels  21.7 us (20%)
  other arithmetic  7.11 us (6%)
  local copies, waits for them, and re-layouts  5.45 us (5%)
    all_to_all x1, waiting for transfers between devices, per_device(): lax.all_to_all(message_two, 'lat', split_axis=0, concat_axis=0, tiled=True)  27.1 us
    all_to_all x1, waiting for transfers between devices, per_device(): lax.all_to_all(message_one, 'lat', split_axis=0, concat_axis=0, tiled=True)  21.6 us
    all_to_all x1, starting transfers between devices, per_device(): lax.all_to_all(message_one, 'lat', split_axis=0, concat_axis=0, tiled=True)  11.9 us
    all_to_all x1, starting transfers between devices, per_device(): lax.all_to_all(message_two, 'lat', split_axis=0, concat_axis=0, tiled=True)  8.62 us
    pallas_call x1, Pallas kernels, per_device(): pl.pallas_call(spectral_kernel, in_specs=[vmem, vmem, hbm, vmem, hbm], ou...  8.11 us
    another operation x1, other arithmetic  5.81 us
    ppermute x1, starting transfers between devices, per_device(): lax.ppermute(lowest, 'lev', [(i, i - 1) for i in range(1, lev_count)])  5.49 us
    pallas_call x1, Pallas kernels, per_device(): pl.pallas_call(pack_kernel, out_shape=jax.ShapeDtypeStruct((lat_count, ti...  3.88 us
  transfers between devices with their start and end apart: 3, of which 3 were waited for; matrix products, arithmetic and copies ran while one was open for 9% of the time, Pallas kernels for 3%

profile of v9, /device:TPU:1, one launch (start us, length us, event | category | flops | bytes accessed | tf_op | source)
XLA Modules:
  0.0 110.3 jit_solution(11375271026678118020)
XLA Ops:
  0.6 3.9 %pack.1 = bf16[32,128,128]{2,1,0:T(8,128)(2,1)} custom-call(s32[1,64]{1,0:T(1,128)} %bitcast.32, s32[2,32]{1,0:T(2,128)} %bitcast.30, f32[1,40]{1,0:T(1,128)} %bitcast.31, bf16[40,3,16,128]{3,2,1,0:T(8,128)(2,1)} %fourier_in.1), custom_call_target="tpu_custom_call" | custom-call | tf_op jit(solution)/shard_map/pack/pallas_call | solution.py:376
  4.5 11.9 %all-to-all-start = ((bf16[32,128,128]{2,1,0:T(8,128)(2,1)}), bf16[32,128,128]{2,1,0:T(8,128)(2,1)S(1)}, u32[]{:S(2)}, u32[]{:S(2)}) async-start(bf16[32,128,128]{2,1,0:T(8,128)(2,1)} %pack.1), calls=%async_computation | async-start | bytes 2097152 | tf_op jit(solution)/shard_map/all_to_all | solution.py:395
  16.4 0.0 copy-start.5
  16.4 1.4 %fetch.1 = (bf16[1280,640]{1,0:T(8,128)(2,1)S(1)}, bf16[32,64,384]{2,1,0:T(8,128)(2,1)}) custom-call(bf16[4,1280,640]{2,1,0:T(8,128)(2,1)} %bitcast.27), custom_call_target="tpu_custom_call" | custom-call | bytes 3276800 | tf_op jit(solution)/shard_map/fetch/pallas_call | solution.py:406
  17.9 0.0 copy-start.1
  17.9 1.2 %copy-done.1 = bf16[1280,640]{1,0:T(8,128)(2,1)} copy-done((bf16[1280,640]{1,0:T(8,128)(2,1)}, bf16[1280,640]{1,0:T(8,128)(2,1)S(1)}, u32[]{:S(2)}) %copy-start.1) | copy-done | bytes 1638424
  19.1 0.0 copy-done.5
  19.1 0.1 convert_reduce_fusion.1
  19.2 0.2 dynamic-slice_reduce_fusion
  19.3 0.1 fusion.9.damping
  19.4 21.6 %all-to-all-done.arrived = bf16[32,128,128]{2,1,0:T(8,128)(2,1)S(1)} async-done(((bf16[32,128,128]{2,1,0:T(8,128)(2,1)}), bf16[32,128,128]{2,1,0:T(8,128)(2,1)S(1)}, u32[]{:S(2)}, u32[]{:S(2)}) %all-to-all-start) | async-done | bytes 1048608 | tf_op jit(solution)/shard_map/all_to_all | solution.py:395
  41.0 0.0 copy-start.2
  41.0 1.4 %copy-done.2 = bf16[1280,640]{1,0:T(8,128)(2,1)S(1)} copy-done((bf16[1280,640]{1,0:T(8,128)(2,1)S(1)}, bf16[1280,640]{1,0:T(8,128)(2,1)}, u32[]{:S(2)}) %copy-start.2) | copy-done | bytes 1638424
  42.5 8.1 %spectral.1 = (bf16[4,96,640]{2,1,0:T(8,128)(2,1)S(1)}, bf16[32,64,384]{2,1,0:T(8,128)(2,1)}) custom-call(bf16[32,128,128]{2,1,0:T(8,128)(2,1)S(1)} %all-to-all-done.arrived, bf16[1280,640]{1,0:T(8,128)(2,1)S(1)} %copy-done.2, bf16[4,1280,640]{2,1,0:T(8,128)(2,1)} %bitcast.28, f32[4,640]{1,0:T(4,128)S(1)} %fusion.9.damping, ...), custom_call_target="tpu_custom_call", output_to_operand_aliasing={{1}: (4, {})} | custom-call | tf_op jit(solution)/shard_map/spectral/pallas_call | solution.py:419
  50.6 8.6 %all-to-all-start.1 = ((bf16[32,64,384]{2,1,0:T(8,128)(2,1)}), bf16[32,64,384]{2,1,0:T(8,128)(2,1)S(1)}, u32[]{:S(2)}, u32[]{:S(2)}) async-start(bf16[32,64,384]{2,1,0:T(8,128)(2,1)} %get-tuple-element.20), calls=%async_computation.1 | async-start | bytes 3145728 | tf_op jit(solution)/shard_map/all_to_all | solution.py:442
  59.2 0.1 fusion.7
  59.3 0.1 slice_reduce_fusion
  59.5 0.1 reshape_squeeze.3
  59.5 0.7 convert_reduce_fusion
  60.2 0.1 reshape.145.column_of
  60.4 1.2 %copy.24 = bf16[4,3,2,16,640]{4,2,3,1,0:T(2,128)(2,1)} copy(bf16[4,3,2,16,640]{4,3,2,1,0:T(8,128)(2,1)S(1)} %bitcast.23) | data formatting | bytes 983040 | tf_op jit(solution)/shard_map/reshape | solution.py:445
  61.5 5.8 %multiply_convert_fusion.1 = (bf16[20,128,1,128]{3,1,2,0:T(8,128)(2,1)S(1)}, bf16[20,128,1,128]{3,1,2,0:T(8,128)(2,1)S(1)}) fusion(f32[128]{0:T(128)S(1)} %compare_select_fusion, s32[20,128]{1,0:T(8,128)S(1)} %multiply_add_fusion, s32[128]{0:T(128)S(1)} %get-tuple-element.24), kind=kLoop, calls=%fused_computation.5 | loop fusion | flops 4587520 | bytes 1321984 | tf_op jit(solution)/shard_map/convert.2
  67.3 0.1 pad_maximum_fusion
  67.5 0.0 copy-start.3
  67.5 1.4 %copy.20 = bf16[20,128,2,128]{3,2,1,0:T(2,128)(2,1)S(1)} copy(bf16[20,128,2,128]{3,1,2,0:T(8,128)(2,1)S(1)} %pad_maximum_fusion) | data formatting | bytes 2621440 | tf_op jit(solution)/shard_map/concatenate | solution.py:454
  68.9 27.1 %all-to-all-done.1.received = bf16[32,64,384]{2,1,0:T(8,128)(2,1)S(1)} async-done(((bf16[32,64,384]{2,1,0:T(8,128)(2,1)}), bf16[32,64,384]{2,1,0:T(8,128)(2,1)S(1)}, u32[]{:S(2)}, u32[]{:S(2)}) %all-to-all-start.1) | async-done | bytes 1572896 | tf_op jit(solution)/shard_map/all_to_all | solution.py:442
  96.0 0.0 copy-done.3
  96.0 0.0 copy-start
  96.0 0.0 copy-start.4
  96.0 2.5 %blocks.1 = (f32[64,48,128]{2,1,0:T(8,128)S(1)}, bf16[192,128]{1,0:T(8,128)(2,1)S(1)}, bf16[192,128]{1,0:T(8,128)(2,1)S(1)}, f32[256,16,128]{2,1,0:T(8,128)S(1)}) custom-call(s32[64]{0:T(128)S(1)} %reshape.145.column_of, bf16[32,64,384]{2,1,0:T(8,128)(2,1)S(1)} %all-to-all-done.1.received, bf16[20,256,128]{2,1,0:T(8,128)(2,1)S(1)} %bitcast.22, ...), custom_call_target="tpu_custom_call" | custom-call | tf_op jit(solution)/shard_map/blocks/pallas_call | solution.py:464
  98.6 5.5 %collective-permute-start = (bf16[192,128]{1,0:T(8,128)(2,1)S(1)}, bf16[192,128]{1,0:T(8,128)(2,1)S(1)}, u32[]{:S(2)}, u32[]{:S(2)}) collective-permute-start(bf16[192,128]{1,0:T(8,128)(2,1)S(1)} %get-tuple-element.28), channel_id=1, source_target_pairs={{1,0},{2,1},{3,2},{4,3},{5,4},{6,5},{7,6},{9,8},{10,9},{11,10},{12... | collective-permute-start | bytes 147464 | tf_op jit(solution)/shard_map/ppermute | solution.py:479
  104.1 0.0 copy-done
  104.1 0.0 copy-done.4
  104.1 2.4 %horizontal.1 = f32[256,48,128]{2,1,0:T(8,128)S(1)} custom-call(s32[4,256]{1,0:T(4,128)S(1)} %bitcast.25, f32[64,48,128]{2,1,0:T(8,128)S(1)} %get-tuple-element.26.blocks, f32[256,4,128]{2,1,0:T(4,128)S(1)} %copy-done), custom_call_target="tpu_custom_call" | custom-call | flops 12582912 | bytes 6291456 | tf_op jit(solution)/shard_map/horizontal/pallas_call | solution.py:480
  106.5 0.5 collective-permute-done.above
  107.0 3.3 %vertical.1 = bf16[256,3,16,128]{3,2,1,0:T(8,128)(2,1)} custom-call(s32[4,256]{1,0:T(4,128)S(1)} %bitcast.26, s32[1]{0:T(128)} %bitcast.13.at_top, f32[256,48,128]{2,1,0:T(8,128)S(1)} %horizontal.1, bf16[192,128]{1,0:T(8,128)(2,1)S(1)} %get-tuple-element.27.highest, bf16[192,128]{1,0:T(8,128)(2,1)S(1)} %collective-permute-done.above, ...), custom_call_target="tpu_custom_call" | custom-call | tf_op jit(solution)/shard_map/vertical/pallas_call | solution.py:491
  (7 shorter events, 0.1 us)
Async XLA Ops:
  4.5 36.5 %all-to-all-start = ((bf16[32,128,128]{2,1,0:T(8,128)(2,1)}), bf16[32,128,128]{2,1,0:T(8,128)(2,1)S(1)}, u32[]{:S(2)}, u32[]{:S(2)}) async-start(bf16[32,128,128]{2,1,0:T(8,128)(2,1)} %pack.1), calls=%async_computation | async-start | bytes 2097152 | tf_op jit(solution)/shard_map/all_to_all | solution.py:395
  16.4 2.7 %copy-start.5 = (s32[64,1]{0,1:T(1,128)S(1)}, s32[64,1]{0,1:T(1,128)}, u32[]{:S(2)}) copy-start(s32[64,1]{0,1:T(1,128)} %param.11) | copy-start | bytes 772
  17.9 1.2 %copy-start.1 = (bf16[1280,640]{1,0:T(8,128)(2,1)}, bf16[1280,640]{1,0:T(8,128)(2,1)S(1)}, u32[]{:S(2)}) copy-start(bf16[1280,640]{1,0:T(8,128)(2,1)S(1)} %get-tuple-element.16.first_table) | copy-start | bytes 4915204
  41.0 1.4 %copy-start.2 = (bf16[1280,640]{1,0:T(8,128)(2,1)S(1)}, bf16[1280,640]{1,0:T(8,128)(2,1)}, u32[]{:S(2)}) copy-start(bf16[1280,640]{1,0:T(8,128)(2,1)} %copy-done.1) | copy-start | bytes 4915204
  50.6 45.4 %all-to-all-start.1 = ((bf16[32,64,384]{2,1,0:T(8,128)(2,1)}), bf16[32,64,384]{2,1,0:T(8,128)(2,1)S(1)}, u32[]{:S(2)}, u32[]{:S(2)}) async-start(bf16[32,64,384]{2,1,0:T(8,128)(2,1)} %get-tuple-element.20), calls=%async_computation.1 | async-start | bytes 3145728 | tf_op jit(solution)/shard_map/all_to_all | solution.py:442
  67.5 28.5 %copy-start.3 = (f32[256,16]{0,1:T(8,128)S(1)}, f32[256,16]{0,1:T(8,128)}, u32[]{:S(2)}) copy-start(f32[256,16]{0,1:T(8,128)} %param.15) | copy-start | bytes 49156
  96.0 8.1 %copy-start = (f32[256,4,128]{2,1,0:T(4,128)S(1)}, f32[256,4,128]{2,1,0:T(4,128)}, u32[]{:S(2)}) copy-start(f32[256,4,128]{2,1,0:T(4,128)} %hweight.3) | copy-start | bytes 1572868
  96.0 8.1 %copy-start.4 = (s32[256,4]{0,1:T(4,128)S(1)}, s32[256,4]{0,1:T(4,128)}, u32[]{:S(2)}) copy-start(s32[256,4]{0,1:T(4,128)} %param.13) | copy-start | bytes 12292
  98.6 8.4 %collective-permute-start = (bf16[192,128]{1,0:T(8,128)(2,1)S(1)}, bf16[192,128]{1,0:T(8,128)(2,1)S(1)}, u32[]{:S(2)}, u32[]{:S(2)}) collective-permute-start(bf16[192,128]{1,0:T(8,128)(2,1)S(1)} %get-tuple-element.28), channel_id=1, source_target_pairs={{1,0},{2,1},{3,2},{4,3},{5,4},{6,5},{7,6},{9,8},{10,9},{11,10},{12... | collective-permute-start | bytes 147464 | tf_op jit(solution)/shard_map/ppermute | solution.py:479

commit v10 on v8

--- a/solution.py
+++ b/solution.py
@@ -82,20 +82,29 @@
     weights = jnp.where(turn_row == turn_column, jnp.broadcast_to(gauss[...], (lat_dev, lat_dev)), 0.0)
     weight[...] = jnp.broadcast_to(jnp.sum(weights, axis=1, keepdims=True), weight.shape)
 
-    for t in range(lat_dev):
-        if t % chunk == 0:
-            large[t // chunk].wait()
-        rows = fourier[t].reshape(fields * levels, columns).astype(jnp.float32)
-        rows = (rows * weight[t : t + 1, :]).astype(jnp.bfloat16)
-        parts = []
-        for slot in range(slots):
-            for field in range(fields):
-                for part in range(2):
-                    parts.append(rows[field * levels : (field + 1) * levels] * masks[2 * slot + part])
-        spread = jnp.concatenate(parts, axis=0)
-        chosen = mxu(chooser, spread, NT)
-        for tile in range(tiles):
-            scratch[tile, pl.ds(t, owners, stride=lat_dev), :] = chosen[:, tile * LANES : (tile + 1) * LANES]
+    none = jnp.zeros_like(chooser)
+    chooser = jnp.concatenate(
+        [jnp.concatenate([chooser, none], axis=1), jnp.concatenate([none, chooser], axis=1)], axis=0
+    )
+    for pair in range(0, lat_dev, 2):
+        if pair % chunk == 0:
+            large[pair // chunk].wait()
+        spread = []
+        for t in range(pair, pair + 2):
+            rows = fourier[t].reshape(fields * levels, columns).astype(jnp.float32)
+            rows = (rows * weight[t : t + 1, :]).astype(jnp.bfloat16)
+            parts = []
+            for slot in range(slots):
+                for field in range(fields):
+                    for part in range(2):
+                        parts.append(rows[field * levels : (field + 1) * levels] * masks[2 * slot + part])
+            spread.append(jnp.concatenate(parts, axis=0))
+        chosen = mxu(chooser, jnp.concatenate(spread, axis=1), NT)
+        for side in range(2):
+            for tile in range(tiles):
+                scratch[tile, pl.ds(pair + side, owners, stride=lat_dev), :] = chosen[
+                    side * owners : (side + 1) * owners, tile * LANES : (tile + 1) * LANES
+                ]
 
     ids = send_ids[...].astype(jnp.float32)
     in_row = jnp.floor((ids + 0.5) * (1.0 / BLOCKS_X))
@@ -144,10 +153,13 @@
     lists = pltpu.make_async_copy(listed, row_of, listed_sem)
 
     wide = arrived[...].astype(jnp.float32)
-    band = lax.broadcasted_iota(jnp.int32, (bands, LANES), 0)
-    listed[...] = (wide[:, tiles * lat_dev, :].astype(jnp.int32) + band * lat_dev) * 8
+    unit = identity(LANES)
+    band = lax.broadcasted_iota(jnp.int32, listed.shape, 1)
+    rows = wide[:, tiles * lat_dev, :].astype(jnp.bfloat16)
+    rows = jnp.concatenate([rows, jnp.zeros((LANES - bands, LANES), jnp.bfloat16)], axis=0)
+    rows = mxu(unit[: listed.shape[0]], rows, NT).astype(jnp.int32)
+    listed[...] = (rows + jnp.where(band < bands, band, 0) * lat_dev) * 8
     lists.start()
-    unit = identity(LANES)
     for tile in range(tiles):
         columns = wide[:, tile * lat_dev : (tile + 1) * lat_dev, :].reshape(latitudes, LANES)
         turned[tile * LANES : (tile + 1) * LANES, :] = mxu(unit, columns.astype(jnp.bfloat16), NT).astype(jnp.bfloat16)
@@ -198,7 +210,7 @@
                     built = [None] * wide_tiles
                     for e in range(8):
                         entry = (pair * 2 + side) * 8 + e
-                        at = pl.multiple_of(row_of[entry // 2, receivers * (entry % 2) + r], 8)
+                        at = pl.multiple_of(row_of[receivers * (entry % 2) + r, entry // 2], 8)
                         row = rows_at[pl.ds(at, 8), :]
                         start = e * half
                         if start % LANES:
@@ -260,14 +272,14 @@
 
 def horizontal_kernel(stencil, blocks, hweight, horizontal):
     rows = horizontal.shape[0]
-    together = 32
+    together = stencil.shape[1] // 4
 
     def some_rows(i, carry):
         for k in range(together):
             a = i * together + k
             total = None
             for q in range(4):
-                term = hweight[a, q : q + 1, :] * blocks[stencil[q, a]]
+                term = hweight[a, q : q + 1, :] * blocks[stencil[i, k * 4 + q]]
                 total = term if total is None else total + term
             horizontal[a] = total
         return carry
@@ -292,7 +304,7 @@
     lax.fori_loop(0, entries // together, widen, 0)
 
     row = lax.broadcasted_iota(jnp.int32, (8, LANES), 0)
-    piece = 32
+    piece = stencil.shape[1] // 4
     pieces = rows // piece
 
     def send(i):
@@ -304,7 +316,7 @@
             a = i * piece + k
             last = None
             for q in range(4):
-                term = hweight[a, q : q + 1, :] * wide[stencil[q, a]]
+                term = hweight[a, q : q + 1, :] * wide[stencil[i, k * 4 + q]]
                 last = term if last is None else last + term
             for field in range(fields):
                 parts = []
@@ -393,8 +405,8 @@
             pltpu.VMEM(message_shape, jnp.bfloat16),
             pltpu.VMEM((message_lanes, latitudes), jnp.bfloat16),
             pltpu.VMEM((latitudes * 2 * slot_most, LANES), jnp.float32),
-            pltpu.VMEM((lat_count, LANES), jnp.int32),
-            pltpu.SMEM((lat_count, LANES), jnp.int32),
+            pltpu.VMEM((entries, LANES), jnp.int32),
+            pltpu.SMEM((entries, LANES), jnp.int32),
             pltpu.SemaphoreType.DMA,
             pltpu.SemaphoreType.DMA((slot_most,)),
             pltpu.SemaphoreType.DMA((lat_count // 4,)),
@@ -426,7 +438,7 @@
     lev_count = lax.axis_size("lev")
     at_top = (lax.axis_index("lev") == lev_count - 1).astype(jnp.int32).reshape(1)
     vertical = vweight.T
-    corners = stencil.T
+    corners = stencil.reshape(arrivals // 32, 128)
     received, vertical, corners, at_top = lax.optimization_barrier((received, vertical, corners, at_top))
     blocks, lowest, highest, spread = pl.pallas_call(
         block_kernel,

time: 110 us -> 110 us (level)
  no operation moved by 1% of the time
where the time goes in v10:
time: 110 us; the launch traced here: 109 us
  waiting for transfers between devices  51.5 us (47%)
  starting transfers between devices  25.9 us (24%)
  Pallas kernels  20.7 us (19%)
  other arithmetic  7.12 us (6%)
  local copies, waits for them, and re-layouts  3.11 us (3%)
    all_to_all x1, waiting for transfers between devices, per_device(): lax.all_to_all(message_two, 'lat', split_axis=0, concat_axis=0, tiled=True)  26.9 us
    all_to_all x1, waiting for transfers between devices, per_device(): lax.all_to_all(message_one, 'lat', split_axis=0, concat_axis=0, tiled=True)  24.2 us
    all_to_all x1, starting transfers between devices, per_device(): lax.all_to_all(message_one, 'lat', split_axis=0, concat_axis=0, tiled=True)  11.9 us
    all_to_all x1, starting transfers between devices, per_device(): lax.all_to_all(message_two, 'lat', split_axis=0, concat_axis=0, tiled=True)  8.59 us
    pallas_call x1, Pallas kernels, per_device(): pl.pallas_call(spectral_kernel, in_specs=[vmem, hbm, vmem], out_specs=[vm...  8.58 us
    another operation x1, other arithmetic  5.81 us
    ppermute x1, starting transfers between devices, per_device(): lax.ppermute(lowest, 'lev', [(i, i - 1) for i in range(1, lev_count)])  5.48 us
    pallas_call x1, Pallas kernels, per_device(): pl.pallas_call(pack_kernel, out_shape=jax.ShapeDtypeStruct((lat_count, ti...  3.87 us
  transfers between devices with their start and end apart: 3, of which 3 were waited for; matrix products, arithmetic and copies ran while one was open for 9% of the time, Pallas kernels for 2%

profile of v10, /device:TPU:1, one launch (start us, length us, event | category | flops | bytes accessed | tf_op | source)
XLA Modules:
  0.0 109.2 jit_solution(17673270002886193304)
XLA Ops:
  0.6 3.9 %pack.1 = bf16[32,128,128]{2,1,0:T(8,128)(2,1)} custom-call(s32[1,64]{1,0:T(1,128)} %bitcast.28, s32[2,32]{1,0:T(2,128)} %bitcast.26, f32[1,40]{1,0:T(1,128)} %bitcast.27, bf16[40,3,16,128]{3,2,1,0:T(8,128)(2,1)} %fourier_in.1), custom_call_target="tpu_custom_call" | custom-call | tf_op jit(solution)/shard_map/pack/pallas_call | solution.py:369
  4.5 0.0 copy-start.3
  4.5 11.9 %all-to-all-start = ((bf16[32,128,128]{2,1,0:T(8,128)(2,1)}), bf16[32,128,128]{2,1,0:T(8,128)(2,1)S(1)}, u32[]{:S(2)}, u32[]{:S(2)}) async-start(bf16[32,128,128]{2,1,0:T(8,128)(2,1)} %pack.1), calls=%async_computation | async-start | bytes 2097152 | tf_op jit(solution)/shard_map/all_to_all | solution.py:388
  16.4 0.0 copy-done.3
  16.5 0.1 convert_reduce_fusion.1
  16.6 0.2 dynamic-slice_reduce_fusion
  16.7 0.1 fusion.9.damping
  16.8 24.2 %all-to-all-done.arrived = bf16[32,128,128]{2,1,0:T(8,128)(2,1)S(1)} async-done(((bf16[32,128,128]{2,1,0:T(8,128)(2,1)}), bf16[32,128,128]{2,1,0:T(8,128)(2,1)S(1)}, u32[]{:S(2)}, u32[]{:S(2)}) %all-to-all-start) | async-done | bytes 1048608 | tf_op jit(solution)/shard_map/all_to_all | solution.py:388
  41.0 8.6 %spectral.1 = (bf16[4,96,640]{2,1,0:T(8,128)(2,1)S(1)}, bf16[32,64,384]{2,1,0:T(8,128)(2,1)}) custom-call(bf16[32,128,128]{2,1,0:T(8,128)(2,1)S(1)} %all-to-all-done.arrived, bf16[4,1280,640]{2,1,0:T(8,128)(2,1)} %bitcast.24, f32[4,640]{1,0:T(4,128)S(1)} %fusion.9.damping), custom_call_target="tpu_custom_call" | custom-call | tf_op jit(solution)/shard_map/spectral/pallas_call | solution.py:399
  49.6 0.0 copy-start.2
  49.6 8.6 %all-to-all-start.1 = ((bf16[32,64,384]{2,1,0:T(8,128)(2,1)}), bf16[32,64,384]{2,1,0:T(8,128)(2,1)S(1)}, u32[]{:S(2)}, u32[]{:S(2)}) async-start(bf16[32,64,384]{2,1,0:T(8,128)(2,1)} %get-tuple-element.16), calls=%async_computation.1 | async-start | bytes 3145728 | tf_op jit(solution)/shard_map/all_to_all | solution.py:421
  58.2 0.0 copy-done.2
  58.2 0.1 copy.21
  58.4 0.1 reshape.141.stencil
  58.5 0.1 fusion.7
  58.6 0.1 slice_reduce_fusion
  58.8 0.1 reshape_squeeze.3
  58.9 0.7 convert_reduce_fusion
  59.6 0.1 reshape.149.column_of
  59.7 1.2 %copy.27 = bf16[4,3,2,16,640]{4,2,3,1,0:T(2,128)(2,1)} copy(bf16[4,3,2,16,640]{4,3,2,1,0:T(8,128)(2,1)S(1)} %bitcast.22) | data formatting | bytes 983040 | tf_op jit(solution)/shard_map/reshape | solution.py:424
  60.8 5.8 %multiply_convert_fusion.1 = (bf16[20,128,1,128]{3,1,2,0:T(8,128)(2,1)S(1)}, bf16[20,128,1,128]{3,1,2,0:T(8,128)(2,1)S(1)}) fusion(f32[128]{0:T(128)S(1)} %compare_select_fusion, s32[20,128]{1,0:T(8,128)S(1)} %multiply_add_fusion, s32[128]{0:T(128)S(1)} %get-tuple-element.20), kind=kLoop, calls=%fused_computation.5 | loop fusion | flops 4587520 | bytes 1321984 | tf_op jit(solution)/shard_map/convert.2
  66.6 0.1 pad_maximum_fusion
  66.8 0.0 copy-start.1
  66.8 1.4 %copy.23 = bf16[20,128,2,128]{3,2,1,0:T(2,128)(2,1)S(1)} copy(bf16[20,128,2,128]{3,1,2,0:T(8,128)(2,1)S(1)} %pad_maximum_fusion) | data formatting | bytes 2621440 | tf_op jit(solution)/shard_map/concatenate | solution.py:433
  68.2 26.9 %all-to-all-done.1.received = bf16[32,64,384]{2,1,0:T(8,128)(2,1)S(1)} async-done(((bf16[32,64,384]{2,1,0:T(8,128)(2,1)}), bf16[32,64,384]{2,1,0:T(8,128)(2,1)S(1)}, u32[]{:S(2)}, u32[]{:S(2)}) %all-to-all-start.1) | async-done | bytes 1572896 | tf_op jit(solution)/shard_map/all_to_all | solution.py:421
  95.1 0.0 copy-done.1
  95.1 0.0 copy-start
  95.1 2.5 %blocks.1 = (f32[64,48,128]{2,1,0:T(8,128)S(1)}, bf16[192,128]{1,0:T(8,128)(2,1)S(1)}, bf16[192,128]{1,0:T(8,128)(2,1)S(1)}, f32[256,16,128]{2,1,0:T(8,128)S(1)}) custom-call(s32[64]{0:T(128)S(1)} %reshape.149.column_of, bf16[32,64,384]{2,1,0:T(8,128)(2,1)S(1)} %all-to-all-done.1.received, bf16[20,256,128]{2,1,0:T(8,128)(2,1)S(1)} %bitcast.21, ...), custom_call_target="tpu_custom_call" | custom-call | tf_op jit(solution)/shard_map/blocks/pallas_call | solution.py:443
  97.6 5.5 %collective-permute-start = (bf16[192,128]{1,0:T(8,128)(2,1)S(1)}, bf16[192,128]{1,0:T(8,128)(2,1)S(1)}, u32[]{:S(2)}, u32[]{:S(2)}) collective-permute-start(bf16[192,128]{1,0:T(8,128)(2,1)S(1)} %get-tuple-element.24), channel_id=1, source_target_pairs={{1,0},{2,1},{3,2},{4,3},{5,4},{6,5},{7,6},{9,8},{10,9},{11,10},{12... | collective-permute-start | bytes 147464 | tf_op jit(solution)/shard_map/ppermute | solution.py:458
  103.1 0.0 copy-done
  103.1 2.5 %horizontal.1 = f32[256,48,128]{2,1,0:T(8,128)S(1)} custom-call(s32[8,128]{1,0:T(8,128)S(1)} %reshape.141.stencil, f32[64,48,128]{2,1,0:T(8,128)S(1)} %get-tuple-element.22.blocks, f32[256,4,128]{2,1,0:T(4,128)S(1)} %copy-done), custom_call_target="tpu_custom_call" | custom-call | flops 12582912 | bytes 6291456 | tf_op jit(solution)/shard_map/horizontal/pallas_call | solution.py:459
  105.6 0.4 collective-permute-done.above
  106.0 3.2 %vertical.1 = bf16[256,3,16,128]{3,2,1,0:T(8,128)(2,1)} custom-call(s32[8,128]{1,0:T(8,128)S(1)} %reshape.141.stencil, s32[1]{0:T(128)} %bitcast.12.at_top, f32[256,48,128]{2,1,0:T(8,128)S(1)} %horizontal.1, bf16[192,128]{1,0:T(8,128)(2,1)S(1)} %get-tuple-element.23.highest, bf16[192,128]{1,0:T(8,128)(2,1)S(1)} %collective-permute-done.above, ...), custom_call_target="tpu_custom_call" | custom-call | tf_op jit(solution)/shard_map/vertical/pallas_call | solution.py:470
  (7 shorter events, 0.1 us)
Async XLA Ops:
  4.5 11.9 %copy-start.3 = (s32[64,1]{0,1:T(1,128)S(1)}, s32[64,1]{0,1:T(1,128)}, u32[]{:S(2)}) copy-start(s32[64,1]{0,1:T(1,128)} %param.11) | copy-start | bytes 772
  4.5 36.5 %all-to-all-start = ((bf16[32,128,128]{2,1,0:T(8,128)(2,1)}), bf16[32,128,128]{2,1,0:T(8,128)(2,1)S(1)}, u32[]{:S(2)}, u32[]{:S(2)}) async-start(bf16[32,128,128]{2,1,0:T(8,128)(2,1)} %pack.1), calls=%async_computation | async-start | bytes 2097152 | tf_op jit(solution)/shard_map/all_to_all | solution.py:388
  49.6 8.6 %copy-start.2 = (s32[256,4]{0,1:T(4,128)S(1)}, s32[256,4]{0,1:T(4,128)}, u32[]{:S(2)}) copy-start(s32[256,4]{0,1:T(4,128)} %param.13) | copy-start | bytes 12292
  49.6 45.4 %all-to-all-start.1 = ((bf16[32,64,384]{2,1,0:T(8,128)(2,1)}), bf16[32,64,384]{2,1,0:T(8,128)(2,1)S(1)}, u32[]{:S(2)}, u32[]{:S(2)}) async-start(bf16[32,64,384]{2,1,0:T(8,128)(2,1)} %get-tuple-element.16), calls=%async_computation.1 | async-start | bytes 3145728 | tf_op jit(solution)/shard_map/all_to_all | solution.py:421
  66.8 28.3 %copy-start.1 = (f32[256,16]{0,1:T(8,128)S(1)}, f32[256,16]{0,1:T(8,128)}, u32[]{:S(2)}) copy-start(f32[256,16]{0,1:T(8,128)} %param.15) | copy-start | bytes 49156
  95.1 8.0 %copy-start = (f32[256,4,128]{2,1,0:T(4,128)S(1)}, f32[256,4,128]{2,1,0:T(4,128)}, u32[]{:S(2)}) copy-start(f32[256,4,128]{2,1,0:T(4,128)} %hweight.3) | copy-start | bytes 1572868
  97.6 8.4 %collective-permute-start = (bf16[192,128]{1,0:T(8,128)(2,1)S(1)}, bf16[192,128]{1,0:T(8,128)(2,1)S(1)}, u32[]{:S(2)}, u32[]{:S(2)}) collective-permute-start(bf16[192,128]{1,0:T(8,128)(2,1)S(1)} %get-tuple-element.24), channel_id=1, source_target_pairs={{1,0},{2,1},{3,2},{4,3},{5,4},{6,5},{7,6},{9,8},{10,9},{11,10},{12... | collective-permute-start | bytes 147464 | tf_op jit(solution)/shard_map/ppermute | solution.py:458

commit v11 on v10

--- a/solution.py
+++ b/solution.py
@@ -1,3 +1,4 @@
+import functools
 import math
 
 import jax
@@ -232,8 +233,25 @@
         send(g).wait()
 
 
+def horizontal_rows(stencil, blocks, hweight, horizontal):
+    together = stencil.shape[1] // 4
+
+    def some_rows(i, carry):
+        for k in range(together):
+            a = i * together + k
+            total = None
+            for q in range(4):
+                term = hweight[a, q : q + 1, :] * blocks[stencil[i, k * 4 + q]]
+                total = term if total is None else total + term
+            horizontal[a] = total
+        return carry
+
+    lax.fori_loop(0, stencil.shape[0], some_rows, 0)
+
+
 def block_kernel(
-    column_of, received, zonal, vweight, blocks, lowest, highest, spread, lowest_scratch, highest_scratch
+    column_of, stencil, flags, received, zonal, vweight, hweight, blocks, lowest, highest, spread, horizontal,
+    lowest_scratch, highest_scratch,
 ):
     owners, message_rows, message_lanes = received.shape
     unit = identity(LANES)
@@ -269,28 +287,23 @@
     lowest[...] = lowest_scratch[...].astype(jnp.bfloat16)
     highest[...] = highest_scratch[...].astype(jnp.bfloat16)
 
-
-def horizontal_kernel(stencil, blocks, hweight, horizontal):
-    rows = horizontal.shape[0]
-    together = stencil.shape[1] // 4
-
-    def some_rows(i, carry):
-        for k in range(together):
-            a = i * together + k
-            total = None
-            for q in range(4):
-                term = hweight[a, q : q + 1, :] * blocks[stencil[i, k * 4 + q]]
-                total = term if total is None else total + term
-            horizontal[a] = total
-        return carry
-
-    lax.fori_loop(0, rows // together, some_rows, 0)
-
-
-def vertical_kernel(stencil, at_top, horizontal, highest, above, hweight, spread, arrival, made, over_rows, wide, out_sem):
+    @pl.when(flags[1] == 1)
+    def _():
+        horizontal_rows(stencil, blocks, hweight, horizontal)
+
+
+def horizontal_kernel(stencil, flags, blocks, hweight, horizontal):
+    @pl.when(flags[1] == 0)
+    def _():
+        horizontal_rows(stencil, blocks, hweight, horizontal)
+
+
+def vertical_kernel(
+    stencil, flags, early, late, highest, above, hweight, spread, arrival, made, over_rows, wide, out_sem
+):
     rows, fields, levels, _ = made.shape
     entries = wide.shape[0]
-    top = at_top[0] == 1
+    top = flags[0] == 1
     over_rows[...] = jnp.where(top, highest[...].astype(jnp.float32), above[...].astype(jnp.float32))
     together = 8
 
@@ -311,7 +324,7 @@
         at = pl.multiple_of(i * piece, piece)
         return pltpu.make_async_copy(made.at[pl.ds(at, piece)], arrival.at[pl.ds(at, piece)], out_sem.at[i])
 
-    def some_rows(i, carry):
+    def some_rows(horizontal, i, carry):
         for k in range(piece):
             a = i * piece + k
             last = None
@@ -331,7 +344,14 @@
         send(i).start()
         return carry
 
-    lax.fori_loop(0, pieces, some_rows, 0)
+    @pl.when(flags[1] == 1)
+    def _():
+        lax.fori_loop(0, pieces, functools.partial(some_rows, early), 0)
+
+    @pl.when(flags[1] == 0)
+    def _():
+        lax.fori_loop(0, pieces, functools.partial(some_rows, late), 0)
+
     for i in range(pieces):
         send(i).wait()
 
@@ -436,41 +456,43 @@
     column_of = lax.dynamic_index_in_dim(all_columns, device_row, 2, keepdims=False)
     column_of = column_of.astype(jnp.int32).reshape(-1)
     lev_count = lax.axis_size("lev")
-    at_top = (lax.axis_index("lev") == lev_count - 1).astype(jnp.int32).reshape(1)
+    level_group = lax.axis_index("lev")
+    flags = jnp.stack([(level_group == lev_count - 1).astype(jnp.int32), (level_group % 2).astype(jnp.int32)])
     vertical = vweight.T
     corners = stencil.reshape(arrivals // 32, 128)
-    received, vertical, corners, at_top = lax.optimization_barrier((received, vertical, corners, at_top))
-    blocks, lowest, highest, spread = pl.pallas_call(
+    received, vertical, corners, flags = lax.optimization_barrier((received, vertical, corners, flags))
+    blocks, lowest, highest, spread, early = pl.pallas_call(
         block_kernel,
         out_shape=[
             jax.ShapeDtypeStruct((entries, half, BLK), jnp.float32),
             jax.ShapeDtypeStruct((fields * entries, BLK), jnp.bfloat16),
             jax.ShapeDtypeStruct((fields * entries, BLK), jnp.bfloat16),
             jax.ShapeDtypeStruct((arrivals, levels, BLK), jnp.float32),
+            jax.ShapeDtypeStruct((arrivals, half, BLK), jnp.float32),
         ],
-        in_specs=[smem, vmem, vmem, vmem],
-        out_specs=[vmem, vmem, vmem, vmem],
+        in_specs=[smem, smem, smem, vmem, vmem, vmem, vmem],
+        out_specs=[vmem, vmem, vmem, vmem, vmem],
         scratch_shapes=[pltpu.VMEM((fields * entries, BLK), jnp.float32)] * 2,
         compiler_params=pltpu.CompilerParams(vmem_limit_bytes=16 * 2**20),
         name="blocks",
-    )(column_of, received, zonal, vertical)
+    )(column_of, corners, flags, received, zonal, vertical, hweight)
 
     above = lax.ppermute(lowest, "lev", [(i, i - 1) for i in range(1, lev_count)])
-    horizontal = pl.pallas_call(
+    late = pl.pallas_call(
         horizontal_kernel,
         out_shape=jax.ShapeDtypeStruct((arrivals, half, BLK), jnp.float32),
-        in_specs=[smem, vmem, vmem],
+        in_specs=[smem, smem, vmem, vmem],
         out_specs=vmem,
         compiler_params=pltpu.CompilerParams(vmem_limit_bytes=16 * 2**20),
         cost_estimate=pl.CostEstimate(
             flops=8 * arrivals * half * BLK, bytes_accessed=4 * arrivals * half * BLK, transcendentals=0
         ),
         name="horizontal",
-    )(corners, blocks, hweight)
+    )(corners, flags, blocks, hweight)
     arrival = pl.pallas_call(
         vertical_kernel,
         out_shape=jax.ShapeDtypeStruct((arrivals, fields, levels, BLK), jnp.bfloat16),
-        in_specs=[smem, smem, vmem, vmem, vmem, vmem, vmem],
+        in_specs=[smem, smem, vmem, vmem, vmem, vmem, vmem, vmem],
         out_specs=hbm,
         scratch_shapes=[
             pltpu.VMEM((arrivals, fields, levels, BLK), jnp.bfloat16),
@@ -480,7 +502,7 @@
         ],
         compiler_params=pltpu.CompilerParams(vmem_limit_bytes=16 * 2**20),
         name="vertical",
-    )(corners, at_top, horizontal, highest, above, hweight, spread)
+    )(corners, flags, early, late, highest, above, hweight, spread)
     return (spectral[None], arrival)
 
 

time: 110 us -> 110 us (level)
  starting transfers between devices: 25.9 us -> 24 us
  waiting for transfers between devices: 51.5 us -> 53.3 us
    pallas_call x1, Pallas kernels: 2.54 us -> 4.55 us  [per_device(): pl.pallas_call(block_kernel, out_shape=[jax.ShapeDtypeStruct((entries, ha...]
    ppermute x1, starting transfers between devices: 5.48 us -> 3.55 us  [per_device(): lax.ppermute(lowest, 'lev', [(i, i - 1) for i in range(1, lev_count)])]
    ppermute x1, waiting for transfers between devices: 0.44 us -> 2.32 us  [per_device(): lax.ppermute(lowest, 'lev', [(i, i - 1) for i in range(1, lev_count)])]
    pallas_call x1, Pallas kernels: 2.49 us -> 0.61 us  [per_device(): pl.pallas_call(horizontal_kernel, out_shape=jax.ShapeDtypeStruct((arrival...]
    another operation x1 -> x2, other arithmetic: 5.81 us -> 5.89 us
  transfers between devices with their start and end apart: 3 -> 3, of which waited for: 3 -> 3; matrix products, arithmetic and copies ran while one was open for 9% -> 9% of each run, Pallas kernels for 2% -> 1%
where the time goes in v11:
time: 110 us; the launch traced here: 109 us
  waiting for transfers between devices  53.3 us (48%)
  starting transfers between devices  24 us (22%)
  Pallas kernels  20.9 us (19%)
  other arithmetic  7.19 us (7%)
  local copies, waits for them, and re-layouts  3.12 us (3%)
    all_to_all x1, waiting for transfers between devices, per_device(): lax.all_to_all(message_two, 'lat', split_axis=0, concat_axis=0, tiled=True)  26.8 us
    all_to_all x1, waiting for transfers between devices, per_device(): lax.all_to_all(message_one, 'lat', split_axis=0, concat_axis=0, tiled=True)  24.2 us
    all_to_all x1, starting transfers between devices, per_device(): lax.all_to_all(message_one, 'lat', split_axis=0, concat_axis=0, tiled=True)  11.9 us
    all_to_all x1, starting transfers between devices, per_device(): lax.all_to_all(message_two, 'lat', split_axis=0, concat_axis=0, tiled=True)  8.59 us
    pallas_call x1, Pallas kernels, per_device(): pl.pallas_call(spectral_kernel, in_specs=[vmem, hbm, vmem], out_specs=[vm...  8.58 us
    another operation x1, other arithmetic  5.81 us
    pallas_call x1, Pallas kernels, per_device(): pl.pallas_call(block_kernel, out_shape=[jax.ShapeDtypeStruct((entries, ha...  4.55 us
    pallas_call x1, Pallas kernels, per_device(): pl.pallas_call(pack_kernel, out_shape=jax.ShapeDtypeStruct((lat_count, ti...  3.87 us
  transfers between devices with their start and end apart: 3, of which 3 were waited for; matrix products, arithmetic and copies ran while one was open for 9% of the time, Pallas kernels for 1%

profile of v11, /device:TPU:1, one launch (start us, length us, event | category | flops | bytes accessed | tf_op | source)
XLA Modules:
  0.0 109.4 jit_solution(17338433737705348073)
XLA Ops:
  0.6 3.9 %pack.1 = bf16[32,128,128]{2,1,0:T(8,128)(2,1)} custom-call(s32[1,64]{1,0:T(1,128)} %bitcast.29, s32[2,32]{1,0:T(2,128)} %bitcast.27, f32[1,40]{1,0:T(1,128)} %bitcast.28, bf16[40,3,16,128]{3,2,1,0:T(8,128)(2,1)} %fourier_in.1), custom_call_target="tpu_custom_call" | custom-call | tf_op jit(solution)/shard_map/pack/pallas_call | solution.py:389
  4.5 0.0 copy-start.3
  4.5 11.9 %all-to-all-start = ((bf16[32,128,128]{2,1,0:T(8,128)(2,1)}), bf16[32,128,128]{2,1,0:T(8,128)(2,1)S(1)}, u32[]{:S(2)}, u32[]{:S(2)}) async-start(bf16[32,128,128]{2,1,0:T(8,128)(2,1)} %pack.1), calls=%async_computation | async-start | bytes 2097152 | tf_op jit(solution)/shard_map/all_to_all | solution.py:408
  16.4 0.0 copy-done.3
  16.5 0.1 convert_reduce_fusion.1
  16.6 0.2 dynamic-slice_reduce_fusion
  16.7 0.1 fusion.9.damping
  16.8 24.2 %all-to-all-done.arrived = bf16[32,128,128]{2,1,0:T(8,128)(2,1)S(1)} async-done(((bf16[32,128,128]{2,1,0:T(8,128)(2,1)}), bf16[32,128,128]{2,1,0:T(8,128)(2,1)S(1)}, u32[]{:S(2)}, u32[]{:S(2)}) %all-to-all-start) | async-done | bytes 1048608 | tf_op jit(solution)/shard_map/all_to_all | solution.py:408
  41.0 8.6 %spectral.1 = (bf16[4,96,640]{2,1,0:T(8,128)(2,1)S(1)}, bf16[32,64,384]{2,1,0:T(8,128)(2,1)}) custom-call(bf16[32,128,128]{2,1,0:T(8,128)(2,1)S(1)} %all-to-all-done.arrived, bf16[4,1280,640]{2,1,0:T(8,128)(2,1)} %bitcast.25, f32[4,640]{1,0:T(4,128)S(1)} %fusion.9.damping), custom_call_target="tpu_custom_call" | custom-call | tf_op jit(solution)/shard_map/spectral/pallas_call | solution.py:419
  49.6 0.0 copy-start.2
  49.6 8.6 %all-to-all-start.1 = ((bf16[32,64,384]{2,1,0:T(8,128)(2,1)}), bf16[32,64,384]{2,1,0:T(8,128)(2,1)S(1)}, u32[]{:S(2)}, u32[]{:S(2)}) async-start(bf16[32,64,384]{2,1,0:T(8,128)(2,1)} %get-tuple-element.17), calls=%async_computation.1 | async-start | bytes 3145728 | tf_op jit(solution)/shard_map/all_to_all | solution.py:441
  58.2 0.0 copy-done.2
  58.2 0.1 copy.21
  58.4 0.1 reshape.135.stencil
  58.5 0.1 pad_add_fusion.flags
  58.6 0.1 fusion.7
  58.7 0.1 slice_reduce_fusion
  58.9 0.1 reshape_squeeze.3
  58.9 0.7 convert_reduce_fusion
  59.6 0.1 reshape.140.column_of
  59.7 1.2 %copy.27 = bf16[4,3,2,16,640]{4,2,3,1,0:T(2,128)(2,1)} copy(bf16[4,3,2,16,640]{4,3,2,1,0:T(8,128)(2,1)S(1)} %bitcast.23) | data formatting | bytes 983040 | tf_op jit(solution)/shard_map/reshape | solution.py:444
  60.9 5.8 %multiply_convert_fusion.1 = (bf16[20,128,1,128]{3,1,2,0:T(8,128)(2,1)S(1)}, bf16[20,128,1,128]{3,1,2,0:T(8,128)(2,1)S(1)}) fusion(f32[128]{0:T(128)S(1)} %compare_select_fusion, s32[20,128]{1,0:T(8,128)S(1)} %multiply_add_fusion, s32[128]{0:T(128)S(1)} %get-tuple-element.21), kind=kLoop, calls=%fused_computation.5 | loop fusion | flops 4587520 | bytes 1321984 | tf_op jit(solution)/shard_map/convert.2
  66.7 0.1 pad_maximum_fusion
  66.9 0.0 copy-start
  66.9 0.0 copy-start.1
  66.9 1.4 %copy.23 = bf16[20,128,2,128]{3,2,1,0:T(2,128)(2,1)S(1)} copy(bf16[20,128,2,128]{3,1,2,0:T(8,128)(2,1)S(1)} %pad_maximum_fusion) | data formatting | bytes 2621440 | tf_op jit(solution)/shard_map/concatenate | solution.py:453
  68.3 26.8 %all-to-all-done.1.received = bf16[32,64,384]{2,1,0:T(8,128)(2,1)S(1)} async-done(((bf16[32,64,384]{2,1,0:T(8,128)(2,1)}), bf16[32,64,384]{2,1,0:T(8,128)(2,1)S(1)}, u32[]{:S(2)}, u32[]{:S(2)}) %all-to-all-start.1) | async-done | bytes 1572896 | tf_op jit(solution)/shard_map/all_to_all | solution.py:441
  95.1 0.0 copy-done
  95.1 0.0 copy-done.1
  95.1 4.5 %blocks.1 = (f32[64,48,128]{2,1,0:T(8,128)S(1)}, bf16[192,128]{1,0:T(8,128)(2,1)S(1)}, bf16[192,128]{1,0:T(8,128)(2,1)S(1)}, f32[256,16,128]{2,1,0:T(8,128)S(1)}, f32[256,48,128]{2,1,0:T(8,128)S(1)}) custom-call(s32[64]{0:T(128)S(1)} %reshape.140.column_of, s32[8,128]{1,0:T(8,128)S(1)} %reshape.135.stencil, s32[2]{0:T(128)S(1)} %pad_add_fusion.flags, ...), custom_call_target="tpu_custom_call" | custom-call | tf_op jit(solution)/shard_map/blocks/pallas_call | solution.py:464
  99.6 3.6 %collective-permute-start = (bf16[192,128]{1,0:T(8,128)(2,1)S(1)}, bf16[192,128]{1,0:T(8,128)(2,1)S(1)}, u32[]{:S(2)}, u32[]{:S(2)}) collective-permute-start(bf16[192,128]{1,0:T(8,128)(2,1)S(1)} %get-tuple-element.26), channel_id=1, source_target_pairs={{1,0},{2,1},{3,2},{4,3},{5,4},{6,5},{7,6},{9,8},{10,9},{11,10},{12... | collective-permute-start | bytes 147464 | tf_op jit(solution)/shard_map/ppermute | solution.py:480
  103.2 0.6 horizontal.1.late
  103.8 2.3 %collective-permute-done.above = bf16[192,128]{1,0:T(8,128)(2,1)S(1)} collective-permute-done((bf16[192,128]{1,0:T(8,128)(2,1)S(1)}, bf16[192,128]{1,0:T(8,128)(2,1)S(1)}, u32[]{:S(2)}, u32[]{:S(2)}) %collective-permute-start) | collective-permute-done | bytes 49184 | tf_op jit(solution)/shard_map/ppermute | solution.py:480
  106.1 3.3 %vertical.1 = bf16[256,3,16,128]{3,2,1,0:T(8,128)(2,1)} custom-call(s32[8,128]{1,0:T(8,128)S(1)} %reshape.135.stencil, s32[2]{0:T(128)S(1)} %pad_add_fusion.flags, f32[256,48,128]{2,1,0:T(8,128)S(1)} %get-tuple-element.23.early, f32[256,48,128]{2,1,0:T(8,128)S(1)} %horizontal.1.late, bf16[192,128]{1,0:T(8,128)(2,1)S(1)} %get-tuple-element.25.highest, ...), custom_call_target="tpu_custom_call" | custom-call | tf_op jit(solution)/shard_map/vertical/pallas_call | solution.py:492
  (7 shorter events, 0.1 us)
Async XLA Ops:
  4.5 11.9 %copy-start.3 = (s32[64,1]{0,1:T(1,128)S(1)}, s32[64,1]{0,1:T(1,128)}, u32[]{:S(2)}) copy-start(s32[64,1]{0,1:T(1,128)} %param.11) | copy-start | bytes 772
  4.5 36.5 %all-to-all-start = ((bf16[32,128,128]{2,1,0:T(8,128)(2,1)}), bf16[32,128,128]{2,1,0:T(8,128)(2,1)S(1)}, u32[]{:S(2)}, u32[]{:S(2)}) async-start(bf16[32,128,128]{2,1,0:T(8,128)(2,1)} %pack.1), calls=%async_computation | async-start | bytes 2097152 | tf_op jit(solution)/shard_map/all_to_all | solution.py:408
  49.6 8.6 %copy-start.2 = (s32[256,4]{0,1:T(4,128)S(1)}, s32[256,4]{0,1:T(4,128)}, u32[]{:S(2)}) copy-start(s32[256,4]{0,1:T(4,128)} %param.13) | copy-start | bytes 12292
  49.6 45.4 %all-to-all-start.1 = ((bf16[32,64,384]{2,1,0:T(8,128)(2,1)}), bf16[32,64,384]{2,1,0:T(8,128)(2,1)S(1)}, u32[]{:S(2)}, u32[]{:S(2)}) async-start(bf16[32,64,384]{2,1,0:T(8,128)(2,1)} %get-tuple-element.17), calls=%async_computation.1 | async-start | bytes 3145728 | tf_op jit(solution)/shard_map/all_to_all | solution.py:441
  66.9 28.2 %copy-start = (f32[256,4,128]{2,1,0:T(4,128)S(1)}, f32[256,4,128]{2,1,0:T(4,128)}, u32[]{:S(2)}) copy-start(f32[256,4,128]{2,1,0:T(4,128)} %hweight.5) | copy-start | bytes 1572868
  66.9 28.2 %copy-start.1 = (f32[256,16]{0,1:T(8,128)S(1)}, f32[256,16]{0,1:T(8,128)}, u32[]{:S(2)}) copy-start(f32[256,16]{0,1:T(8,128)} %param.15) | copy-start | bytes 49156
  99.6 6.5 %collective-permute-start = (bf16[192,128]{1,0:T(8,128)(2,1)S(1)}, bf16[192,128]{1,0:T(8,128)(2,1)S(1)}, u32[]{:S(2)}, u32[]{:S(2)}) collective-permute-start(bf16[192,128]{1,0:T(8,128)(2,1)S(1)} %get-tuple-element.26), channel_id=1, source_target_pairs={{1,0},{2,1},{3,2},{4,3},{5,4},{6,5},{7,6},{9,8},{10,9},{11,10},{12... | collective-permute-start | bytes 147464 | tf_op jit(solution)/shard_map/ppermute | solution.py:480

commit v12 on v10

--- a/solution.py
+++ b/solution.py
@@ -270,9 +270,10 @@
     highest[...] = highest_scratch[...].astype(jnp.bfloat16)
 
 
-def horizontal_kernel(stencil, blocks, hweight, horizontal):
-    rows = horizontal.shape[0]
+def horizontal_kernel(stencil, blocks, hweight, spread, partial, tops):
+    _, fields, levels, _ = partial.shape
     together = stencil.shape[1] // 4
+    row = lax.broadcasted_iota(jnp.int32, (8, LANES), 0)
 
     def some_rows(i, carry):
         for k in range(together):
@@ -281,13 +282,28 @@
             for q in range(4):
                 term = hweight[a, q : q + 1, :] * blocks[stencil[i, k * 4 + q]]
                 total = term if total is None else total + term
-            horizontal[a] = total
-        return carry
-
-    lax.fori_loop(0, rows // together, some_rows, 0)
-
-
-def vertical_kernel(stencil, at_top, horizontal, highest, above, hweight, spread, arrival, made, over_rows, wide, out_sem):
+            lower = spread[a, 0:8, :]
+            upper = spread[a, 8:16, :]
+            top = None
+            for field in range(fields):
+                first = total[field * levels : field * levels + 8]
+                second = total[field * levels + 8 : field * levels + 16]
+                turned = pltpu.roll(second, 7, 0)
+                up = jnp.where(row == 7, turned, pltpu.roll(first, 7, 0))
+                low = first + lower * (up - first)
+                high = jnp.where(row == 7, 0.0, second + upper * (turned - second))
+                partial[a, field] = jnp.concatenate([low, high], axis=0).astype(jnp.bfloat16)
+                placed = second if field == 0 else turned if field == 1 else pltpu.roll(second, 8 - field, 0)
+                top = placed if top is None else jnp.where(row == 7 - field, placed, top)
+            tops[a] = top
+        return carry
+
+    lax.fori_loop(0, stencil.shape[0], some_rows, 0)
+
+
+def vertical_kernel(
+    stencil, at_top, partial, tops, highest, above, hweight, spread, arrival, made, over_rows, wide, out_sem
+):
     rows, fields, levels, _ = made.shape
     entries = wide.shape[0]
     top = at_top[0] == 1
@@ -318,16 +334,13 @@
             for q in range(4):
                 term = hweight[a, q : q + 1, :] * wide[stencil[i, k * 4 + q]]
                 last = term if last is None else last + term
+            here = tops[a]
+            top = here + spread[a, levels - 1 : levels, :] * (last - here)
             for field in range(fields):
-                parts = []
-                over = last if field == 0 else pltpu.roll(last, field, 0)
-                for part in reversed(range(levels // 8)):
-                    here = horizontal[a, field * levels + part * 8 : field * levels + (part + 1) * 8, :]
-                    turned = pltpu.roll(here, 7, 0)
-                    up = jnp.where(row == 7, over, turned)
-                    parts.insert(0, here + spread[a, part * 8 : (part + 1) * 8, :] * (up - here))
-                    over = turned
-                made[a, field] = jnp.concatenate(parts, axis=0).astype(jnp.bfloat16)
+                placed = top if field == 0 else pltpu.roll(top, field, 0)
+                placed = jnp.where(row == 7, placed, 0.0)
+                patch = jnp.concatenate([jnp.zeros_like(placed), placed], axis=0).astype(jnp.bfloat16)
+                made[a, field] = partial[a, field] + patch
         send(i).start()
         return carry
 
@@ -456,21 +469,24 @@
     )(column_of, received, zonal, vertical)
 
     above = lax.ppermute(lowest, "lev", [(i, i - 1) for i in range(1, lev_count)])
-    horizontal = pl.pallas_call(
+    partial, tops = pl.pallas_call(
         horizontal_kernel,
-        out_shape=jax.ShapeDtypeStruct((arrivals, half, BLK), jnp.float32),
-        in_specs=[smem, vmem, vmem],
-        out_specs=vmem,
+        out_shape=[
+            jax.ShapeDtypeStruct((arrivals, fields, levels, BLK), jnp.bfloat16),
+            jax.ShapeDtypeStruct((arrivals, 8, BLK), jnp.float32),
+        ],
+        in_specs=[smem, vmem, vmem, vmem],
+        out_specs=[vmem, vmem],
         compiler_params=pltpu.CompilerParams(vmem_limit_bytes=16 * 2**20),
         cost_estimate=pl.CostEstimate(
             flops=8 * arrivals * half * BLK, bytes_accessed=4 * arrivals * half * BLK, transcendentals=0
         ),
         name="horizontal",
-    )(corners, blocks, hweight)
+    )(corners, blocks, hweight, spread)
     arrival = pl.pallas_call(
         vertical_kernel,
         out_shape=jax.ShapeDtypeStruct((arrivals, fields, levels, BLK), jnp.bfloat16),
-        in_specs=[smem, smem, vmem, vmem, vmem, vmem, vmem],
+        in_specs=[smem, smem, vmem, vmem, vmem, vmem, vmem, vmem],
         out_specs=hbm,
         scratch_shapes=[
             pltpu.VMEM((arrivals, fields, levels, BLK), jnp.bfloat16),
@@ -480,7 +496,7 @@
         ],
         compiler_params=pltpu.CompilerParams(vmem_limit_bytes=16 * 2**20),
         name="vertical",
-    )(corners, at_top, horizontal, highest, above, hweight, spread)
+    )(corners, at_top, partial, tops, highest, above, hweight, spread)
     return (spectral[None], arrival)
 
 

time: 110 us -> 110 us (level)
  transfers between devices with their start and end apart: 3 -> 3, of which waited for: 3 -> 2; matrix products, arithmetic and copies ran while one was open for 9% -> 9% of each run, Pallas kernels for 2% -> 3%
where the time goes in v12:
time: 110 us
  waiting for transfers between devices  51.1 us (46%)
  starting transfers between devices  25.9 us (24%)
  Pallas kernels  21.6 us (20%)
  other arithmetic  7.12 us (6%)
  local copies, waits for them, and re-layouts  3.11 us (3%)
    all_to_all x1, waiting for transfers between devices, per_device(): lax.all_to_all(message_two, 'lat', split_axis=0, concat_axis=0, tiled=True)  26.9 us
    all_to_all x1, waiting for transfers between devices, per_device(): lax.all_to_all(message_one, 'lat', split_axis=0, concat_axis=0, tiled=True)  24.2 us
    all_to_all x1, starting transfers between devices, per_device(): lax.all_to_all(message_one, 'lat', split_axis=0, concat_axis=0, tiled=True)  11.9 us
    all_to_all x1, starting transfers between devices, per_device(): lax.all_to_all(message_two, 'lat', split_axis=0, concat_axis=0, tiled=True)  8.59 us
    pallas_call x1, Pallas kernels, per_device(): pl.pallas_call(spectral_kernel, in_specs=[vmem, hbm, vmem], out_specs=[vm...  8.58 us
    another operation x1, other arithmetic  5.81 us
    ppermute x1, starting transfers between devices, per_device(): lax.ppermute(lowest, 'lev', [(i, i - 1) for i in range(1, lev_count)])  5.48 us
    pallas_call x1, Pallas kernels, per_device(): pl.pallas_call(pack_kernel, out_shape=jax.ShapeDtypeStruct((lat_count, ti...  3.87 us
  transfers between devices with their start and end apart: 3, of which 2 were waited for; matrix products, arithmetic and copies ran while one was open for 9% of the time, Pallas kernels for 3%

profile of v12, /device:TPU:1, one launch (start us, length us, event | category | flops | bytes accessed | tf_op | source)
XLA Modules:
  0.0 109.7 jit_solution(1158650777155550715)
XLA Ops:
  0.6 3.9 %pack.1 = bf16[32,128,128]{2,1,0:T(8,128)(2,1)} custom-call(s32[1,64]{1,0:T(1,128)} %bitcast.28, s32[2,32]{1,0:T(2,128)} %bitcast.26, f32[1,40]{1,0:T(1,128)} %bitcast.27, bf16[40,3,16,128]{3,2,1,0:T(8,128)(2,1)} %fourier_in.1), custom_call_target="tpu_custom_call" | custom-call | tf_op jit(solution)/shard_map/pack/pallas_call | solution.py:382
  4.5 0.0 copy-start.3
  4.5 11.9 %all-to-all-start = ((bf16[32,128,128]{2,1,0:T(8,128)(2,1)}), bf16[32,128,128]{2,1,0:T(8,128)(2,1)S(1)}, u32[]{:S(2)}, u32[]{:S(2)}) async-start(bf16[32,128,128]{2,1,0:T(8,128)(2,1)} %pack.1), calls=%async_computation | async-start | bytes 2097152 | tf_op jit(solution)/shard_map/all_to_all | solution.py:401
  16.4 0.0 copy-done.3
  16.5 0.1 convert_reduce_fusion.1
  16.6 0.2 dynamic-slice_reduce_fusion
  16.7 0.1 fusion.9.damping
  16.8 24.2 %all-to-all-done.arrived = bf16[32,128,128]{2,1,0:T(8,128)(2,1)S(1)} async-done(((bf16[32,128,128]{2,1,0:T(8,128)(2,1)}), bf16[32,128,128]{2,1,0:T(8,128)(2,1)S(1)}, u32[]{:S(2)}, u32[]{:S(2)}) %all-to-all-start) | async-done | bytes 1048608 | tf_op jit(solution)/shard_map/all_to_all | solution.py:401
  41.0 8.6 %spectral.1 = (bf16[4,96,640]{2,1,0:T(8,128)(2,1)S(1)}, bf16[32,64,384]{2,1,0:T(8,128)(2,1)}) custom-call(bf16[32,128,128]{2,1,0:T(8,128)(2,1)S(1)} %all-to-all-done.arrived, bf16[4,1280,640]{2,1,0:T(8,128)(2,1)} %bitcast.24, f32[4,640]{1,0:T(4,128)S(1)} %fusion.9.damping), custom_call_target="tpu_custom_call" | custom-call | tf_op jit(solution)/shard_map/spectral/pallas_call | solution.py:412
  49.6 0.0 copy-start.2
  49.6 8.6 %all-to-all-start.1 = ((bf16[32,64,384]{2,1,0:T(8,128)(2,1)}), bf16[32,64,384]{2,1,0:T(8,128)(2,1)S(1)}, u32[]{:S(2)}, u32[]{:S(2)}) async-start(bf16[32,64,384]{2,1,0:T(8,128)(2,1)} %get-tuple-element.18), calls=%async_computation.1 | async-start | bytes 3145728 | tf_op jit(solution)/shard_map/all_to_all | solution.py:434
  58.2 0.0 copy-done.2
  58.2 0.1 copy.21
  58.4 0.1 reshape.141.stencil
  58.5 0.1 fusion.7
  58.6 0.1 slice_reduce_fusion
  58.8 0.1 reshape_squeeze.3
  58.9 0.7 convert_reduce_fusion
  59.6 0.1 reshape.149.column_of
  59.7 1.2 %copy.27 = bf16[4,3,2,16,640]{4,2,3,1,0:T(2,128)(2,1)} copy(bf16[4,3,2,16,640]{4,3,2,1,0:T(8,128)(2,1)S(1)} %bitcast.22) | data formatting | bytes 983040 | tf_op jit(solution)/shard_map/reshape | solution.py:437
  60.8 5.8 %multiply_convert_fusion.1 = (bf16[20,128,1,128]{3,1,2,0:T(8,128)(2,1)S(1)}, bf16[20,128,1,128]{3,1,2,0:T(8,128)(2,1)S(1)}) fusion(f32[128]{0:T(128)S(1)} %compare_select_fusion, s32[20,128]{1,0:T(8,128)S(1)} %multiply_add_fusion, s32[128]{0:T(128)S(1)} %get-tuple-element.22), kind=kLoop, calls=%fused_computation.5 | loop fusion | flops 4587520 | bytes 1321984 | tf_op jit(solution)/shard_map/convert.2
  66.6 0.1 pad_maximum_fusion
  66.8 0.0 copy-start.1
  66.8 1.4 %copy.23 = bf16[20,128,2,128]{3,2,1,0:T(2,128)(2,1)S(1)} copy(bf16[20,128,2,128]{3,1,2,0:T(8,128)(2,1)S(1)} %pad_maximum_fusion) | data formatting | bytes 2621440 | tf_op jit(solution)/shard_map/concatenate | solution.py:446
  68.2 26.9 %all-to-all-done.1.received = bf16[32,64,384]{2,1,0:T(8,128)(2,1)S(1)} async-done(((bf16[32,64,384]{2,1,0:T(8,128)(2,1)}), bf16[32,64,384]{2,1,0:T(8,128)(2,1)S(1)}, u32[]{:S(2)}, u32[]{:S(2)}) %all-to-all-start.1) | async-done | bytes 1572896 | tf_op jit(solution)/shard_map/all_to_all | solution.py:434
  95.1 0.0 copy-done.1
  95.1 0.0 copy-start
  95.1 2.5 %blocks.1 = (f32[64,48,128]{2,1,0:T(8,128)S(1)}, bf16[192,128]{1,0:T(8,128)(2,1)S(1)}, bf16[192,128]{1,0:T(8,128)(2,1)S(1)}, f32[256,16,128]{2,1,0:T(8,128)S(1)}) custom-call(s32[64]{0:T(128)S(1)} %reshape.149.column_of, bf16[32,64,384]{2,1,0:T(8,128)(2,1)S(1)} %all-to-all-done.1.received, bf16[20,256,128]{2,1,0:T(8,128)(2,1)S(1)} %bitcast.21, ...), custom_call_target="tpu_custom_call" | custom-call | tf_op jit(solution)/shard_map/blocks/pallas_call | solution.py:456
  97.6 5.5 %collective-permute-start = (bf16[192,128]{1,0:T(8,128)(2,1)S(1)}, bf16[192,128]{1,0:T(8,128)(2,1)S(1)}, u32[]{:S(2)}, u32[]{:S(2)}) collective-permute-start(bf16[192,128]{1,0:T(8,128)(2,1)S(1)} %get-tuple-element.29), channel_id=1, source_target_pairs={{1,0},{2,1},{3,2},{4,3},{5,4},{6,5},{7,6},{9,8},{10,9},{11,10},{12... | collective-permute-start | bytes 147464 | tf_op jit(solution)/shard_map/ppermute | solution.py:471
  103.1 0.0 copy-done
  103.1 3.5 %horizontal.1 = (bf16[256,3,16,128]{3,2,1,0:T(8,128)(2,1)S(1)}, f32[256,8,128]{2,1,0:T(8,128)S(1)}) custom-call(s32[8,128]{1,0:T(8,128)S(1)} %reshape.141.stencil, f32[64,48,128]{2,1,0:T(8,128)S(1)} %get-tuple-element.24.blocks, f32[256,4,128]{2,1,0:T(4,128)S(1)} %copy-done, f32[256,16,128]{2,1,0:T(8,128)S(1)} %get-tuple-element.25.spread), custom_call_target="tpu_custom_call" | custom-call | flops 12582912 | bytes 6291456 | tf_op jit(solution)/shard_map/horizontal/pallas_call | solution.py:472
  106.6 0.0 collective-permute-done.above
  106.6 3.0 %vertical.1 = bf16[256,3,16,128]{3,2,1,0:T(8,128)(2,1)} custom-call(s32[8,128]{1,0:T(8,128)S(1)} %reshape.141.stencil, s32[1]{0:T(128)} %bitcast.12.at_top, bf16[256,3,16,128]{3,2,1,0:T(8,128)(2,1)S(1)} %get-tuple-element.26.partial, f32[256,8,128]{2,1,0:T(8,128)S(1)} %get-tuple-element.27.tops, bf16[192,128]{1,0:T(8,128)(2,1)S(1)} %get-tuple-element.28.highest, ...), custom_call_target="tpu_custom_call" | custom-call | tf_op jit(solution)/shard_map/vertical/pallas_call | solution.py:486
  (7 shorter events, 0.1 us)
Async XLA Ops:
  4.5 11.9 %copy-start.3 = (s32[64,1]{0,1:T(1,128)S(1)}, s32[64,1]{0,1:T(1,128)}, u32[]{:S(2)}) copy-start(s32[64,1]{0,1:T(1,128)} %param.11) | copy-start | bytes 772
  4.5 36.5 %all-to-all-start = ((bf16[32,128,128]{2,1,0:T(8,128)(2,1)}), bf16[32,128,128]{2,1,0:T(8,128)(2,1)S(1)}, u32[]{:S(2)}, u32[]{:S(2)}) async-start(bf16[32,128,128]{2,1,0:T(8,128)(2,1)} %pack.1), calls=%async_computation | async-start | bytes 2097152 | tf_op jit(solution)/shard_map/all_to_all | solution.py:401
  49.6 8.6 %copy-start.2 = (s32[256,4]{0,1:T(4,128)S(1)}, s32[256,4]{0,1:T(4,128)}, u32[]{:S(2)}) copy-start(s32[256,4]{0,1:T(4,128)} %param.13) | copy-start | bytes 12292
  49.6 45.4 %all-to-all-start.1 = ((bf16[32,64,384]{2,1,0:T(8,128)(2,1)}), bf16[32,64,384]{2,1,0:T(8,128)(2,1)S(1)}, u32[]{:S(2)}, u32[]{:S(2)}) async-start(bf16[32,64,384]{2,1,0:T(8,128)(2,1)} %get-tuple-element.18), calls=%async_computation.1 | async-start | bytes 3145728 | tf_op jit(solution)/shard_map/all_to_all | solution.py:434
  66.8 28.3 %copy-start.1 = (f32[256,16]{0,1:T(8,128)S(1)}, f32[256,16]{0,1:T(8,128)}, u32[]{:S(2)}) copy-start(f32[256,16]{0,1:T(8,128)} %param.15) | copy-start | bytes 49156
  95.1 8.0 %copy-start = (f32[256,4,128]{2,1,0:T(4,128)S(1)}, f32[256,4,128]{2,1,0:T(4,128)}, u32[]{:S(2)}) copy-start(f32[256,4,128]{2,1,0:T(4,128)} %hweight.3) | copy-start | bytes 1572868
  97.6 9.0 %collective-permute-start = (bf16[192,128]{1,0:T(8,128)(2,1)S(1)}, bf16[192,128]{1,0:T(8,128)(2,1)S(1)}, u32[]{:S(2)}, u32[]{:S(2)}) collective-permute-start(bf16[192,128]{1,0:T(8,128)(2,1)S(1)} %get-tuple-element.29), channel_id=1, source_target_pairs={{1,0},{2,1},{3,2},{4,3},{5,4},{6,5},{7,6},{9,8},{10,9},{11,10},{12... | collective-permute-start | bytes 147464 | tf_op jit(solution)/shard_map/ppermute | solution.py:471

commit v13 on v12

--- a/solution.py
+++ b/solution.py
@@ -162,7 +162,7 @@
     lists.start()
     for tile in range(tiles):
         columns = wide[:, tile * lat_dev : (tile + 1) * lat_dev, :].reshape(latitudes, LANES)
-        turned[tile * LANES : (tile + 1) * LANES, :] = mxu(unit, columns.astype(jnp.bfloat16), NT).astype(jnp.bfloat16)
+        turned[tile * LANES : (tile + 1) * LANES, :] = jnp.transpose(columns).astype(jnp.bfloat16)
 
     gap = jnp.zeros((LANES - half, degrees), jnp.bfloat16)
     chunk = 256
@@ -236,7 +236,6 @@
     column_of, received, zonal, vweight, blocks, lowest, highest, spread, lowest_scratch, highest_scratch
 ):
     owners, message_rows, message_lanes = received.shape
-    unit = identity(LANES)
     half = message_lanes // 8
     groups = message_rows // 8
     entries = blocks.shape[0]
@@ -246,9 +245,9 @@
         wide = received[:, pair * 16 : (pair + 1) * 16, :].astype(jnp.float32)
         for side in range(2):
             group = pair * 2 + side
-            own = wide[:, side * 8 : (side + 1) * 8, :].reshape(owners * 8, message_lanes).astype(jnp.bfloat16)
+            own = wide[:, side * 8 : (side + 1) * 8, :].reshape(owners * 8, message_lanes)
             turned = [
-                mxu(unit, own[:, tile * LANES : (tile + 1) * LANES], NT).astype(jnp.bfloat16)
+                jnp.transpose(own[:, tile * LANES : (tile + 1) * LANES]).astype(jnp.bfloat16)
                 for tile in range(message_lanes // LANES)
             ]
             turned = jnp.concatenate(turned, axis=0)

time: 110 us -> 109 us (level)
  no operation moved by 1% of the time
where the time goes in v13:
time: 109 us
  waiting for transfers between devices  51.1 us (47%)
  starting transfers between devices  25.9 us (24%)
  Pallas kernels  20.9 us (19%)
  other arithmetic  7.12 us (7%)
  local copies, waits for them, and re-layouts  3.11 us (3%)
    all_to_all x1, waiting for transfers between devices, per_device(): lax.all_to_all(message_two, 'lat', split_axis=0, concat_axis=0, tiled=True)  26.9 us
    all_to_all x1, waiting for transfers between devices, per_device(): lax.all_to_all(message_one, 'lat', split_axis=0, concat_axis=0, tiled=True)  24.2 us
    all_to_all x1, starting transfers between devices, per_device(): lax.all_to_all(message_one, 'lat', split_axis=0, concat_axis=0, tiled=True)  11.9 us
    all_to_all x1, starting transfers between devices, per_device(): lax.all_to_all(message_two, 'lat', split_axis=0, concat_axis=0, tiled=True)  8.59 us
    pallas_call x1, Pallas kernels, per_device(): pl.pallas_call(spectral_kernel, in_specs=[vmem, hbm, vmem], out_specs=[vm...  8.58 us
    another operation x1, other arithmetic  5.81 us
    ppermute x1, starting transfers between devices, per_device(): lax.ppermute(lowest, 'lev', [(i, i - 1) for i in range(1, lev_count)])  5.47 us
    pallas_call x1, Pallas kernels, per_device(): pl.pallas_call(pack_kernel, out_shape=jax.ShapeDtypeStruct((lat_count, ti...  3.87 us
  transfers between devices with their start and end apart: 3, of which 2 were waited for; matrix products, arithmetic and copies ran while one was open for 9% of the time, Pallas kernels for 3%

profile of v13, /device:TPU:1, one launch (start us, length us, event | category | flops | bytes accessed | tf_op | source)
XLA Modules:
  0.0 109.0 jit_solution(6289992585910275714)
XLA Ops:
  0.6 3.9 %pack.1 = bf16[32,128,128]{2,1,0:T(8,128)(2,1)} custom-call(s32[1,64]{1,0:T(1,128)} %bitcast.28, s32[2,32]{1,0:T(2,128)} %bitcast.26, f32[1,40]{1,0:T(1,128)} %bitcast.27, bf16[40,3,16,128]{3,2,1,0:T(8,128)(2,1)} %fourier_in.1), custom_call_target="tpu_custom_call" | custom-call | tf_op jit(solution)/shard_map/pack/pallas_call | solution.py:381
  4.5 0.0 copy-start.3
  4.5 11.9 %all-to-all-start = ((bf16[32,128,128]{2,1,0:T(8,128)(2,1)}), bf16[32,128,128]{2,1,0:T(8,128)(2,1)S(1)}, u32[]{:S(2)}, u32[]{:S(2)}) async-start(bf16[32,128,128]{2,1,0:T(8,128)(2,1)} %pack.1), calls=%async_computation | async-start | bytes 2097152 | tf_op jit(solution)/shard_map/all_to_all | solution.py:400
  16.4 0.0 copy-done.3
  16.5 0.1 convert_reduce_fusion.1
  16.6 0.2 dynamic-slice_reduce_fusion
  16.7 0.1 fusion.9.damping
  16.8 24.2 %all-to-all-done.arrived = bf16[32,128,128]{2,1,0:T(8,128)(2,1)S(1)} async-done(((bf16[32,128,128]{2,1,0:T(8,128)(2,1)}), bf16[32,128,128]{2,1,0:T(8,128)(2,1)S(1)}, u32[]{:S(2)}, u32[]{:S(2)}) %all-to-all-start) | async-done | bytes 1048608 | tf_op jit(solution)/shard_map/all_to_all | solution.py:400
  41.0 8.6 %spectral.1 = (bf16[4,96,640]{2,1,0:T(8,128)(2,1)S(1)}, bf16[32,64,384]{2,1,0:T(8,128)(2,1)}) custom-call(bf16[32,128,128]{2,1,0:T(8,128)(2,1)S(1)} %all-to-all-done.arrived, bf16[4,1280,640]{2,1,0:T(8,128)(2,1)} %bitcast.24, f32[4,640]{1,0:T(4,128)S(1)} %fusion.9.damping), custom_call_target="tpu_custom_call" | custom-call | tf_op jit(solution)/shard_map/spectral/pallas_call | solution.py:411
  49.6 0.0 copy-start.2
  49.6 8.6 %all-to-all-start.1 = ((bf16[32,64,384]{2,1,0:T(8,128)(2,1)}), bf16[32,64,384]{2,1,0:T(8,128)(2,1)S(1)}, u32[]{:S(2)}, u32[]{:S(2)}) async-start(bf16[32,64,384]{2,1,0:T(8,128)(2,1)} %get-tuple-element.18), calls=%async_computation.1 | async-start | bytes 3145728 | tf_op jit(solution)/shard_map/all_to_all | solution.py:433
  58.2 0.0 copy-done.2
  58.2 0.1 copy.21
  58.4 0.1 reshape.141.stencil
  58.5 0.1 fusion.7
  58.6 0.1 slice_reduce_fusion
  58.8 0.1 reshape_squeeze.3
  58.9 0.7 convert_reduce_fusion
  59.6 0.1 reshape.149.column_of
  59.7 1.2 %copy.27 = bf16[4,3,2,16,640]{4,2,3,1,0:T(2,128)(2,1)} copy(bf16[4,3,2,16,640]{4,3,2,1,0:T(8,128)(2,1)S(1)} %bitcast.22) | data formatting | bytes 983040 | tf_op jit(solution)/shard_map/reshape | solution.py:436
  60.8 5.8 %multiply_convert_fusion.1 = (bf16[20,128,1,128]{3,1,2,0:T(8,128)(2,1)S(1)}, bf16[20,128,1,128]{3,1,2,0:T(8,128)(2,1)S(1)}) fusion(f32[128]{0:T(128)S(1)} %compare_select_fusion, s32[20,128]{1,0:T(8,128)S(1)} %multiply_add_fusion, s32[128]{0:T(128)S(1)} %get-tuple-element.22), kind=kLoop, calls=%fused_computation.5 | loop fusion | flops 4587520 | bytes 1321984 | tf_op jit(solution)/shard_map/convert.2
  66.6 0.1 pad_maximum_fusion
  66.8 0.0 copy-start.1
  66.8 1.4 %copy.23 = bf16[20,128,2,128]{3,2,1,0:T(2,128)(2,1)S(1)} copy(bf16[20,128,2,128]{3,1,2,0:T(8,128)(2,1)S(1)} %pad_maximum_fusion) | data formatting | bytes 2621440 | tf_op jit(solution)/shard_map/concatenate | solution.py:445
  68.2 26.9 %all-to-all-done.1.received = bf16[32,64,384]{2,1,0:T(8,128)(2,1)S(1)} async-done(((bf16[32,64,384]{2,1,0:T(8,128)(2,1)}), bf16[32,64,384]{2,1,0:T(8,128)(2,1)S(1)}, u32[]{:S(2)}, u32[]{:S(2)}) %all-to-all-start.1) | async-done | bytes 1572896 | tf_op jit(solution)/shard_map/all_to_all | solution.py:433
  95.1 0.0 copy-done.1
  95.1 0.0 copy-start
  95.1 1.9 %blocks.1 = (f32[64,48,128]{2,1,0:T(8,128)S(1)}, bf16[192,128]{1,0:T(8,128)(2,1)S(1)}, bf16[192,128]{1,0:T(8,128)(2,1)S(1)}, f32[256,16,128]{2,1,0:T(8,128)S(1)}) custom-call(s32[64]{0:T(128)S(1)} %reshape.149.column_of, bf16[32,64,384]{2,1,0:T(8,128)(2,1)S(1)} %all-to-all-done.1.received, bf16[20,256,128]{2,1,0:T(8,128)(2,1)S(1)} %bitcast.21, ...), custom_call_target="tpu_custom_call" | custom-call | tf_op jit(solution)/shard_map/blocks/pallas_call | solution.py:455
  96.9 5.5 %collective-permute-start = (bf16[192,128]{1,0:T(8,128)(2,1)S(1)}, bf16[192,128]{1,0:T(8,128)(2,1)S(1)}, u32[]{:S(2)}, u32[]{:S(2)}) collective-permute-start(bf16[192,128]{1,0:T(8,128)(2,1)S(1)} %get-tuple-element.29), channel_id=1, source_target_pairs={{1,0},{2,1},{3,2},{4,3},{5,4},{6,5},{7,6},{9,8},{10,9},{11,10},{12... | collective-permute-start | bytes 147464 | tf_op jit(solution)/shard_map/ppermute | solution.py:470
  102.4 0.0 copy-done
  102.4 3.5 %horizontal.1 = (bf16[256,3,16,128]{3,2,1,0:T(8,128)(2,1)S(1)}, f32[256,8,128]{2,1,0:T(8,128)S(1)}) custom-call(s32[8,128]{1,0:T(8,128)S(1)} %reshape.141.stencil, f32[64,48,128]{2,1,0:T(8,128)S(1)} %get-tuple-element.24.blocks, f32[256,4,128]{2,1,0:T(4,128)S(1)} %copy-done, f32[256,16,128]{2,1,0:T(8,128)S(1)} %get-tuple-element.25.spread), custom_call_target="tpu_custom_call" | custom-call | flops 12582912 | bytes 6291456 | tf_op jit(solution)/shard_map/horizontal/pallas_call | solution.py:471
  106.0 0.0 collective-permute-done.above
  106.0 3.0 %vertical.1 = bf16[256,3,16,128]{3,2,1,0:T(8,128)(2,1)} custom-call(s32[8,128]{1,0:T(8,128)S(1)} %reshape.141.stencil, s32[1]{0:T(128)} %bitcast.12.at_top, bf16[256,3,16,128]{3,2,1,0:T(8,128)(2,1)S(1)} %get-tuple-element.26.partial, f32[256,8,128]{2,1,0:T(8,128)S(1)} %get-tuple-element.27.tops, bf16[192,128]{1,0:T(8,128)(2,1)S(1)} %get-tuple-element.28.highest, ...), custom_call_target="tpu_custom_call" | custom-call | tf_op jit(solution)/shard_map/vertical/pallas_call | solution.py:485
  (7 shorter events, 0.1 us)
Async XLA Ops:
  4.5 11.9 %copy-start.3 = (s32[64,1]{0,1:T(1,128)S(1)}, s32[64,1]{0,1:T(1,128)}, u32[]{:S(2)}) copy-start(s32[64,1]{0,1:T(1,128)} %param.11) | copy-start | bytes 772
  4.5 36.5 %all-to-all-start = ((bf16[32,128,128]{2,1,0:T(8,128)(2,1)}), bf16[32,128,128]{2,1,0:T(8,128)(2,1)S(1)}, u32[]{:S(2)}, u32[]{:S(2)}) async-start(bf16[32,128,128]{2,1,0:T(8,128)(2,1)} %pack.1), calls=%async_computation | async-start | bytes 2097152 | tf_op jit(solution)/shard_map/all_to_all | solution.py:400
  49.6 8.6 %copy-start.2 = (s32[256,4]{0,1:T(4,128)S(1)}, s32[256,4]{0,1:T(4,128)}, u32[]{:S(2)}) copy-start(s32[256,4]{0,1:T(4,128)} %param.13) | copy-start | bytes 12292
  49.6 45.4 %all-to-all-start.1 = ((bf16[32,64,384]{2,1,0:T(8,128)(2,1)}), bf16[32,64,384]{2,1,0:T(8,128)(2,1)S(1)}, u32[]{:S(2)}, u32[]{:S(2)}) async-start(bf16[32,64,384]{2,1,0:T(8,128)(2,1)} %get-tuple-element.18), calls=%async_computation.1 | async-start | bytes 3145728 | tf_op jit(solution)/shard_map/all_to_all | solution.py:433
  66.8 28.3 %copy-start.1 = (f32[256,16]{0,1:T(8,128)S(1)}, f32[256,16]{0,1:T(8,128)}, u32[]{:S(2)}) copy-start(f32[256,16]{0,1:T(8,128)} %param.15) | copy-start | bytes 49156
  95.1 7.4 %copy-start = (f32[256,4,128]{2,1,0:T(4,128)S(1)}, f32[256,4,128]{2,1,0:T(4,128)}, u32[]{:S(2)}) copy-start(f32[256,4,128]{2,1,0:T(4,128)} %hweight.3) | copy-start | bytes 1572868
  96.9 9.0 %collective-permute-start = (bf16[192,128]{1,0:T(8,128)(2,1)S(1)}, bf16[192,128]{1,0:T(8,128)(2,1)S(1)}, u32[]{:S(2)}, u32[]{:S(2)}) collective-permute-start(bf16[192,128]{1,0:T(8,128)(2,1)S(1)} %get-tuple-element.29), channel_id=1, source_target_pairs={{1,0},{2,1},{3,2},{4,3},{5,4},{6,5},{7,6},{9,8},{10,9},{11,10},{12... | collective-permute-start | bytes 147464 | tf_op jit(solution)/shard_map/ppermute | solution.py:470

commit v14 on v10

--- a/solution.py
+++ b/solution.py
@@ -162,7 +162,7 @@
     lists.start()
     for tile in range(tiles):
         columns = wide[:, tile * lat_dev : (tile + 1) * lat_dev, :].reshape(latitudes, LANES)
-        turned[tile * LANES : (tile + 1) * LANES, :] = mxu(unit, columns.astype(jnp.bfloat16), NT).astype(jnp.bfloat16)
+        turned[tile * LANES : (tile + 1) * LANES, :] = jnp.transpose(columns).astype(jnp.bfloat16)
 
     gap = jnp.zeros((LANES - half, degrees), jnp.bfloat16)
     chunk = 256
@@ -236,7 +236,6 @@
     column_of, received, zonal, vweight, blocks, lowest, highest, spread, lowest_scratch, highest_scratch
 ):
     owners, message_rows, message_lanes = received.shape
-    unit = identity(LANES)
     half = message_lanes // 8
     groups = message_rows // 8
     entries = blocks.shape[0]
@@ -246,9 +245,9 @@
         wide = received[:, pair * 16 : (pair + 1) * 16, :].astype(jnp.float32)
         for side in range(2):
             group = pair * 2 + side
-            own = wide[:, side * 8 : (side + 1) * 8, :].reshape(owners * 8, message_lanes).astype(jnp.bfloat16)
+            own = wide[:, side * 8 : (side + 1) * 8, :].reshape(owners * 8, message_lanes)
             turned = [
-                mxu(unit, own[:, tile * LANES : (tile + 1) * LANES], NT).astype(jnp.bfloat16)
+                jnp.transpose(own[:, tile * LANES : (tile + 1) * LANES]).astype(jnp.bfloat16)
                 for tile in range(message_lanes // LANES)
             ]
             turned = jnp.concatenate(turned, axis=0)

time: 110 us -> 109 us (level)
  no operation moved by 1% of the time
where the time goes in v14:
time: 109 us
  waiting for transfers between devices  51.6 us (47%)
  starting transfers between devices  25.9 us (24%)
  Pallas kernels  20 us (18%)
  other arithmetic  7.12 us (7%)
  local copies, waits for them, and re-layouts  3.11 us (3%)
    all_to_all x1, waiting for transfers between devices, per_device(): lax.all_to_all(message_two, 'lat', split_axis=0, concat_axis=0, tiled=True)  26.9 us
    all_to_all x1, waiting for transfers between devices, per_device(): lax.all_to_all(message_one, 'lat', split_axis=0, concat_axis=0, tiled=True)  24.2 us
    all_to_all x1, starting transfers between devices, per_device(): lax.all_to_all(message_one, 'lat', split_axis=0, concat_axis=0, tiled=True)  11.9 us
    all_to_all x1, starting transfers between devices, per_device(): lax.all_to_all(message_two, 'lat', split_axis=0, concat_axis=0, tiled=True)  8.59 us
    pallas_call x1, Pallas kernels, per_device(): pl.pallas_call(spectral_kernel, in_specs=[vmem, hbm, vmem], out_specs=[vm...  8.58 us
    another operation x1, other arithmetic  5.81 us
    ppermute x1, starting transfers between devices, per_device(): lax.ppermute(lowest, 'lev', [(i, i - 1) for i in range(1, lev_count)])  5.47 us
    pallas_call x1, Pallas kernels, per_device(): pl.pallas_call(pack_kernel, out_shape=jax.ShapeDtypeStruct((lat_count, ti...  3.87 us
  transfers between devices with their start and end apart: 3, of which 3 were waited for; matrix products, arithmetic and copies ran while one was open for 9% of the time, Pallas kernels for 2%

profile of v14, /device:TPU:1, one launch (start us, length us, event | category | flops | bytes accessed | tf_op | source)
XLA Modules:
  0.0 108.6 jit_solution(4665868119525753802)
XLA Ops:
  0.6 3.9 %pack.1 = bf16[32,128,128]{2,1,0:T(8,128)(2,1)} custom-call(s32[1,64]{1,0:T(1,128)} %bitcast.28, s32[2,32]{1,0:T(2,128)} %bitcast.26, f32[1,40]{1,0:T(1,128)} %bitcast.27, bf16[40,3,16,128]{3,2,1,0:T(8,128)(2,1)} %fourier_in.1), custom_call_target="tpu_custom_call" | custom-call | tf_op jit(solution)/shard_map/pack/pallas_call | solution.py:368
  4.5 0.0 copy-start.3
  4.5 11.9 %all-to-all-start = ((bf16[32,128,128]{2,1,0:T(8,128)(2,1)}), bf16[32,128,128]{2,1,0:T(8,128)(2,1)S(1)}, u32[]{:S(2)}, u32[]{:S(2)}) async-start(bf16[32,128,128]{2,1,0:T(8,128)(2,1)} %pack.1), calls=%async_computation | async-start | bytes 2097152 | tf_op jit(solution)/shard_map/all_to_all | solution.py:387
  16.4 0.0 copy-done.3
  16.5 0.1 convert_reduce_fusion.1
  16.6 0.2 dynamic-slice_reduce_fusion
  16.7 0.1 fusion.9.damping
  16.8 24.2 %all-to-all-done.arrived = bf16[32,128,128]{2,1,0:T(8,128)(2,1)S(1)} async-done(((bf16[32,128,128]{2,1,0:T(8,128)(2,1)}), bf16[32,128,128]{2,1,0:T(8,128)(2,1)S(1)}, u32[]{:S(2)}, u32[]{:S(2)}) %all-to-all-start) | async-done | bytes 1048608 | tf_op jit(solution)/shard_map/all_to_all | solution.py:387
  41.0 8.6 %spectral.1 = (bf16[4,96,640]{2,1,0:T(8,128)(2,1)S(1)}, bf16[32,64,384]{2,1,0:T(8,128)(2,1)}) custom-call(bf16[32,128,128]{2,1,0:T(8,128)(2,1)S(1)} %all-to-all-done.arrived, bf16[4,1280,640]{2,1,0:T(8,128)(2,1)} %bitcast.24, f32[4,640]{1,0:T(4,128)S(1)} %fusion.9.damping), custom_call_target="tpu_custom_call" | custom-call | tf_op jit(solution)/shard_map/spectral/pallas_call | solution.py:398
  49.6 0.0 copy-start.2
  49.6 8.6 %all-to-all-start.1 = ((bf16[32,64,384]{2,1,0:T(8,128)(2,1)}), bf16[32,64,384]{2,1,0:T(8,128)(2,1)S(1)}, u32[]{:S(2)}, u32[]{:S(2)}) async-start(bf16[32,64,384]{2,1,0:T(8,128)(2,1)} %get-tuple-element.16), calls=%async_computation.1 | async-start | bytes 3145728 | tf_op jit(solution)/shard_map/all_to_all | solution.py:420
  58.2 0.0 copy-done.2
  58.2 0.1 copy.21
  58.4 0.1 reshape.141.stencil
  58.5 0.1 fusion.7
  58.6 0.1 slice_reduce_fusion
  58.8 0.1 reshape_squeeze.3
  58.9 0.7 convert_reduce_fusion
  59.6 0.1 reshape.149.column_of
  59.7 1.2 %copy.27 = bf16[4,3,2,16,640]{4,2,3,1,0:T(2,128)(2,1)} copy(bf16[4,3,2,16,640]{4,3,2,1,0:T(8,128)(2,1)S(1)} %bitcast.22) | data formatting | bytes 983040 | tf_op jit(solution)/shard_map/reshape | solution.py:423
  60.8 5.8 %multiply_convert_fusion.1 = (bf16[20,128,1,128]{3,1,2,0:T(8,128)(2,1)S(1)}, bf16[20,128,1,128]{3,1,2,0:T(8,128)(2,1)S(1)}) fusion(f32[128]{0:T(128)S(1)} %compare_select_fusion, s32[20,128]{1,0:T(8,128)S(1)} %multiply_add_fusion, s32[128]{0:T(128)S(1)} %get-tuple-element.20), kind=kLoop, calls=%fused_computation.5 | loop fusion | flops 4587520 | bytes 1321984 | tf_op jit(solution)/shard_map/convert.2
  66.6 0.1 pad_maximum_fusion
  66.8 0.0 copy-start.1
  66.8 1.4 %copy.23 = bf16[20,128,2,128]{3,2,1,0:T(2,128)(2,1)S(1)} copy(bf16[20,128,2,128]{3,1,2,0:T(8,128)(2,1)S(1)} %pad_maximum_fusion) | data formatting | bytes 2621440 | tf_op jit(solution)/shard_map/concatenate | solution.py:432
  68.2 26.9 %all-to-all-done.1.received = bf16[32,64,384]{2,1,0:T(8,128)(2,1)S(1)} async-done(((bf16[32,64,384]{2,1,0:T(8,128)(2,1)}), bf16[32,64,384]{2,1,0:T(8,128)(2,1)S(1)}, u32[]{:S(2)}, u32[]{:S(2)}) %all-to-all-start.1) | async-done | bytes 1572896 | tf_op jit(solution)/shard_map/all_to_all | solution.py:420
  95.1 0.0 copy-done.1
  95.1 0.0 copy-start
  95.1 1.9 %blocks.1 = (f32[64,48,128]{2,1,0:T(8,128)S(1)}, bf16[192,128]{1,0:T(8,128)(2,1)S(1)}, bf16[192,128]{1,0:T(8,128)(2,1)S(1)}, f32[256,16,128]{2,1,0:T(8,128)S(1)}) custom-call(s32[64]{0:T(128)S(1)} %reshape.149.column_of, bf16[32,64,384]{2,1,0:T(8,128)(2,1)S(1)} %all-to-all-done.1.received, bf16[20,256,128]{2,1,0:T(8,128)(2,1)S(1)} %bitcast.21, ...), custom_call_target="tpu_custom_call" | custom-call | tf_op jit(solution)/shard_map/blocks/pallas_call | solution.py:442
  96.9 5.5 %collective-permute-start = (bf16[192,128]{1,0:T(8,128)(2,1)S(1)}, bf16[192,128]{1,0:T(8,128)(2,1)S(1)}, u32[]{:S(2)}, u32[]{:S(2)}) collective-permute-start(bf16[192,128]{1,0:T(8,128)(2,1)S(1)} %get-tuple-element.24), channel_id=1, source_target_pairs={{1,0},{2,1},{3,2},{4,3},{5,4},{6,5},{7,6},{9,8},{10,9},{11,10},{12... | collective-permute-start | bytes 147464 | tf_op jit(solution)/shard_map/ppermute | solution.py:457
  102.4 0.0 copy-done
  102.4 2.5 %horizontal.1 = f32[256,48,128]{2,1,0:T(8,128)S(1)} custom-call(s32[8,128]{1,0:T(8,128)S(1)} %reshape.141.stencil, f32[64,48,128]{2,1,0:T(8,128)S(1)} %get-tuple-element.22.blocks, f32[256,4,128]{2,1,0:T(4,128)S(1)} %copy-done), custom_call_target="tpu_custom_call" | custom-call | flops 12582912 | bytes 6291456 | tf_op jit(solution)/shard_map/horizontal/pallas_call | solution.py:458
  104.9 0.5 collective-permute-done.above
  105.4 3.2 %vertical.1 = bf16[256,3,16,128]{3,2,1,0:T(8,128)(2,1)} custom-call(s32[8,128]{1,0:T(8,128)S(1)} %reshape.141.stencil, s32[1]{0:T(128)} %bitcast.12.at_top, f32[256,48,128]{2,1,0:T(8,128)S(1)} %horizontal.1, bf16[192,128]{1,0:T(8,128)(2,1)S(1)} %get-tuple-element.23.highest, bf16[192,128]{1,0:T(8,128)(2,1)S(1)} %collective-permute-done.above, ...), custom_call_target="tpu_custom_call" | custom-call | tf_op jit(solution)/shard_map/vertical/pallas_call | solution.py:469
  (7 shorter events, 0.1 us)
Async XLA Ops:
  4.5 11.9 %copy-start.3 = (s32[64,1]{0,1:T(1,128)S(1)}, s32[64,1]{0,1:T(1,128)}, u32[]{:S(2)}) copy-start(s32[64,1]{0,1:T(1,128)} %param.11) | copy-start | bytes 772
  4.5 36.5 %all-to-all-start = ((bf16[32,128,128]{2,1,0:T(8,128)(2,1)}), bf16[32,128,128]{2,1,0:T(8,128)(2,1)S(1)}, u32[]{:S(2)}, u32[]{:S(2)}) async-start(bf16[32,128,128]{2,1,0:T(8,128)(2,1)} %pack.1), calls=%async_computation | async-start | bytes 2097152 | tf_op jit(solution)/shard_map/all_to_all | solution.py:387
  49.6 8.6 %copy-start.2 = (s32[256,4]{0,1:T(4,128)S(1)}, s32[256,4]{0,1:T(4,128)}, u32[]{:S(2)}) copy-start(s32[256,4]{0,1:T(4,128)} %param.13) | copy-start | bytes 12292
  49.6 45.4 %all-to-all-start.1 = ((bf16[32,64,384]{2,1,0:T(8,128)(2,1)}), bf16[32,64,384]{2,1,0:T(8,128)(2,1)S(1)}, u32[]{:S(2)}, u32[]{:S(2)}) async-start(bf16[32,64,384]{2,1,0:T(8,128)(2,1)} %get-tuple-element.16), calls=%async_computation.1 | async-start | bytes 3145728 | tf_op jit(solution)/shard_map/all_to_all | solution.py:420
  66.8 28.3 %copy-start.1 = (f32[256,16]{0,1:T(8,128)S(1)}, f32[256,16]{0,1:T(8,128)}, u32[]{:S(2)}) copy-start(f32[256,16]{0,1:T(8,128)} %param.15) | copy-start | bytes 49156
  95.1 7.4 %copy-start = (f32[256,4,128]{2,1,0:T(4,128)S(1)}, f32[256,4,128]{2,1,0:T(4,128)}, u32[]{:S(2)}) copy-start(f32[256,4,128]{2,1,0:T(4,128)} %hweight.3) | copy-start | bytes 1572868
  96.9 8.4 %collective-permute-start = (bf16[192,128]{1,0:T(8,128)(2,1)S(1)}, bf16[192,128]{1,0:T(8,128)(2,1)S(1)}, u32[]{:S(2)}, u32[]{:S(2)}) collective-permute-start(bf16[192,128]{1,0:T(8,128)(2,1)S(1)} %get-tuple-element.24), channel_id=1, source_target_pairs={{1,0},{2,1},{3,2},{4,3},{5,4},{6,5},{7,6},{9,8},{10,9},{11,10},{12... | collective-permute-start | bytes 147464 | tf_op jit(solution)/shard_map/ppermute | solution.py:457

commit v15 on v14

--- a/solution.py
+++ b/solution.py
@@ -376,7 +376,7 @@
             pltpu.VMEM((1, lat_dev), jnp.float32),
             pltpu.VMEM(fourier.shape, jnp.bfloat16),
             pltpu.VMEM((lat_count, tiles * lat_dev + 8, LANES), jnp.bfloat16),
-            pltpu.VMEM((tiles, lat_count * lat_dev, LANES), jnp.float32),
+            pltpu.VMEM((tiles, (lat_count + 1) * lat_dev, LANES), jnp.float32),
             pltpu.VMEM((lat_dev, columns), jnp.float32),
             pltpu.SemaphoreType.DMA((lat_dev // 8 + 3,)),
             pltpu.SemaphoreType.DMA((lat_count // 8,)),
@@ -403,7 +403,7 @@
             pltpu.VMEM((slot_most, latitudes, degrees), jnp.bfloat16),
             pltpu.VMEM(message_shape, jnp.bfloat16),
             pltpu.VMEM((message_lanes, latitudes), jnp.bfloat16),
-            pltpu.VMEM((latitudes * 2 * slot_most, LANES), jnp.float32),
+            pltpu.VMEM(((latitudes + 1) * 2 * slot_most, LANES), jnp.float32),
             pltpu.VMEM((entries, LANES), jnp.int32),
             pltpu.SMEM((entries, LANES), jnp.int32),
             pltpu.SemaphoreType.DMA,

time: 109 us -> 109 us (level)
  no operation moved by 1% of the time
where the time goes in v15:
time: 109 us
  waiting for transfers between devices  51.5 us (47%)
  starting transfers between devices  26 us (24%)
  Pallas kernels  20 us (18%)
  other arithmetic  7.12 us (7%)
  local copies, waits for them, and re-layouts  3.11 us (3%)
    all_to_all x1, waiting for transfers between devices, per_device(): lax.all_to_all(message_two, 'lat', split_axis=0, concat_axis=0, tiled=True)  26.9 us
    all_to_all x1, waiting for transfers between devices, per_device(): lax.all_to_all(message_one, 'lat', split_axis=0, concat_axis=0, tiled=True)  24.2 us
    all_to_all x1, starting transfers between devices, per_device(): lax.all_to_all(message_one, 'lat', split_axis=0, concat_axis=0, tiled=True)  11.9 us
    all_to_all x1, starting transfers between devices, per_device(): lax.all_to_all(message_two, 'lat', split_axis=0, concat_axis=0, tiled=True)  8.6 us
    pallas_call x1, Pallas kernels, per_device(): pl.pallas_call(spectral_kernel, in_specs=[vmem, hbm, vmem], out_specs=[vm...  8.57 us
    another operation x1, other arithmetic  5.81 us
    ppermute x1, starting transfers between devices, per_device(): lax.ppermute(lowest, 'lev', [(i, i - 1) for i in range(1, lev_count)])  5.49 us
    pallas_call x1, Pallas kernels, per_device(): pl.pallas_call(pack_kernel, out_shape=jax.ShapeDtypeStruct((lat_count, ti...  3.87 us
  transfers between devices with their start and end apart: 3, of which 3 were waited for; matrix products, arithmetic and copies ran while one was open for 9% of the time, Pallas kernels for 2%

profile of v15, /device:TPU:1, one launch (start us, length us, event | category | flops | bytes accessed | tf_op | source)
XLA Modules:
  0.0 108.6 jit_solution(11162007497739667152)
XLA Ops:
  0.6 3.9 %pack.1 = bf16[32,128,128]{2,1,0:T(8,128)(2,1)} custom-call(s32[1,64]{1,0:T(1,128)} %bitcast.28, s32[2,32]{1,0:T(2,128)} %bitcast.26, f32[1,40]{1,0:T(1,128)} %bitcast.27, bf16[40,3,16,128]{3,2,1,0:T(8,128)(2,1)} %fourier_in.1), custom_call_target="tpu_custom_call" | custom-call | tf_op jit(solution)/shard_map/pack/pallas_call | solution.py:368
  4.5 0.0 copy-start.3
  4.5 11.9 %all-to-all-start = ((bf16[32,128,128]{2,1,0:T(8,128)(2,1)}), bf16[32,128,128]{2,1,0:T(8,128)(2,1)S(1)}, u32[]{:S(2)}, u32[]{:S(2)}) async-start(bf16[32,128,128]{2,1,0:T(8,128)(2,1)} %pack.1), calls=%async_computation | async-start | bytes 2097152 | tf_op jit(solution)/shard_map/all_to_all | solution.py:387
  16.4 0.0 copy-done.3
  16.4 0.1 convert_reduce_fusion.1
  16.6 0.2 dynamic-slice_reduce_fusion
  16.7 0.1 fusion.9.damping
  16.8 24.2 %all-to-all-done.arrived = bf16[32,128,128]{2,1,0:T(8,128)(2,1)S(1)} async-done(((bf16[32,128,128]{2,1,0:T(8,128)(2,1)}), bf16[32,128,128]{2,1,0:T(8,128)(2,1)S(1)}, u32[]{:S(2)}, u32[]{:S(2)}) %all-to-all-start) | async-done | bytes 1048608 | tf_op jit(solution)/shard_map/all_to_all | solution.py:387
  41.0 8.6 %spectral.1 = (bf16[4,96,640]{2,1,0:T(8,128)(2,1)S(1)}, bf16[32,64,384]{2,1,0:T(8,128)(2,1)}) custom-call(bf16[32,128,128]{2,1,0:T(8,128)(2,1)S(1)} %all-to-all-done.arrived, bf16[4,1280,640]{2,1,0:T(8,128)(2,1)} %bitcast.24, f32[4,640]{1,0:T(4,128)S(1)} %fusion.9.damping), custom_call_target="tpu_custom_call" | custom-call | tf_op jit(solution)/shard_map/spectral/pallas_call | solution.py:398
  49.6 0.0 copy-start.2
  49.6 8.6 %all-to-all-start.1 = ((bf16[32,64,384]{2,1,0:T(8,128)(2,1)}), bf16[32,64,384]{2,1,0:T(8,128)(2,1)S(1)}, u32[]{:S(2)}, u32[]{:S(2)}) async-start(bf16[32,64,384]{2,1,0:T(8,128)(2,1)} %get-tuple-element.16), calls=%async_computation.1 | async-start | bytes 3145728 | tf_op jit(solution)/shard_map/all_to_all | solution.py:420
  58.2 0.0 copy-done.2
  58.3 0.1 copy.21
  58.4 0.1 reshape.141.stencil
  58.5 0.1 fusion.7
  58.7 0.1 slice_reduce_fusion
  58.8 0.1 reshape_squeeze.3
  58.9 0.7 convert_reduce_fusion
  59.6 0.1 reshape.149.column_of
  59.7 1.2 %copy.27 = bf16[4,3,2,16,640]{4,2,3,1,0:T(2,128)(2,1)} copy(bf16[4,3,2,16,640]{4,3,2,1,0:T(8,128)(2,1)S(1)} %bitcast.22) | data formatting | bytes 983040 | tf_op jit(solution)/shard_map/reshape | solution.py:423
  60.8 5.8 %multiply_convert_fusion.1 = (bf16[20,128,1,128]{3,1,2,0:T(8,128)(2,1)S(1)}, bf16[20,128,1,128]{3,1,2,0:T(8,128)(2,1)S(1)}) fusion(f32[128]{0:T(128)S(1)} %compare_select_fusion, s32[20,128]{1,0:T(8,128)S(1)} %multiply_add_fusion, s32[128]{0:T(128)S(1)} %get-tuple-element.20), kind=kLoop, calls=%fused_computation.5 | loop fusion | flops 4587520 | bytes 1321984 | tf_op jit(solution)/shard_map/convert.2
  66.7 0.1 pad_maximum_fusion
  66.8 0.0 copy-start.1
  66.8 1.4 %copy.23 = bf16[20,128,2,128]{3,2,1,0:T(2,128)(2,1)S(1)} copy(bf16[20,128,2,128]{3,1,2,0:T(8,128)(2,1)S(1)} %pad_maximum_fusion) | data formatting | bytes 2621440 | tf_op jit(solution)/shard_map/concatenate | solution.py:432
  68.2 26.9 %all-to-all-done.1.received = bf16[32,64,384]{2,1,0:T(8,128)(2,1)S(1)} async-done(((bf16[32,64,384]{2,1,0:T(8,128)(2,1)}), bf16[32,64,384]{2,1,0:T(8,128)(2,1)S(1)}, u32[]{:S(2)}, u32[]{:S(2)}) %all-to-all-start.1) | async-done | bytes 1572896 | tf_op jit(solution)/shard_map/all_to_all | solution.py:420
  95.0 0.0 copy-done.1
  95.0 0.0 copy-start
  95.0 1.9 %blocks.1 = (f32[64,48,128]{2,1,0:T(8,128)S(1)}, bf16[192,128]{1,0:T(8,128)(2,1)S(1)}, bf16[192,128]{1,0:T(8,128)(2,1)S(1)}, f32[256,16,128]{2,1,0:T(8,128)S(1)}) custom-call(s32[64]{0:T(128)S(1)} %reshape.149.column_of, bf16[32,64,384]{2,1,0:T(8,128)(2,1)S(1)} %all-to-all-done.1.received, bf16[20,256,128]{2,1,0:T(8,128)(2,1)S(1)} %bitcast.21, ...), custom_call_target="tpu_custom_call" | custom-call | tf_op jit(solution)/shard_map/blocks/pallas_call | solution.py:442
  96.9 5.5 %collective-permute-start = (bf16[192,128]{1,0:T(8,128)(2,1)S(1)}, bf16[192,128]{1,0:T(8,128)(2,1)S(1)}, u32[]{:S(2)}, u32[]{:S(2)}) collective-permute-start(bf16[192,128]{1,0:T(8,128)(2,1)S(1)} %get-tuple-element.24), channel_id=1, source_target_pairs={{1,0},{2,1},{3,2},{4,3},{5,4},{6,5},{7,6},{9,8},{10,9},{11,10},{12... | collective-permute-start | bytes 147464 | tf_op jit(solution)/shard_map/ppermute | solution.py:457
  102.4 0.0 copy-done
  102.4 2.5 %horizontal.1 = f32[256,48,128]{2,1,0:T(8,128)S(1)} custom-call(s32[8,128]{1,0:T(8,128)S(1)} %reshape.141.stencil, f32[64,48,128]{2,1,0:T(8,128)S(1)} %get-tuple-element.22.blocks, f32[256,4,128]{2,1,0:T(4,128)S(1)} %copy-done), custom_call_target="tpu_custom_call" | custom-call | flops 12582912 | bytes 6291456 | tf_op jit(solution)/shard_map/horizontal/pallas_call | solution.py:458
  104.9 0.4 collective-permute-done.above
  105.4 3.2 %vertical.1 = bf16[256,3,16,128]{3,2,1,0:T(8,128)(2,1)} custom-call(s32[8,128]{1,0:T(8,128)S(1)} %reshape.141.stencil, s32[1]{0:T(128)} %bitcast.12.at_top, f32[256,48,128]{2,1,0:T(8,128)S(1)} %horizontal.1, bf16[192,128]{1,0:T(8,128)(2,1)S(1)} %get-tuple-element.23.highest, bf16[192,128]{1,0:T(8,128)(2,1)S(1)} %collective-permute-done.above, ...), custom_call_target="tpu_custom_call" | custom-call | tf_op jit(solution)/shard_map/vertical/pallas_call | solution.py:469
  (7 shorter events, 0.1 us)
Async XLA Ops:
  4.5 11.9 %copy-start.3 = (s32[64,1]{0,1:T(1,128)S(1)}, s32[64,1]{0,1:T(1,128)}, u32[]{:S(2)}) copy-start(s32[64,1]{0,1:T(1,128)} %param.11) | copy-start | bytes 772
  4.5 36.5 %all-to-all-start = ((bf16[32,128,128]{2,1,0:T(8,128)(2,1)}), bf16[32,128,128]{2,1,0:T(8,128)(2,1)S(1)}, u32[]{:S(2)}, u32[]{:S(2)}) async-start(bf16[32,128,128]{2,1,0:T(8,128)(2,1)} %pack.1), calls=%async_computation | async-start | bytes 2097152 | tf_op jit(solution)/shard_map/all_to_all | solution.py:387
  49.6 8.6 %copy-start.2 = (s32[256,4]{0,1:T(4,128)S(1)}, s32[256,4]{0,1:T(4,128)}, u32[]{:S(2)}) copy-start(s32[256,4]{0,1:T(4,128)} %param.13) | copy-start | bytes 12292
  49.6 45.4 %all-to-all-start.1 = ((bf16[32,64,384]{2,1,0:T(8,128)(2,1)}), bf16[32,64,384]{2,1,0:T(8,128)(2,1)S(1)}, u32[]{:S(2)}, u32[]{:S(2)}) async-start(bf16[32,64,384]{2,1,0:T(8,128)(2,1)} %get-tuple-element.16), calls=%async_computation.1 | async-start | bytes 3145728 | tf_op jit(solution)/shard_map/all_to_all | solution.py:420
  66.8 28.3 %copy-start.1 = (f32[256,16]{0,1:T(8,128)S(1)}, f32[256,16]{0,1:T(8,128)}, u32[]{:S(2)}) copy-start(f32[256,16]{0,1:T(8,128)} %param.15) | copy-start | bytes 49156
  95.0 7.4 %copy-start = (f32[256,4,128]{2,1,0:T(4,128)S(1)}, f32[256,4,128]{2,1,0:T(4,128)}, u32[]{:S(2)}) copy-start(f32[256,4,128]{2,1,0:T(4,128)} %hweight.3) | copy-start | bytes 1572868
  96.9 8.4 %collective-permute-start = (bf16[192,128]{1,0:T(8,128)(2,1)S(1)}, bf16[192,128]{1,0:T(8,128)(2,1)S(1)}, u32[]{:S(2)}, u32[]{:S(2)}) collective-permute-start(bf16[192,128]{1,0:T(8,128)(2,1)S(1)} %get-tuple-element.24), channel_id=1, source_target_pairs={{1,0},{2,1},{3,2},{4,3},{5,4},{6,5},{7,6},{9,8},{10,9},{11,10},{12... | collective-permute-start | bytes 147464 | tf_op jit(solution)/shard_map/ppermute | solution.py:457

commit v16 on v15

--- a/solution.py
+++ b/solution.py
@@ -259,10 +259,10 @@
                 for a in range(entry * per_entry, (entry + 1) * per_entry):
                     spread[a] = jnp.broadcast_to(vweight[:, a : a + 1], (levels, LANES))
                 for field in range(3):
-                    lowest_scratch[field * entries + entry : field * entries + entry + 1, :] = made[
+                    lowest_scratch[entry * 3 + 2 - field : entry * 3 + 3 - field, :] = made[
                         field * 16 : field * 16 + 1, :
                     ]
-                    highest_scratch[field * entries + entry : field * entries + entry + 1, :] = made[
+                    highest_scratch[entry * 3 + 2 - field : entry * 3 + 3 - field, :] = made[
                         field * 16 + 15 : field * 16 + 16, :
                     ]
     lowest[...] = lowest_scratch[...].astype(jnp.bfloat16)
@@ -286,22 +286,11 @@
     lax.fori_loop(0, rows // together, some_rows, 0)
 
 
-def vertical_kernel(stencil, at_top, horizontal, highest, above, hweight, spread, arrival, made, over_rows, wide, out_sem):
+def vertical_kernel(stencil, at_top, horizontal, highest, above, hweight, spread, arrival, made, over_rows, out_sem):
     rows, fields, levels, _ = made.shape
-    entries = wide.shape[0]
     top = at_top[0] == 1
-    over_rows[...] = jnp.where(top, highest[...].astype(jnp.float32), above[...].astype(jnp.float32))
-    together = 8
-
-    def widen(i, carry):
-        for k in range(together):
-            entry = i * together + k
-            for field in range(fields):
-                wide[entry, 7 - field : 8 - field, :] = over_rows[pl.ds(field * entries + entry, 1), :]
-        return carry
-
-    lax.fori_loop(0, entries // together, widen, 0)
-
+    count = above.shape[0]
+    over_rows[8 : 8 + count, :] = jnp.where(top, highest[...].astype(jnp.float32), above[...].astype(jnp.float32))
     row = lax.broadcasted_iota(jnp.int32, (8, LANES), 0)
     piece = stencil.shape[1] // 4
     pieces = rows // piece
@@ -315,7 +304,7 @@
             a = i * piece + k
             last = None
             for q in range(4):
-                term = hweight[a, q : q + 1, :] * wide[stencil[i, k * 4 + q]]
+                term = hweight[a, q : q + 1, :] * over_rows[pl.ds(stencil[i, k * 4 + q] * 3 + 3, 8), :]
                 last = term if last is None else last + term
             for field in range(fields):
                 parts = []
@@ -473,8 +462,7 @@
         out_specs=hbm,
         scratch_shapes=[
             pltpu.VMEM((arrivals, fields, levels, BLK), jnp.bfloat16),
-            pltpu.VMEM((fields * entries, BLK), jnp.float32),
-            pltpu.VMEM((entries, 8, BLK), jnp.float32),
+            pltpu.VMEM((fields * entries + 8, BLK), jnp.float32),
             pltpu.SemaphoreType.DMA((arrivals // 32,)),
         ],
         compiler_params=pltpu.CompilerParams(vmem_limit_bytes=16 * 2**20),

time: 109 us -> 109 us (level)
  no operation moved by 1% of the time
where the time goes in v16:
time: 109 us; the launch traced here: 108 us
  waiting for transfers between devices  51.5 us (47%)
  starting transfers between devices  26 us (24%)
  Pallas kernels  19.9 us (18%)
  other arithmetic  7.12 us (7%)
  local copies, waits for them, and re-layouts  3.11 us (3%)
    all_to_all x1, waiting for transfers between devices, per_device(): lax.all_to_all(message_two, 'lat', split_axis=0, concat_axis=0, tiled=True)  26.9 us
    all_to_all x1, waiting for transfers between devices, per_device(): lax.all_to_all(message_one, 'lat', split_axis=0, concat_axis=0, tiled=True)  24.2 us
    all_to_all x1, starting transfers between devices, per_device(): lax.all_to_all(message_one, 'lat', split_axis=0, concat_axis=0, tiled=True)  11.9 us
    all_to_all x1, starting transfers between devices, per_device(): lax.all_to_all(message_two, 'lat', split_axis=0, concat_axis=0, tiled=True)  8.6 us
    pallas_call x1, Pallas kernels, per_device(): pl.pallas_call(spectral_kernel, in_specs=[vmem, hbm, vmem], out_specs=[vm...  8.57 us
    another operation x1, other arithmetic  5.81 us
    ppermute x1, starting transfers between devices, per_device(): lax.ppermute(lowest, 'lev', [(i, i - 1) for i in range(1, lev_count)])  5.49 us
    pallas_call x1, Pallas kernels, per_device(): pl.pallas_call(pack_kernel, out_shape=jax.ShapeDtypeStruct((lat_count, ti...  3.87 us
  transfers between devices with their start and end apart: 3, of which 3 were waited for; matrix products, arithmetic and copies ran while one was open for 9% of the time, Pallas kernels for 2%

profile of v16, /device:TPU:1, one launch (start us, length us, event | category | flops | bytes accessed | tf_op | source)
XLA Modules:
  0.0 108.5 jit_solution(17747972855480282472)
XLA Ops:
  0.6 3.9 %pack.1 = bf16[32,128,128]{2,1,0:T(8,128)(2,1)} custom-call(s32[1,64]{1,0:T(1,128)} %bitcast.28, s32[2,32]{1,0:T(2,128)} %bitcast.26, f32[1,40]{1,0:T(1,128)} %bitcast.27, bf16[40,3,16,128]{3,2,1,0:T(8,128)(2,1)} %fourier_in.1), custom_call_target="tpu_custom_call" | custom-call | tf_op jit(solution)/shard_map/pack/pallas_call | solution.py:357
  4.5 0.0 copy-start.3
  4.5 11.9 %all-to-all-start = ((bf16[32,128,128]{2,1,0:T(8,128)(2,1)}), bf16[32,128,128]{2,1,0:T(8,128)(2,1)S(1)}, u32[]{:S(2)}, u32[]{:S(2)}) async-start(bf16[32,128,128]{2,1,0:T(8,128)(2,1)} %pack.1), calls=%async_computation | async-start | bytes 2097152 | tf_op jit(solution)/shard_map/all_to_all | solution.py:376
  16.4 0.0 copy-done.3
  16.4 0.1 convert_reduce_fusion.1
  16.6 0.2 dynamic-slice_reduce_fusion
  16.7 0.1 fusion.9.damping
  16.8 24.2 %all-to-all-done.arrived = bf16[32,128,128]{2,1,0:T(8,128)(2,1)S(1)} async-done(((bf16[32,128,128]{2,1,0:T(8,128)(2,1)}), bf16[32,128,128]{2,1,0:T(8,128)(2,1)S(1)}, u32[]{:S(2)}, u32[]{:S(2)}) %all-to-all-start) | async-done | bytes 1048608 | tf_op jit(solution)/shard_map/all_to_all | solution.py:376
  41.0 8.6 %spectral.1 = (bf16[4,96,640]{2,1,0:T(8,128)(2,1)S(1)}, bf16[32,64,384]{2,1,0:T(8,128)(2,1)}) custom-call(bf16[32,128,128]{2,1,0:T(8,128)(2,1)S(1)} %all-to-all-done.arrived, bf16[4,1280,640]{2,1,0:T(8,128)(2,1)} %bitcast.24, f32[4,640]{1,0:T(4,128)S(1)} %fusion.9.damping), custom_call_target="tpu_custom_call" | custom-call | tf_op jit(solution)/shard_map/spectral/pallas_call | solution.py:387
  49.6 0.0 copy-start.2
  49.6 8.6 %all-to-all-start.1 = ((bf16[32,64,384]{2,1,0:T(8,128)(2,1)}), bf16[32,64,384]{2,1,0:T(8,128)(2,1)S(1)}, u32[]{:S(2)}, u32[]{:S(2)}) async-start(bf16[32,64,384]{2,1,0:T(8,128)(2,1)} %get-tuple-element.16), calls=%async_computation.1 | async-start | bytes 3145728 | tf_op jit(solution)/shard_map/all_to_all | solution.py:409
  58.2 0.0 copy-done.2
  58.3 0.1 copy.21
  58.4 0.1 reshape.141.stencil
  58.5 0.1 fusion.7
  58.7 0.1 slice_reduce_fusion
  58.8 0.1 reshape_squeeze.3
  58.9 0.7 convert_reduce_fusion
  59.6 0.1 reshape.149.column_of
  59.7 1.2 %copy.27 = bf16[4,3,2,16,640]{4,2,3,1,0:T(2,128)(2,1)} copy(bf16[4,3,2,16,640]{4,3,2,1,0:T(8,128)(2,1)S(1)} %bitcast.22) | data formatting | bytes 983040 | tf_op jit(solution)/shard_map/reshape | solution.py:412
  60.8 5.8 %multiply_convert_fusion.1 = (bf16[20,128,1,128]{3,1,2,0:T(8,128)(2,1)S(1)}, bf16[20,128,1,128]{3,1,2,0:T(8,128)(2,1)S(1)}) fusion(f32[128]{0:T(128)S(1)} %compare_select_fusion, s32[20,128]{1,0:T(8,128)S(1)} %multiply_add_fusion, s32[128]{0:T(128)S(1)} %get-tuple-element.20), kind=kLoop, calls=%fused_computation.5 | loop fusion | flops 4587520 | bytes 1321984 | tf_op jit(solution)/shard_map/convert.2
  66.7 0.1 pad_maximum_fusion
  66.8 0.0 copy-start.1
  66.8 1.4 %copy.23 = bf16[20,128,2,128]{3,2,1,0:T(2,128)(2,1)S(1)} copy(bf16[20,128,2,128]{3,1,2,0:T(8,128)(2,1)S(1)} %pad_maximum_fusion) | data formatting | bytes 2621440 | tf_op jit(solution)/shard_map/concatenate | solution.py:421
  68.2 26.9 %all-to-all-done.1.received = bf16[32,64,384]{2,1,0:T(8,128)(2,1)S(1)} async-done(((bf16[32,64,384]{2,1,0:T(8,128)(2,1)}), bf16[32,64,384]{2,1,0:T(8,128)(2,1)S(1)}, u32[]{:S(2)}, u32[]{:S(2)}) %all-to-all-start.1) | async-done | bytes 1572896 | tf_op jit(solution)/shard_map/all_to_all | solution.py:409
  95.0 0.0 copy-done.1
  95.0 0.0 copy-start
  95.0 1.9 %blocks.1 = (f32[64,48,128]{2,1,0:T(8,128)S(1)}, bf16[192,128]{1,0:T(8,128)(2,1)S(1)}, bf16[192,128]{1,0:T(8,128)(2,1)S(1)}, f32[256,16,128]{2,1,0:T(8,128)S(1)}) custom-call(s32[64]{0:T(128)S(1)} %reshape.149.column_of, bf16[32,64,384]{2,1,0:T(8,128)(2,1)S(1)} %all-to-all-done.1.received, bf16[20,256,128]{2,1,0:T(8,128)(2,1)S(1)} %bitcast.21, ...), custom_call_target="tpu_custom_call" | custom-call | tf_op jit(solution)/shard_map/blocks/pallas_call | solution.py:431
  96.9 5.5 %collective-permute-start = (bf16[192,128]{1,0:T(8,128)(2,1)S(1)}, bf16[192,128]{1,0:T(8,128)(2,1)S(1)}, u32[]{:S(2)}, u32[]{:S(2)}) collective-permute-start(bf16[192,128]{1,0:T(8,128)(2,1)S(1)} %get-tuple-element.24), channel_id=1, source_target_pairs={{1,0},{2,1},{3,2},{4,3},{5,4},{6,5},{7,6},{9,8},{10,9},{11,10},{12... | collective-permute-start | bytes 147464 | tf_op jit(solution)/shard_map/ppermute | solution.py:446
  102.4 0.0 copy-done
  102.4 2.5 %horizontal.1 = f32[256,48,128]{2,1,0:T(8,128)S(1)} custom-call(s32[8,128]{1,0:T(8,128)S(1)} %reshape.141.stencil, f32[64,48,128]{2,1,0:T(8,128)S(1)} %get-tuple-element.22.blocks, f32[256,4,128]{2,1,0:T(4,128)S(1)} %copy-done), custom_call_target="tpu_custom_call" | custom-call | flops 12582912 | bytes 6291456 | tf_op jit(solution)/shard_map/horizontal/pallas_call | solution.py:447
  104.9 0.4 collective-permute-done.above
  105.4 3.1 %vertical.1 = bf16[256,3,16,128]{3,2,1,0:T(8,128)(2,1)} custom-call(s32[8,128]{1,0:T(8,128)S(1)} %reshape.141.stencil, s32[1]{0:T(128)} %bitcast.12.at_top, f32[256,48,128]{2,1,0:T(8,128)S(1)} %horizontal.1, bf16[192,128]{1,0:T(8,128)(2,1)S(1)} %get-tuple-element.23.highest, bf16[192,128]{1,0:T(8,128)(2,1)S(1)} %collective-permute-done.above, ...), custom_call_target="tpu_custom_call" | custom-call | tf_op jit(solution)/shard_map/vertical/pallas_call | solution.py:458
  (7 shorter events, 0.1 us)
Async XLA Ops:
  4.5 11.9 %copy-start.3 = (s32[64,1]{0,1:T(1,128)S(1)}, s32[64,1]{0,1:T(1,128)}, u32[]{:S(2)}) copy-start(s32[64,1]{0,1:T(1,128)} %param.11) | copy-start | bytes 772
  4.5 36.5 %all-to-all-start = ((bf16[32,128,128]{2,1,0:T(8,128)(2,1)}), bf16[32,128,128]{2,1,0:T(8,128)(2,1)S(1)}, u32[]{:S(2)}, u32[]{:S(2)}) async-start(bf16[32,128,128]{2,1,0:T(8,128)(2,1)} %pack.1), calls=%async_computation | async-start | bytes 2097152 | tf_op jit(solution)/shard_map/all_to_all | solution.py:376
  49.6 8.6 %copy-start.2 = (s32[256,4]{0,1:T(4,128)S(1)}, s32[256,4]{0,1:T(4,128)}, u32[]{:S(2)}) copy-start(s32[256,4]{0,1:T(4,128)} %param.13) | copy-start | bytes 12292
  49.6 45.4 %all-to-all-start.1 = ((bf16[32,64,384]{2,1,0:T(8,128)(2,1)}), bf16[32,64,384]{2,1,0:T(8,128)(2,1)S(1)}, u32[]{:S(2)}, u32[]{:S(2)}) async-start(bf16[32,64,384]{2,1,0:T(8,128)(2,1)} %get-tuple-element.16), calls=%async_computation.1 | async-start | bytes 3145728 | tf_op jit(solution)/shard_map/all_to_all | solution.py:409
  66.8 28.3 %copy-start.1 = (f32[256,16]{0,1:T(8,128)S(1)}, f32[256,16]{0,1:T(8,128)}, u32[]{:S(2)}) copy-start(f32[256,16]{0,1:T(8,128)} %param.15) | copy-start | bytes 49156
  95.0 7.4 %copy-start = (f32[256,4,128]{2,1,0:T(4,128)S(1)}, f32[256,4,128]{2,1,0:T(4,128)}, u32[]{:S(2)}) copy-start(f32[256,4,128]{2,1,0:T(4,128)} %hweight.3) | copy-start | bytes 1572868
  96.9 8.4 %collective-permute-start = (bf16[192,128]{1,0:T(8,128)(2,1)S(1)}, bf16[192,128]{1,0:T(8,128)(2,1)S(1)}, u32[]{:S(2)}, u32[]{:S(2)}) collective-permute-start(bf16[192,128]{1,0:T(8,128)(2,1)S(1)} %get-tuple-element.24), channel_id=1, source_target_pairs={{1,0},{2,1},{3,2},{4,3},{5,4},{6,5},{7,6},{9,8},{10,9},{11,10},{12... | collective-permute-start | bytes 147464 | tf_op jit(solution)/shard_map/ppermute | solution.py:446
